TPU v7x, 256 devices: a whole 4x4x8 slice. The times are simulated.
256 devices in a mesh: seq: 64 (over y, z, core), head: 4 (over x).
Axes of the slice: x: 4, y: 4, z: 8, core: 2. Of those that a mesh axis runs over, the one named last changes fastest.
Arguments:
- queries: bfloat16 [49152, 4096], P(('seq', 'head')), may hold values from -4.6 to 4.6
- key_rows: bfloat16 [49152, 512], P(('seq', 'head')), may hold values from -4.6 to 4.6
- value_rows: bfloat16 [49152, 512], P(('seq', 'head')), may hold values from -6 to 6
- out_grad: bfloat16 [49152, 4096], P(('seq', 'head')), may hold values from -6 to 6
- mover_dest: int32 [3072], P('seq'), may hold values from 0 to 3071, as said below
- segment_ids: int32 [49152], P('seq'), may hold values from 0 to 6399, as said below
Outputs:
- attention_out: bfloat16 [49152, 4096], P('seq', 'head')
- query_grad: bfloat16 [49152, 4096], P('seq', 'head')
- key_grad: bfloat16 [49152, 512], P('seq', 'head')
- value_grad: bfloat16 [49152, 512], P('seq', 'head')
Inputs may be any that keep to these rules, and one draw needn't show every extreme that they name: `mover_dest`: each value names the shard (value // 48) and the block slot (value % 48) that receive one of the last 48 blocks of 4 rows of an owner's 768 rows; every value occurs once. One owner sends at most 3 blocks to one shard, and exactly 3 to some shard. `segment_ids`: equal values mark one completion, a run of consecutive rows inside one shard of 768 rows; values never fall along the rows. From row 576 of each shard on, each block of 4 rows begins a new completion.
All inputs are finite; a program needn't handle non-finite values.
Results may differ from a plain program's by a relative error of at most 0.0052.
Values may be sent and summed in bfloat16 or wider, within the bound.
No kernel may reach another device: no remote copies, remote signals or barrier semaphores. Data moves between devices by JAX's collectives and lax.ppermute only.
A program may use at most 128 MiB of HBM per device.

v0:
```python
import math

import jax
import jax.numpy as jnp
from jax import lax
from jax.sharding import PartitionSpec as P

DH = 128
BLK = 4
CAPB = 3


neg_large = -1e30


def attend_shard(query_part, key_part, value_part, grad_part, segments, head_dim):
    row_count = query_part.shape[0]
    shared_heads = key_part.shape[1] // head_dim
    group_size = query_part.shape[1] // head_dim // shared_heads
    query_heads = query_part.reshape(row_count, shared_heads, group_size, head_dim)
    key_heads = key_part.reshape(row_count, shared_heads, head_dim)
    value_heads = value_part.reshape(row_count, shared_heads, head_dim)
    grad_heads = grad_part.reshape(row_count, shared_heads, group_size, head_dim)
    inv_root = 1.0 / math.sqrt(head_dim)
    block_rows = min(768, row_count)
    places = jnp.arange(row_count, dtype=jnp.int32)
    allowed = (segments[0:block_rows, None] == segments[None, :]) & (
        places[None, :] <= places[0:block_rows, None]
    )
    scores = (
        jnp.einsum("qkgd,pkd->kgqp", query_heads, key_heads, preferred_element_type=jnp.float32)
        * inv_root
    )
    scores = jnp.where(allowed[None, None], scores, neg_large)
    highest = jnp.max(scores, axis=-1, keepdims=True)
    weights = jnp.exp(scores - highest)
    softmaxed = weights / jnp.sum(weights, axis=-1, keepdims=True)
    probs_low = softmaxed.astype(jnp.bfloat16)
    attended = jnp.einsum(
        "kgqp,pkd->qkgd", probs_low, value_heads, preferred_element_type=jnp.float32
    )
    outputs = attended.astype(jnp.bfloat16).reshape(block_rows, -1)
    grad_probs = jnp.einsum(
        "qkgd,pkd->kgqp", grad_heads, value_heads, preferred_element_type=jnp.float32
    )
    centre = jnp.sum(softmaxed * grad_probs, axis=-1, keepdims=True)
    grad_scores = (softmaxed * (grad_probs - centre) * inv_root).astype(jnp.bfloat16)
    query_grads = (
        jnp.einsum("kgqp,pkd->qkgd", grad_scores, key_heads, preferred_element_type=jnp.float32)
        .astype(jnp.bfloat16)
        .reshape(block_rows, -1)
    )
    key_total = jnp.einsum(
        "kgqp,qkgd->pkd", grad_scores, query_heads, preferred_element_type=jnp.float32
    )
    value_total = jnp.einsum(
        "kgqp,qkgd->pkd", probs_low, grad_heads, preferred_element_type=jnp.float32
    )
    return (
        outputs,
        query_grads,
        key_total.astype(jnp.bfloat16).reshape(row_count, -1),
        value_total.astype(jnp.bfloat16).reshape(row_count, -1),
    )


def send_slots(destination, valid, seq_count, movers):
    target = destination // movers
    onehot = (target[:, None] == jnp.arange(seq_count)[None, :]).astype(jnp.int32)
    earlier = jnp.cumsum(onehot, axis=0) - onehot
    ranking = jnp.sum(earlier * onehot, axis=1)
    return jnp.where(valid & (ranking < CAPB), target * CAPB + ranking, seq_count * CAPB)


def build_sends(arrays, destination, valid):
    seq_count = lax.axis_size("seq")
    movers = destination.shape[0]
    flat_slots = send_slots(destination, valid, seq_count, movers)
    buffers = []
    for member in arrays:
        column_count = member.shape[1]
        blocks = member.reshape(movers, BLK, column_count)
        empty = jnp.zeros((seq_count * CAPB, BLK, column_count), member.dtype)
        filled = empty.at[flat_slots].set(blocks, mode="drop")
        buffers.append(filled.reshape(seq_count, CAPB, BLK, column_count))
    return buffers


def receive_labels(all_dest, valid, movers):
    seq_count = lax.axis_size("seq")
    here = lax.axis_index("seq")
    table = all_dest.reshape(seq_count, movers)

    def one_source(plan_row):
        flat_slots = send_slots(plan_row, valid, seq_count, movers)
        position = jnp.where(valid & (plan_row // movers == here), flat_slots - here * CAPB, CAPB)
        return jnp.full((CAPB,), -1, jnp.int32).at[position].set(plan_row, mode="drop")

    return jax.vmap(one_source)(table)


def assemble(arrays, received, labels, tail_start, movers):
    first_block = lax.axis_index("seq") * movers
    flat_labels = labels.reshape(-1)
    slots = jnp.where(flat_labels >= 0, flat_labels - first_block, movers)
    result = []
    for member, moved in zip(arrays, received):
        column_count = member.shape[1]
        incoming = moved.reshape(-1, BLK, column_count)
        area = (
            jnp.zeros((movers, BLK, column_count), member.dtype)
            .at[slots]
            .set(incoming, mode="drop")
        )
        result.append(
            jnp.concatenate([member[:tail_start], area.reshape(movers * BLK, column_count)], axis=0)
        )
    return result


def regroup(query_part, key_part, value_part, grad_part):
    return (
        lax.all_to_all(query_part, "head", split_axis=1, concat_axis=0, tiled=True),
        lax.all_to_all(key_part, "head", split_axis=1, concat_axis=0, tiled=True),
        lax.all_to_all(value_part, "head", split_axis=1, concat_axis=0, tiled=True),
        lax.all_to_all(grad_part, "head", split_axis=1, concat_axis=0, tiled=True),
    )


def on_device(queries, key_rows, value_rows, out_grad, mover_dest, segment_ids):
    movers = mover_dest.shape[0]
    all_dest = lax.all_gather(mover_dest, "seq", axis=0, tiled=True)
    region_rows = queries.shape[0]
    tail_start = region_rows - movers * BLK
    active = lax.axis_index("head") == lax.axis_size("head") - 1
    held_rows = (queries, key_rows, value_rows, out_grad)
    buffers = build_sends(held_rows, mover_dest, active)
    received = (
        lax.all_to_all(buffers[0], "seq", split_axis=0, concat_axis=0, tiled=True),
        lax.all_to_all(buffers[1], "seq", split_axis=0, concat_axis=0, tiled=True),
        lax.all_to_all(buffers[2], "seq", split_axis=0, concat_axis=0, tiled=True),
        lax.all_to_all(buffers[3], "seq", split_axis=0, concat_axis=0, tiled=True),
    )
    labels = receive_labels(all_dest, active, movers)
    placed = assemble(held_rows, received, labels, tail_start, movers)
    merged = [jnp.where(active, updated, unmoved) for updated, unmoved in zip(placed, held_rows)]
    packed = regroup(merged[0], merged[1], merged[2], merged[3])
    return attend_shard(packed[0], packed[1], packed[2], packed[3], segment_ids, DH)


def solution(mesh):
    in_specs = (
        P(("seq", "head"), None),
        P(("seq", "head"), None),
        P(("seq", "head"), None),
        P(("seq", "head"), None),
        P("seq"),
        P("seq"),
    )
    out_specs = (P("seq", "head"), P("seq", "head"), P("seq", "head"), P("seq", "head"))
    return jax.shard_map(
        on_device, mesh=mesh, in_specs=in_specs, out_specs=out_specs, check_vma=False
    )
```

profile of v0, /device:TPU:1, one launch (start us, length us, event | category | flops | bytes accessed | tf_op | source)
XLA Modules:
  0.0 828.7 jit_solution(12072629219434939891)
XLA Ops:
  4.4 5.6 scatter_fusion.2
  10.0 13.2 %all-to-all-start.2 = ((bf16[64,3,4,512]{3,2,1,0:T(4,128)(2,1)}), bf16[64,3,4,512]{3,2,1,0:T(4,128)(2,1)S(1)}, u32[]{:S(2)}, u32[]{:S(2)}) async-start(bf16[64,3,4,512]{3,2,1,0:T(4,128)(2,1)} %bitcast.9), calls=%async_computation.2 | async-start | bytes 1572864 | tf_op jit(solution)/shard_map/all_to_all | solution.py:140
  25.6 5.8 broadcast.252.clone
  31.5 5.8 scatter_fusion.6
  37.3 8.8 %all-to-all-done.2 = bf16[64,3,4,512]{3,2,1,0:T(4,128)(2,1)S(1)} async-done(((bf16[64,3,4,512]{3,2,1,0:T(4,128)(2,1)}), bf16[64,3,4,512]{3,2,1,0:T(4,128)(2,1)S(1)}, u32[]{:S(2)}, u32[]{:S(2)}) %all-to-all-start.2) | async-done | bytes 786464 | tf_op jit(solution)/shard_map/all_to_all | solution.py:140
  47.0 6.4 all-to-all-start.6
  54.0 5.8 broadcast.252.clone.1
  59.8 5.8 scatter_fusion.4
  65.7 128.6 %all-to-all-done.6 = bf16[64,3,4,4096]{3,2,1,0:T(4,128)(2,1)} async-done(((bf16[64,3,4,4096]{3,2,1,0:T(4,128)(2,1)}), bf16[64,3,4,4096]{3,2,1,0:T(4,128)(2,1)}, u32[]{:S(2)}, u32[]{:S(2)}) %all-to-all-start.6) | async-done | bytes 6291488 | tf_op jit(solution)/shard_map/all_to_all | solution.py:142
  194.3 6.1 all-to-all-start.4
  201.9 369.3 %all-reduce = s32[3072]{0:T(1024)S(1)} all-reduce(s32[3072]{0:T(1024)S(1)} %dynamic-update-slice), channel_id=1, replica_groups=mesh['seq'=64,'head'=4] {'seq'}, use_global_device_ids=true, to_apply=%add | all-reduce | flops 3072 | bytes 24576
  572.8 5.6 scatter_fusion
  578.4 11.1 %all-to-all-start = ((bf16[64,3,4,512]{3,2,1,0:T(4,128)(2,1)}), bf16[64,3,4,512]{3,2,1,0:T(4,128)(2,1)}, u32[]{:S(2)}, u32[]{:S(2)}) async-start(bf16[64,3,4,512]{3,2,1,0:T(4,128)(2,1)} %bitcast.4), calls=%async_computation | async-start | bytes 1572864 | tf_op jit(solution)/shard_map/all_to_all | solution.py:141
  591.7 11.8 %scatter_custom_fusion.8 = s32[192]{0:T(256)S(1)} fusion(s32[3072]{0:T(1024)S(1)} %reshape.432, s32[3072]{0:T(1024)S(1)} %all-reduce, s32[]{:T(128)} %constant.21.clone.1), kind=kCustom, calls=%fused_computation.69 | custom fusion | bytes 772
  603.9 6.8 scatter_fusion.3
  612.2 19.2 %scatter_fusion.7 = bf16[48,4,4096]{2,1,0:T(4,128)(2,1)S(1)} fusion(bf16[48,4,4096]{2,1,0:T(4,128)(2,1)S(1)} %broadcast.251.clone, s32[192]{0:T(256)S(1)} %bitcast.157, bf16[192,4,4096]{2,1,0:T(4,128)(2,1)} %bitcast.28), kind=kCustom, calls=%fused_computation.7 | custom fusion | bytes 18875136 | tf_op jit(solution)/shard_map/scatter | solution.py:113
  634.1 19.2 %scatter_fusion.5 = bf16[48,4,4096]{2,1,0:T(4,128)(2,1)S(1)} fusion(bf16[48,4,4096]{2,1,0:T(4,128)(2,1)S(1)} %broadcast.251.clone.1, s32[192]{0:T(256)S(1)} %bitcast.158, bf16[192,4,4096]{2,1,0:T(4,128)(2,1)} %bitcast.15), kind=kCustom, calls=%fused_computation.5 | custom fusion | bytes 18875136 | tf_op jit(solution)/shard_map/scatter | solution.py:113
  655.1 4.2 all-to-all-start.3
  669.4 17.5 %all-to-all-done.5 = bf16[192,4,1024]{2,0,1:T(8,128)(2,1)S(1)} async-done(((bf16[192,4,1024]{2,0,1:T(8,128)(2,1)}), bf16[192,4,1024]{2,0,1:T(8,128)(2,1)S(1)}, u32[]{:S(2)}, u32[]{:S(2)}) %all-to-all-start.5) | async-done | bytes 1572896 | tf_op jit(solution)/shard_map/all_to_all | solution.py:123
  686.9 4.3 all-to-all-start.7
  691.7 16.6 %scatter_fusion.1 = bf16[48,4,512]{2,1,0:T(4,128)(2,1)S(1)} fusion(bf16[48,4,512]{2,1,0:T(4,128)(2,1)S(1)} %broadcast.243.clone, s32[192]{0:T(256)S(1)} %bitcast.159, bf16[192,4,512]{2,1,0:T(4,128)(2,1)} %bitcast.5), kind=kCustom, calls=%fused_computation.1 | custom fusion | bytes 2360064 | tf_op jit(solution)/shard_map/scatter | solution.py:113
  711.0 8.4 %fusion.6 = (f32[8,768]{1,0:T(8,128)S(1)}, f32[768,768,8]{1,0,2:T(8,128)}) fusion(pred[768,768]{0,1:T(8,128)(4,1)S(1)} %fusion.8, bf16[768,128,1]{1,0,2:T(8,128)(2,1)S(1)} %bitcast.151, bf16[768,8,128]{2,1,0:T(8,128)(2,1)S(1)} %bitcast.140), kind=kOutput, calls=%fused_computation.19 | convolution fusion | flops 1222109184 | bytes 21258240 | tf_op jit(solution)/shard_map/qkgd,pkd->kgqp/dot_general | solution.py:31
  719.4 4.4 all-to-all-start.1
  723.8 10.2 %fusion.5 = f32[8,768]{1,0:T(8,128)S(1)} fusion(f32[768,768,8]{1,0,2:T(8,128)} %get-tuple-element.23, f32[8,768]{1,0:T(8,128)S(1)} %get-tuple-element.22, pred[768,768]{0,1:T(8,128)(4,1)S(1)} %fusion.8), kind=kLoop, calls=%fused_computation.18 | loop fusion | flops 18868224 | bytes 19513344 | tf_op jit(solution)/shard_map/reduce_sum | solution.py:37
  737.0 17.9 %fusion = (f32[8,768]{1,0:T(8,128)S(1)}, f32[768,768,8]{1,0,2:T(8,128)}) fusion(f32[8,768]{1,0:T(8,128)S(1)} %fusion.5, f32[8,768]{1,0:T(8,128)S(1)} %get-tuple-element.22, f32[768,768,8]{1,0,2:T(8,128)} %get-tuple-element.23, pred[768,768]{0,1:T(8,128)(4,1)S(1)} %fusion.8, bf16[768,128,1]{1,0,2:T(8,128)(2,1)S(1)} %bitcast.153, ...), kind=kOutput, calls=%fused_computation.12 | convolution fusion | flops 1236264960 | bytes 40181760 | tf_op jit(solution)/shard_map/qkgd,pkd->kgqp/dot_general | solution.py:43
  754.9 17.9 %fusion.7 = (bf16[8,768,768]{1,2,0:T(8,128)(2,1)S(1)}, bf16[8,768,768]{1,2,0:T(8,128)(2,1)}) fusion(f32[768,768,8]{1,0,2:T(8,128)} %get-tuple-element.25, f32[8,768]{1,0:T(8,128)S(1)} %get-tuple-element.24, f32[8,768]{1,0:T(8,128)S(1)} %fusion.5, f32[8,768]{1,0:T(8,128)S(1)} %get-tuple-element.22, f32[768,768,8]{1,0,2:T(8,128)} %get-tuple-element.23, ...), kind=kLoop, calls=%fused_computation.20 | loop fusion | flops 42467328 | bytes 57286656 | tf_op jit(solution)/shard_map/reshape.18
  772.9 3.7 copy-done
  779.2 13.1 %copy.78 = bf16[8,768,768]{2,0,1:T(8,128)(2,1)} copy(bf16[8,768,768]{1,2,0:T(8,128)(2,1)} %copy-done) | data formatting | bytes 18874368 | tf_op jit(solution)/shard_map/reshape.18
  792.3 6.3 convolution_convert_fusion.1
  798.6 13.4 %copy.79 = bf16[8,768,768]{2,0,1:T(8,128)(2,1)} copy(bf16[8,768,768]{1,2,0:T(8,128)(2,1)} %get-tuple-element.21) | data formatting | bytes 18874368 | tf_op jit(solution)/shard_map/reshape.10
  812.0 5.3 fusion.21
  820.7 5.3 fusion.20
  (93 shorter events, 43.3 us)
Async XLA Ops:
  10.0 36.2 %all-to-all-start.2 = ((bf16[64,3,4,512]{3,2,1,0:T(4,128)(2,1)}), bf16[64,3,4,512]{3,2,1,0:T(4,128)(2,1)S(1)}, u32[]{:S(2)}, u32[]{:S(2)}) async-start(bf16[64,3,4,512]{3,2,1,0:T(4,128)(2,1)} %bitcast.9), calls=%async_computation.2 | async-start | bytes 1572864 | tf_op jit(solution)/shard_map/all_to_all | solution.py:140
  46.1 0.9 copy-start.7
  46.1 7.2 copy-start.2
  47.0 147.2 %all-to-all-start.6 = ((bf16[64,3,4,4096]{3,2,1,0:T(4,128)(2,1)}), bf16[64,3,4,4096]{3,2,1,0:T(4,128)(2,1)}, u32[]{:S(2)}, u32[]{:S(2)}) async-start(bf16[64,3,4,4096]{3,2,1,0:T(4,128)(2,1)} %bitcast.138), calls=%async_computation.6 | async-start | bytes 12582912 | tf_op jit(solution)/shard_map/all_to_all | solution.py:142
  194.2 6.2 copy-start.15
  194.2 7.4 copy-start.14
  194.2 377.4 %copy-start.10 = (bf16[192,512]{1,0:T(8,128)(2,1)S(1)}, bf16[192,512]{1,0:T(8,128)(2,1)}, u32[]{:S(2)}) copy-start(bf16[192,512]{1,0:T(8,128)(2,1)} %param.8) | copy-start | bytes 589828
  194.2 397.2 %copy-start.13 = (s32[2]{0:T(128)S(1)}, s32[2]{0:T(128)}, u32[]{:S(2)}) copy-start(s32[2]{0:T(128)} %constant.66) | copy-start | bytes 28
  194.2 397.3 %copy-start.12 = (s32[2]{0:T(128)S(1)}, s32[2]{0:T(128)}, u32[]{:S(2)}) copy-start(s32[2]{0:T(128)} %constant.69) | copy-start | bytes 28
  194.2 409.6 %copy-start.8 = (bf16[64,3,4,512]{3,2,1,0:T(4,128)(2,1)S(1)}, bf16[64,3,4,512]{3,2,1,0:T(4,128)(2,1)}, u32[]{:S(2)}) copy-start(bf16[64,3,4,512]{3,2,1,0:T(4,128)(2,1)} %copy-done.7) | copy-start | bytes 2359300
  194.3 384.2 %all-to-all-start.4 = ((bf16[64,3,4,4096]{3,2,1,0:T(4,128)(2,1)}), bf16[64,3,4,4096]{3,2,1,0:T(4,128)(2,1)}, u32[]{:S(2)}, u32[]{:S(2)}) async-start(bf16[64,3,4,4096]{3,2,1,0:T(4,128)(2,1)} %bitcast.139), calls=%async_computation.4 | async-start | bytes 12582912 | tf_op jit(solution)/shard_map/all_to_all | solution.py:139
  200.4 410.4 %copy-start.9 = (bf16[192,512]{1,0:T(8,128)(2,1)S(1)}, bf16[192,512]{1,0:T(8,128)(2,1)}, u32[]{:S(2)}) copy-start(bf16[192,512]{1,0:T(8,128)(2,1)} %param.7) | copy-start | bytes 589828
  578.4 76.7 %all-to-all-start = ((bf16[64,3,4,512]{3,2,1,0:T(4,128)(2,1)}), bf16[64,3,4,512]{3,2,1,0:T(4,128)(2,1)}, u32[]{:S(2)}, u32[]{:S(2)}) async-start(bf16[64,3,4,512]{3,2,1,0:T(4,128)(2,1)} %bitcast.4), calls=%async_computation | async-start | bytes 1572864 | tf_op jit(solution)/shard_map/all_to_all | solution.py:141
  634.0 25.3 %copy-start.1 = (bf16[192,4096]{1,0:T(8,128)(2,1)S(1)}, bf16[192,4096]{1,0:T(8,128)(2,1)}, u32[]{:S(2)}) copy-start(bf16[192,4096]{1,0:T(8,128)(2,1)} %param.9) | copy-start | bytes 4718596
  655.1 9.4 %all-to-all-start.3 = ((bf16[192,4,128]{2,0,1:T(8,128)(2,1)}), bf16[192,4,128]{2,0,1:T(8,128)(2,1)S(1)}, u32[]{:S(2)}, u32[]{:S(2)}) async-start(bf16[192,4,128]{2,0,1:T(8,128)(2,1)} %copy_bitcast_fusion.2), calls=%async_computation.3 | async-start | bytes 393216 | tf_op jit(solution)/shard_map/all_to_all | solution.py:124
  662.2 5.9 copy-start.4
  662.2 29.1 %copy-start.11 = (s32[768]{0:T(1024)S(1)}, s32[768]{0:T(1024)}, u32[]{:S(2)}) copy-start(s32[768]{0:T(1024)} %param.11) | copy-start | bytes 9220
  664.5 22.4 %all-to-all-start.5 = ((bf16[192,4,1024]{2,0,1:T(8,128)(2,1)}), bf16[192,4,1024]{2,0,1:T(8,128)(2,1)S(1)}, u32[]{:S(2)}, u32[]{:S(2)}) async-start(bf16[192,4,1024]{2,0,1:T(8,128)(2,1)} %bitcast.144), calls=%async_computation.5 | async-start | bytes 3145728 | tf_op jit(solution)/shard_map/all_to_all | solution.py:123
  686.9 4.7 copy-start.3
  686.9 32.5 %all-to-all-start.7 = ((bf16[192,4,1024]{2,0,1:T(8,128)(2,1)}), bf16[192,4,1024]{2,0,1:T(8,128)(2,1)}, u32[]{:S(2)}, u32[]{:S(2)}) async-start(bf16[192,4,1024]{2,0,1:T(8,128)(2,1)} %bitcast.127), calls=%async_computation.7 | async-start | bytes 3145728 | tf_op jit(solution)/shard_map/all_to_all | solution.py:126
  719.4 17.6 %all-to-all-start.1 = ((bf16[192,4,128]{2,0,1:T(8,128)(2,1)}), bf16[192,4,128]{2,0,1:T(8,128)(2,1)S(1)}, u32[]{:S(2)}, u32[]{:S(2)}) async-start(bf16[192,4,128]{2,0,1:T(8,128)(2,1)} %copy_bitcast_fusion.3), calls=%async_computation.1 | async-start | bytes 393216 | tf_op jit(solution)/shard_map/all_to_all | solution.py:125
  772.9 3.7 copy-start
  812.0 8.7 %copy-start.5 = (bf16[96,8,8,128]{3,2,1,0:T(8,128)(2,1)S(1)}, bf16[96,8,8,128]{3,2,1,0:T(8,128)(2,1)}, u32[]{:S(2)}) copy-start(bf16[96,8,8,128]{3,2,1,0:T(8,128)(2,1)} %copy.95) | copy-start | bytes 4718596
  820.7 6.1 copy-start.6
where the time goes:
time: 844 us; the launch traced here: 829 us
  blocking collectives  369 us (44%)
  local copies, waits for them, and re-layouts  166 us (20%)
  waiting for transfers between devices  156 us (18%)
  starting transfers between devices  53.2 us (6%)
  matrix products  45.9 us (5%)
  other arithmetic  36.5 us (4%)
    unnamed x1, blocking collectives  369 us
    all_to_all x1, waiting for transfers between devices, on_device(): lax.all_to_all(buffers[3], 'seq', split_axis=0, concat_axis=0, tiled=True)  129 us
    scatter x4, local copies, waits for them, and re-layouts, assemble(): area = jnp.zeros((movers, BLK, column_count), member.dtype).at[slots].set...  61.9 us
    another operation x10, local copies, waits for them, and re-layouts  41.9 us
    unnamed x44, local copies, waits for them, and re-layouts  28 us
    scatter x4, local copies, waits for them, and re-layouts, build_sends(): filled = empty.at[flat_slots].set(blocks, mode='drop')  22.8 us
    dot_general x1, matrix products, attend_shard(): jnp.einsum('qkgd,pkd->kgqp', grad_heads, value_heads, preferred_element_t...  17.9 us
    another operation x1, other arithmetic  17.9 us
  transfers between devices with their start and end apart: 8, of which 4 were waited for; matrix products, arithmetic and copies ran while one was open for 18% of the time, Pallas kernels for 0%

commit v1 on v0

v1 whole, which is shorter than its diff:
```python
import functools
import math

import jax
import jax.numpy as jnp
from jax import lax
from jax.experimental import pallas as pl
from jax.experimental.pallas import tpu as pltpu
from jax.sharding import PartitionSpec as P

DH = 128
GROUP = 8
QW = GROUP * DH
ROWS = 768
QUART = 192
STAY = 576
BLK = 4
NBLK = 48
SEQ = 64
SLOT = 56
WIDE = 2 * QW + 2 * DH
INV = 1.0 / math.sqrt(DH)
NEG = -1e30
F32 = jnp.float32
BF16 = jnp.bfloat16
VMEM_LIMIT = 56 * 1024 * 1024


def params():
    return pltpu.CompilerParams(vmem_limit_bytes=VMEM_LIMIT)


def swap_groups(x):
    sub = lax.broadcasted_iota(jnp.int32, x.shape, 1)
    grp = lax.broadcasted_iota(jnp.int32, x.shape, 2) // 16
    for bit in (1, 2, 4):
        s_on = (sub & bit) != 0
        l_on = (grp & bit) != 0
        up = pltpu.roll(pltpu.roll(x, 8 - bit, 1), 16 * bit, 2)
        down = pltpu.roll(pltpu.roll(x, bit, 1), 128 - 16 * bit, 2)
        x = jnp.where(s_on == l_on, x, jnp.where(l_on, up, down))
    return x


def pack_kernel(q_ref, k_ref, v_ref, g_ref, plan_ref, lo_ref, hi_ref, qs, ks, small):
    half = SEQ // 2
    ks[0] = k_ref[...].astype(F32)
    ks[1] = v_ref[...].astype(F32)
    pieces = []
    for r in range(8):
        rows = ks[r // 4, pl.ds(r % 4, NBLK, stride=BLK), :]
        pieces.append(rows.reshape(6, 8, DH))
    mixed = swap_groups(jnp.concatenate(pieces, axis=0))
    small[...] = jnp.zeros_like(small)
    for r in range(8):
        for b in range(6):
            small[pl.ds(r * 8, 8), b, :] = mixed[r * 6 + b]
    plan = plan_ref[...]
    small[:, 6, :] = jnp.broadcast_to((plan // 64).astype(F32), (SEQ, DH))
    small[:, 7, :] = jnp.broadcast_to((plan % 64).astype(F32), (SEQ, DH))
    for src, dst, first in ((q_ref, lo_ref, 0), (g_ref, hi_ref, half)):
        for n in range(GROUP):
            qs[n] = src[:, n * DH : (n + 1) * DH].astype(F32)
            for t in range(BLK):
                rows = qs[n, pl.ds(t, NBLK, stride=BLK), :]
                dst[t * GROUP + n, 0:NBLK, :] = rows.astype(BF16)
        dst[:, NBLK:SLOT, :] = small[pl.ds(first, half)].astype(BF16)


def pack_tail(queries, key_rows, value_rows, out_grad, plan_row, group):
    half = jax.ShapeDtypeStruct((SEQ // 2, SLOT, DH), BF16)
    return pl.pallas_call(
        pack_kernel,
        grid=(1,),
        in_specs=[
            pl.BlockSpec((QUART, QW), lambda i: (0, group)),
            pl.BlockSpec((QUART, DH), lambda i: (0, group)),
            pl.BlockSpec((QUART, DH), lambda i: (0, group)),
            pl.BlockSpec((QUART, QW), lambda i: (0, group)),
            pl.BlockSpec((1, DH), lambda i: (0, 0)),
        ],
        out_specs=[pl.BlockSpec((SEQ // 2, SLOT, DH), lambda i: (0, 0, 0))] * 2,
        out_shape=[half, half],
        scratch_shapes=[
            pltpu.VMEM((GROUP, QUART, DH), F32),
            pltpu.VMEM((2, QUART, DH), F32),
            pltpu.VMEM((SEQ, 8, DH), F32),
        ],
        compiler_params=params(),
        cost_estimate=pl.CostEstimate(flops=0, bytes_accessed=2_000_000, transcendentals=0),
        name="pack_tail",
    )(queries, key_rows, value_rows, out_grad, plan_row)


def slice_kernel(me_ref, q_ref, k_ref, v_ref, g_ref, o_ref):
    o_ref[:, 0:QW] = q_ref[...]
    o_ref[:, QW : 2 * QW] = g_ref[...]
    o_ref[:, 2 * QW : 2 * QW + DH] = k_ref[...]
    o_ref[:, 2 * QW + DH : WIDE] = v_ref[...]


def slice_group(queries, key_rows, value_rows, out_grad, group):
    column = lambda i, g: (0, g[0])
    return pl.pallas_call(
        slice_kernel,
        grid_spec=pltpu.PrefetchScalarGridSpec(
            num_scalar_prefetch=1,
            grid=(1,),
            in_specs=[
                pl.BlockSpec((QUART, QW), column),
                pl.BlockSpec((QUART, DH), column),
                pl.BlockSpec((QUART, DH), column),
                pl.BlockSpec((QUART, QW), column),
            ],
            out_specs=pl.BlockSpec((QUART, WIDE), lambda i, g: (0, 0)),
        ),
        out_shape=jax.ShapeDtypeStruct((QUART, WIDE), BF16),
        compiler_params=params(),
        cost_estimate=pl.CostEstimate(flops=0, bytes_accessed=1_800_000, transcendentals=0),
        name="slice_group",
    )(group.reshape(1), queries, key_rows, value_rows, out_grad)


TILE = 384


def route_kernel(in_ref, out_ref, xs, low, line, sel):
    count = SEQ * NBLK
    col = lax.broadcasted_iota(jnp.int32, (1, count), 1).astype(F32)
    owner = jnp.floor((col + 0.5) * (1.0 / NBLK))
    place = col - owner * NBLK
    pick = (lax.broadcasted_iota(jnp.int32, (DH, count), 0).astype(F32) == place).astype(BF16)
    mine = lax.broadcasted_iota(jnp.int32, (SEQ, count), 0).astype(F32) == owner
    tail = in_ref[:, NBLK:SLOT, :].astype(F32)
    for which, row in ((0, 6), (1, 7)):
        spread = jnp.dot(tail[:, row, :].astype(BF16), pick, preferred_element_type=F32)
        line[which : which + 1, :] = jnp.sum(jnp.where(mine, spread, 0.0), axis=0, keepdims=True)
    low[...] = (
        lax.broadcasted_iota(jnp.int32, (64, count), 0).astype(F32) == line[1:2, :]
    ).astype(BF16)

    lane = lax.broadcasted_iota(jnp.int32, (NBLK, DH), 1) // 16
    sub = lax.broadcasted_iota(jnp.int32, (NBLK, DH), 0) % 8
    here = lane == sub
    fold = (
        lax.broadcasted_iota(jnp.int32, (DH, DH), 0) % 16
        == lax.broadcasted_iota(jnp.int32, (DH, DH), 1) % 16
    ).astype(BF16)
    for s in range(SEQ):
        xs[s * NBLK : (s + 1) * NBLK, 0:DH] = in_ref[s, 0:NBLK, :]
        rows = [jnp.broadcast_to(tail[s, b : b + 1, :], (8, DH)) for b in range(6)]
        wide = jnp.where(here, jnp.concatenate(rows, axis=0), 0.0).astype(BF16)
        xs[s * NBLK : (s + 1) * NBLK, DH : 2 * DH] = jnp.dot(
            wide, fold, preferred_element_type=F32
        ).astype(BF16)

    def step(i, carry):
        for k in range(TILE // 64):
            high = (i * (TILE // 64) + k).astype(F32)
            row = jnp.where(line[0:1, :] == high, 1.0, 0.0).astype(BF16)
            sel[k * 64 : (k + 1) * 64, :] = low[...] * row
        got = jnp.dot(sel[...], xs[...], preferred_element_type=F32)
        for d in range(TILE // NBLK):
            part = got[d * NBLK : (d + 1) * NBLK]
            shard = i * (TILE // NBLK) + d
            out_ref[shard, 0:NBLK, :] = part[:, 0:DH].astype(BF16)
            kept = jnp.where(here, part[:, DH : 2 * DH], 0.0)
            sums = [jnp.sum(kept[b * 8 : b * 8 + 8], axis=0, keepdims=True) for b in range(6)]
            sums.append(jnp.zeros((2, DH), F32))
            out_ref[shard, NBLK:SLOT, :] = jnp.concatenate(sums, axis=0).astype(BF16)
        return carry

    lax.fori_loop(0, count // TILE, step, 0)


def route(slots):
    count = SEQ * NBLK
    shape = (SEQ, SLOT, DH)
    return pl.pallas_call(
        route_kernel,
        in_specs=[pl.BlockSpec(memory_space=pltpu.VMEM)],
        out_specs=pl.BlockSpec(memory_space=pltpu.VMEM),
        out_shape=jax.ShapeDtypeStruct(shape, BF16),
        scratch_shapes=[
            pltpu.VMEM((count, 2 * DH), BF16),
            pltpu.VMEM((64, count), BF16),
            pltpu.VMEM((8, count), F32),
            pltpu.VMEM((TILE, count), BF16),
        ],
        compiler_params=params(),
        cost_estimate=pl.CostEstimate(
            flops=2 * count * count * 2 * DH, bytes_accessed=2_000_000, transcendentals=0
        ),
        name="route",
    )(slots)


def dot(a, b, dims):
    return lax.dot_general(a, b, (dims, ((), ())), preferred_element_type=F32)


NT = ((1,), (1,))
NN = ((1,), (0,))
TN = ((0,), (0,))


def attend(q, g, k, v, allowed):
    scores = jnp.where(allowed, dot(q, k, NT) * INV, NEG)
    weights = jnp.exp(scores - jnp.max(scores, axis=-1, keepdims=True))
    probs = weights * (1.0 / jnp.sum(weights, axis=-1, keepdims=True))
    probs_low = probs.astype(BF16)
    out = dot(probs_low, v, NN).astype(BF16)
    grad_probs = dot(g, v, NT)
    centre = jnp.sum(probs * grad_probs, axis=-1, keepdims=True)
    grad_scores = (probs * (grad_probs - centre) * INV).astype(BF16)
    dq = dot(grad_scores, k, NN).astype(BF16)
    return out, dq, dot(grad_scores, q, TN), dot(probs_low, g, TN)


def causal(seg_col, seg_row, first):
    rows, cols = seg_col.shape[0], seg_row.shape[1]
    i = lax.broadcasted_iota(jnp.int32, (rows, cols), 0) + first
    j = lax.broadcasted_iota(jnp.int32, (rows, cols), 1)
    return (seg_col == seg_row) & (j <= i)


def stay_kernel(
    me_ref, q_any, k_any, v_any, g_any, plus, minus, two, relay, col_ref, row_ref,
    out_ref, dq_ref, dk_ref, dv_ref, rows, dk, dv, sems,
):
    n = pl.program_id(0)
    me = me_ref[0]

    @pl.when(n == 0)
    def _():
        def fetch(src, part):
            pltpu.make_async_copy(src, rows.at[pl.ds(part * QUART, QUART), :], sems.at[part]).start()

        wide = pl.ds(pl.multiple_of(me * QW, QW), QW)
        thin = pl.ds(pl.multiple_of(me * DH, DH), DH)

        def own(part):
            there = pl.ds(part * QUART, QUART)
            pltpu.make_async_copy(q_any.at[:, wide], rows.at[there, 0:QW], sems.at[part]).start()
            pltpu.make_async_copy(g_any.at[:, wide], rows.at[there, QW : 2 * QW], sems.at[part]).start()
            pltpu.make_async_copy(k_any.at[:, thin], rows.at[there, 2 * QW : 2 * QW + DH], sems.at[part]).start()
            pltpu.make_async_copy(v_any.at[:, thin], rows.at[there, 2 * QW + DH : WIDE], sems.at[part]).start()

        @pl.when(me == 0)
        def _():
            own(0)
            fetch(minus, 1)
            fetch(two, 2)

        @pl.when(me == 1)
        def _():
            fetch(plus, 0)
            own(1)
            fetch(minus, 2)

        @pl.when(me == 2)
        def _():
            fetch(two, 0)
            fetch(plus, 1)
            own(2)

        @pl.when(me == 3)
        def _():
            fetch(minus, 0)
            fetch(relay, 1)
            fetch(plus, 2)

        for part in range(3):
            pltpu.make_async_copy(plus, rows.at[pl.ds(part * QUART, QUART), :], sems.at[part]).wait()
        dk[...] = jnp.zeros_like(dk)
        dv[...] = jnp.zeros_like(dv)

    q_at = pl.ds(pl.multiple_of(n * DH, DH), DH)
    g_at = pl.ds(pl.multiple_of(QW + n * DH, DH), DH)
    for part in range(3):
        there = pl.ds(part * QUART, QUART)
        width = (part + 1) * QUART
        k = rows[0:width, 2 * QW : 2 * QW + DH]
        v = rows[0:width, 2 * QW + DH : WIDE]
        allowed = causal(col_ref[there, :], row_ref[:, 0:width], part * QUART)
        out, dq, dk_part, dv_part = attend(rows[there, q_at], rows[there, g_at], k, v, allowed)
        out_ref[there, :] = out
        dq_ref[there, :] = dq
        dk[0:width, :] += dk_part
        dv[0:width, :] += dv_part

    @pl.when(n == GROUP - 1)
    def _():
        dk_ref[...] = dk[...].astype(BF16)
        dv_ref[...] = dv[...].astype(BF16)


OUT_SHAPES = [
    jax.ShapeDtypeStruct((ROWS, QW), BF16),
    jax.ShapeDtypeStruct((ROWS, QW), BF16),
    jax.ShapeDtypeStruct((ROWS, DH), BF16),
    jax.ShapeDtypeStruct((ROWS, DH), BF16),
]


def attend_stay(me, held, received, seg_col, seg_row):
    any_spec = pl.BlockSpec(memory_space=pl.ANY)
    return pl.pallas_call(
        stay_kernel,
        grid_spec=pltpu.PrefetchScalarGridSpec(
            num_scalar_prefetch=1,
            grid=(GROUP,),
            in_specs=[any_spec] * 8
            + [
                pl.BlockSpec((STAY, 1), lambda n, m: (0, 0)),
                pl.BlockSpec((1, ROWS), lambda n, m: (0, 0)),
            ],
            out_specs=[
                pl.BlockSpec((STAY, DH), lambda n, m: (0, n)),
                pl.BlockSpec((STAY, DH), lambda n, m: (0, n)),
                pl.BlockSpec((STAY, DH), lambda n, m: (0, 0)),
                pl.BlockSpec((STAY, DH), lambda n, m: (0, 0)),
            ],
            scratch_shapes=[
                pltpu.VMEM((STAY, WIDE), BF16),
                pltpu.VMEM((STAY, DH), F32),
                pltpu.VMEM((STAY, DH), F32),
                pltpu.SemaphoreType.DMA((3,)),
            ],
        ),
        out_shape=OUT_SHAPES,
        compiler_params=params(),
        cost_estimate=pl.CostEstimate(
            flops=6 * 2 * GROUP * STAY * STAY * DH,
            bytes_accessed=6_000_000,
            transcendentals=GROUP * STAY * STAY,
        ),
        name="attend_stay",
    )(me.reshape(1), *held, *received, seg_col, seg_row)


def tail_kernel(
    slots, col_ref, row_ref, a0, a1, a2, a3, out_ref, dq_ref, dk_ref, dv_ref, qs, gs, ks, small
):
    for t in range(BLK):
        for n in range(GROUP):
            there = pl.ds(t, NBLK, stride=BLK)
            qs[n, there, :] = slots[t * GROUP + n, 0:NBLK, :].astype(F32)
            gs[n, there, :] = slots[SEQ // 2 + t * GROUP + n, 0:NBLK, :].astype(F32)
    small[...] = slots[:, NBLK:SLOT, :].astype(F32)
    pieces = [small[pl.ds(r * 8, 8), b, :][None] for r in range(8) for b in range(6)]
    plain = swap_groups(jnp.concatenate(pieces, axis=0))
    for r in range(8):
        ks[r // 4, pl.ds(r % 4, NBLK, stride=BLK), :] = plain[r * 6 : r * 6 + 6].reshape(NBLK, DH)
    k = ks[0].astype(BF16)
    v = ks[1].astype(BF16)
    allowed = causal(col_ref[...], row_ref[...], 0)
    dk = jnp.zeros((QUART, DH), F32)
    dv = jnp.zeros((QUART, DH), F32)
    for n in range(GROUP):
        at = pl.ds(n * DH, DH)
        out, dq, dk_part, dv_part = attend(
            qs[n].astype(BF16), gs[n].astype(BF16), k, v, allowed
        )
        out_ref[:, at] = out
        dq_ref[:, at] = dq
        dk += dk_part
        dv += dv_part
    dk_ref[...] = dk.astype(BF16)
    dv_ref[...] = dv.astype(BF16)


def attend_tail(slots, seg_col, seg_row, partial):
    any_spec = pl.BlockSpec(memory_space=pl.ANY)
    last = lambda i: (3, 0)
    return pl.pallas_call(
        tail_kernel,
        grid=(1,),
        in_specs=[
            pl.BlockSpec((SEQ, SLOT, DH), lambda i: (0, 0, 0)),
            pl.BlockSpec((QUART, 1), last),
            pl.BlockSpec((1, QUART), lambda i: (0, 0)),
        ]
        + [any_spec] * 4,
        out_specs=[
            pl.BlockSpec((QUART, QW), last),
            pl.BlockSpec((QUART, QW), last),
            pl.BlockSpec((QUART, DH), last),
            pl.BlockSpec((QUART, DH), last),
        ],
        out_shape=OUT_SHAPES,
        input_output_aliases={3: 0, 4: 1, 5: 2, 6: 3},
        scratch_shapes=[
            pltpu.VMEM((GROUP, QUART, DH), F32),
            pltpu.VMEM((GROUP, QUART, DH), F32),
            pltpu.VMEM((2, QUART, DH), F32),
            pltpu.VMEM((SEQ, 8, DH), F32),
        ],
        compiler_params=params(),
        cost_estimate=pl.CostEstimate(
            flops=6 * 2 * GROUP * QUART * QUART * DH,
            bytes_accessed=2_000_000,
            transcendentals=GROUP * QUART * QUART,
        ),
        name="attend_tail",
    )(slots, seg_col, seg_row, *partial)


def on_device(queries, key_rows, value_rows, out_grad, mover_dest, segment_ids):
    me = lax.axis_index("head").astype(jnp.int32)
    held = (queries, key_rows, value_rows, out_grad)
    send = lambda x, *pairs: lax.ppermute(x, "head", list(pairs))
    plan_row = jnp.pad(mover_dest, (0, DH - NBLK)).reshape(1, DH)
    seg_col = segment_ids.reshape(ROWS, 1)
    seg_row = segment_ids.reshape(1, ROWS)

    one_lo, one_hi = pack_tail(*held, plan_row, 1)
    at_zero = send(one_lo, (3, 0))
    at_two = send(one_hi, (3, 2))
    to_zero = [send(x, (3, 0)) for x in pack_tail(*held, plan_row, 0)]
    to_two = [send(x, (3, 2)) for x in pack_tail(*held, plan_row, 2)]
    to_one = [send(at_zero, (0, 1)), send(at_two, (2, 1))]
    kept = pack_tail(*held, plan_row, 3)
    mine = []
    for half in range(2):
        other = jnp.where(me == 2, to_two[half], to_one[half])
        other = jnp.where(me == 0, to_zero[half], other)
        mine.append(jnp.where(me == 3, kept[half], other))
    slots = jnp.concatenate(mine, axis=0)

    pieces = lax.all_to_all(slots, "seq", split_axis=0, concat_axis=0, tiled=True)

    held_later = lax.optimization_barrier(held + (slots,))[:4]
    part = lambda shift: slice_group(*held_later, (me + shift) % 4)
    ahead, behind, across = part(1), part(3), part(2)
    relay = send(send(across, (1, 0)), (0, 3))
    plus = send(ahead, (0, 1), (1, 2), (2, 3))
    minus = send(behind, (1, 0), (2, 1), (0, 3))
    two = send(across, (0, 2), (2, 0))
    partial = attend_stay(me, held, (plus, minus, two, relay), seg_col, seg_row)

    routed = lax.all_to_all(route(pieces), "seq", split_axis=0, concat_axis=0, tiled=True)
    return attend_tail(routed, seg_col, seg_row[:, STAY:], partial)


def solution(mesh):
    rows = P(("seq", "head"), None)
    spread = P("seq", "head")
    return jax.shard_map(
        on_device,
        mesh=mesh,
        in_specs=(rows, rows, rows, rows, P("seq"), P("seq")),
        out_specs=(spread, spread, spread, spread),
        check_vma=False,
    )
```

time: 844 us -> 183 us (0.22); the launches traced: 829 us -> 182 us
  blocking collectives: 369 us -> 0 us
  local copies, waits for them, and re-layouts: 166 us -> 5.51 us
  waiting for transfers between devices: 156 us -> 66.1 us
  Pallas kernels: 0 us -> 59.1 us
  matrix products: 45.9 us -> 0 us
  other arithmetic: 36.5 us -> 1.18 us
    unnamed x1 -> x0, blocking collectives: 369 us -> none
    all_to_all x8 -> x2, waiting for transfers between devices: 156 us -> 22.3 us  [the longest x1 22.3 us: on_device(): lax.all_to_all(slots, 'seq', split_axis=0, concat_axis=0, tiled=True)]
    scatter x8 -> x0, local copies, waits for them, and re-layouts: 84.7 us -> none  [the longest x4 61.9 us: assemble(): area = jnp.zeros((movers, BLK, column_count), member.dtype).at[slots].set...]
    pallas_call x0 -> x10, Pallas kernels: none -> 59.1 us  [the longest x1 25.6 us: attend_stay(): pl.pallas_call(stay_kernel, grid_spec=pltpu.PrefetchScalarGridSpec(num_sc...]
    dot_general x6 -> x0, matrix products: 45.9 us -> none  [the longest x1 17.9 us: attend_shard(): jnp.einsum('qkgd,pkd->kgqp', grad_heads, value_heads, preferred_element_t...]
    ppermute x0 -> x13, waiting for transfers between devices: none -> 43.8 us  [on_device(): send = lambda x, *pairs: lax.ppermute(x, 'head', list(pairs))]
    another operation x10 -> x0, local copies, waits for them, and re-layouts: 41.9 us -> none
    all_to_all x8 -> x2, starting transfers between devices: 53.2 us -> 22.9 us  [the longest x1 16.6 us: on_device(): lax.all_to_all(slots, 'seq', split_axis=0, concat_axis=0, tiled=True)]
  transfers between devices with their start and end apart: 8 -> 15, of which waited for: 4 -> 8; matrix products, arithmetic and copies ran while one was open for 18% -> 1% of each run, Pallas kernels for 0% -> 27%
where the time goes in v1:
time: 183 us; the launch traced here: 182 us
  waiting for transfers between devices  66.1 us (36%)
  Pallas kernels  59.1 us (32%)
  starting transfers between devices  48.9 us (27%)
  local copies, waits for them, and re-layouts  5.51 us (3%)
    ppermute x13, waiting for transfers between devices, on_device(): send = lambda x, *pairs: lax.ppermute(x, 'head', list(pairs))  43.8 us
    ppermute x13, starting transfers between devices, on_device(): send = lambda x, *pairs: lax.ppermute(x, 'head', list(pairs))  26 us
    pallas_call x1, Pallas kernels, attend_stay(): pl.pallas_call(stay_kernel, grid_spec=pltpu.PrefetchScalarGridSpec(num_sc...  25.6 us
    all_to_all x1, waiting for transfers between devices, on_device(): lax.all_to_all(slots, 'seq', split_axis=0, concat_axis=0, tiled=True)  22.3 us
    all_to_all x1, starting transfers between devices, on_device(): lax.all_to_all(slots, 'seq', split_axis=0, concat_axis=0, tiled=True)  16.6 us
    pallas_call x4, Pallas kernels, pack_tail(): pl.pallas_call(pack_kernel, grid=(1,), in_specs=[pl.BlockSpec((QUART, QW)...  10.7 us
    pallas_call x1, Pallas kernels, route(): pl.pallas_call(route_kernel, in_specs=[pl.BlockSpec(memory_space=pltpu.VM...  9.63 us
    pallas_call x1, Pallas kernels, attend_tail(): pl.pallas_call(tail_kernel, grid=(1,), in_specs=[pl.BlockSpec((SEQ, SLOT,...  6.71 us
  transfers between devices with their start and end apart: 15, of which 8 were waited for; matrix products, arithmetic and copies ran while one was open for 1% of the time, Pallas kernels for 27%

profile of v1, /device:TPU:1, one launch (start us, length us, event | category | flops | bytes accessed | tf_op | source)
XLA Modules:
  0.0 181.7 jit_solution(14902055688549893491)
XLA Ops:
  0.6 1.2 pad_bitcast_fusion.plan_ref
  1.8 2.7 %pack_tail.7 = (bf16[32,56,128]{2,1,0:T(8,128)(2,1)}, bf16[32,56,128]{2,1,0:T(8,128)(2,1)}) custom-call(bf16[192,4096]{1,0:T(8,128)(2,1)} %q_any.1, bf16[192,512]{1,0:T(8,128)(2,1)} %k_any.1, bf16[192,512]{1,0:T(8,128)(2,1)} %v_any.1, bf16[192,4096]{1,0:T(8,128)(2,1)} %g_any.1, s32[1,128]{1,0:T(1,128)} %pad_bitcast_fusion.plan_ref), custom_call_target="tpu_custom_call" | custom-call | bytes 2000000 | tf_op jit(solution)/shard_map/pack_tail/pallas_call | solution.py:72
  4.5 1.4 collective-permute-start.2
  5.9 2.7 %pack_tail.5 = (bf16[32,56,128]{2,1,0:T(8,128)(2,1)}, bf16[32,56,128]{2,1,0:T(8,128)(2,1)}) custom-call(bf16[192,4096]{1,0:T(8,128)(2,1)} %q_any.1, bf16[192,512]{1,0:T(8,128)(2,1)} %k_any.1, bf16[192,512]{1,0:T(8,128)(2,1)} %v_any.1, bf16[192,4096]{1,0:T(8,128)(2,1)} %g_any.1, s32[1,128]{1,0:T(1,128)} %pad_bitcast_fusion.plan_ref), custom_call_target="tpu_custom_call" | custom-call | bytes 2000000 | tf_op jit(solution)/shard_map/pack_tail/pallas_call | solution.py:72
  8.6 1.3 collective-permute-start
  9.9 1.4 collective-permute-start.6
  11.3 2.7 %pack_tail.6 = (bf16[32,56,128]{2,1,0:T(8,128)(2,1)}, bf16[32,56,128]{2,1,0:T(8,128)(2,1)}) custom-call(bf16[192,4096]{1,0:T(8,128)(2,1)} %q_any.1, bf16[192,512]{1,0:T(8,128)(2,1)} %k_any.1, bf16[192,512]{1,0:T(8,128)(2,1)} %v_any.1, bf16[192,4096]{1,0:T(8,128)(2,1)} %g_any.1, s32[1,128]{1,0:T(1,128)} %pad_bitcast_fusion.plan_ref), custom_call_target="tpu_custom_call" | custom-call | bytes 2000000 | tf_op jit(solution)/shard_map/pack_tail/pallas_call | solution.py:72
  14.7 2.1 %collective-permute-done.2 = bf16[32,56,128]{2,1,0:T(8,128)(2,1)} collective-permute-done((bf16[32,56,128]{2,1,0:T(8,128)(2,1)}, bf16[32,56,128]{2,1,0:T(8,128)(2,1)}, u32[]{:S(2)}, u32[]{:S(2)}) %collective-permute-start.2) | collective-permute-done | bytes 458784 | tf_op jit(solution)/shard_map/ppermute | solution.py:412
  16.8 1.4 collective-permute-start.3
  18.2 1.3 collective-permute-start.4
  19.5 7.0 %collective-permute-done = bf16[32,56,128]{2,1,0:T(8,128)(2,1)S(1)} collective-permute-done((bf16[32,56,128]{2,1,0:T(8,128)(2,1)}, bf16[32,56,128]{2,1,0:T(8,128)(2,1)S(1)}, u32[]{:S(2)}, u32[]{:S(2)}) %collective-permute-start) | collective-permute-done | bytes 458784 | tf_op jit(solution)/shard_map/ppermute | solution.py:412
  28.0 2.7 %pack_tail.4 = (bf16[32,56,128]{2,1,0:T(8,128)(2,1)}, bf16[32,56,128]{2,1,0:T(8,128)(2,1)}) custom-call(bf16[192,4096]{1,0:T(8,128)(2,1)} %q_any.1, bf16[192,512]{1,0:T(8,128)(2,1)} %k_any.1, bf16[192,512]{1,0:T(8,128)(2,1)} %v_any.1, bf16[192,4096]{1,0:T(8,128)(2,1)} %g_any.1, s32[1,128]{1,0:T(1,128)} %pad_bitcast_fusion.plan_ref), custom_call_target="tpu_custom_call" | custom-call | bytes 2000000 | tf_op jit(solution)/shard_map/pack_tail/pallas_call | solution.py:72
  30.7 5.6 %collective-permute-done.4 = bf16[32,56,128]{2,1,0:T(8,128)(2,1)S(1)} collective-permute-done((bf16[32,56,128]{2,1,0:T(8,128)(2,1)}, bf16[32,56,128]{2,1,0:T(8,128)(2,1)S(1)}, u32[]{:S(2)}, u32[]{:S(2)}) %collective-permute-start.4) | collective-permute-done | bytes 458784 | tf_op jit(solution)/shard_map/ppermute | solution.py:412
  36.5 1.0 pad_maximum_fusion
  37.5 16.6 %all-to-all-start = ((bf16[64,56,128]{2,1,0:T(8,128)(2,1)}), bf16[64,56,128]{2,1,0:T(8,128)(2,1)S(1)}, u32[]{:S(2)}, u32[]{:S(2)}) async-start(bf16[64,56,128]{2,1,0:T(8,128)(2,1)} %pad_maximum_fusion), calls=%async_computation | async-start | bytes 1835008 | tf_op jit(solution)/shard_map/all_to_all | solution.py:431
  54.1 2.2 %slice_group.5 = bf16[192,2304]{1,0:T(8,128)(2,1)} custom-call(s32[1]{0:T(128)} %bitcast.4.me_ref, bf16[192,4096]{1,0:T(8,128)(2,1)} %q_any.1, bf16[192,512]{1,0:T(8,128)(2,1)} %k_any.1, bf16[192,512]{1,0:T(8,128)(2,1)} %v_any.1, bf16[192,4096]{1,0:T(8,128)(2,1)} %g_any.1), custom_call_target="tpu_custom_call" | custom-call | bytes 1800000 | tf_op jit(solution)/shard_map/slice_group/pallas_call | solution.py:104
  56.3 1.3 collective-permute-start.11
  57.6 22.3 %all-to-all-done.in_ref = bf16[64,56,128]{2,1,0:T(8,128)(2,1)S(1)} async-done(((bf16[64,56,128]{2,1,0:T(8,128)(2,1)}), bf16[64,56,128]{2,1,0:T(8,128)(2,1)S(1)}, u32[]{:S(2)}, u32[]{:S(2)}) %all-to-all-start) | async-done | bytes 917536 | tf_op jit(solution)/shard_map/all_to_all | solution.py:431
  80.8 9.6 %route.1 = bf16[64,56,128]{2,1,0:T(8,128)(2,1)} custom-call(bf16[64,56,128]{2,1,0:T(8,128)(2,1)} %copy-done.1), custom_call_target="tpu_custom_call" | custom-call | flops 4831838208 | bytes 2000000 | tf_op jit(solution)/shard_map/route/pallas_call | solution.py:179
  90.4 6.3 %all-to-all-start.1 = ((bf16[64,56,128]{2,1,0:T(8,128)(2,1)}), bf16[64,56,128]{2,1,0:T(8,128)(2,1)S(1)}, u32[]{:S(2)}, u32[]{:S(2)}) async-start(bf16[64,56,128]{2,1,0:T(8,128)(2,1)} %route.1), calls=%async_computation.1 | async-start | bytes 1835008 | tf_op jit(solution)/shard_map/all_to_all | solution.py:442
  96.8 9.0 %collective-permute-start.10 = (bf16[192,2304]{1,0:T(8,128)(2,1)S(1)}, bf16[192,2304]{1,0:T(8,128)(2,1)S(1)}, u32[]{:S(2)}, u32[]{:S(2)}) collective-permute-start(bf16[192,2304]{1,0:T(8,128)(2,1)S(1)} %copy-done.2), channel_id=1, source_target_pairs={{0,2},{2,0},{4,6},{6,4},{8,10},{10,8},{12,14},{14,12},{16,18},{18,... | collective-permute-start | bytes 2654216 | tf_op jit(solution)/shard_map/ppermute | solution.py:412
  105.7 2.2 %slice_group.4 = bf16[192,2304]{1,0:T(8,128)(2,1)} custom-call(s32[1]{0:T(128)} %bitcast.3.me_ref, bf16[192,4096]{1,0:T(8,128)(2,1)} %q_any.1, bf16[192,512]{1,0:T(8,128)(2,1)} %k_any.1, bf16[192,512]{1,0:T(8,128)(2,1)} %v_any.1, bf16[192,4096]{1,0:T(8,128)(2,1)} %g_any.1), custom_call_target="tpu_custom_call" | custom-call | bytes 1800000 | tf_op jit(solution)/shard_map/slice_group/pallas_call | solution.py:104
  107.9 1.9 %collective-permute-start.9 = (bf16[192,2304]{1,0:T(8,128)(2,1)}, bf16[192,2304]{1,0:T(8,128)(2,1)S(1)}, u32[]{:S(2)}, u32[]{:S(2)}) collective-permute-start(bf16[192,2304]{1,0:T(8,128)(2,1)} %slice_group.4), channel_id=1, source_target_pairs={{1,0},{2,1},{0,3},{5,4},{6,5},{4,7},{9,8},{10,9},{8,11},{13,12},{1... | collective-permute-start | bytes 2654216 | tf_op jit(solution)/shard_map/ppermute | solution.py:412
  109.8 2.2 %slice_group.3 = bf16[192,2304]{1,0:T(8,128)(2,1)} custom-call(s32[1]{0:T(128)} %bitcast.2.me_ref, bf16[192,4096]{1,0:T(8,128)(2,1)} %q_any.1, bf16[192,512]{1,0:T(8,128)(2,1)} %k_any.1, bf16[192,512]{1,0:T(8,128)(2,1)} %v_any.1, bf16[192,4096]{1,0:T(8,128)(2,1)} %g_any.1), custom_call_target="tpu_custom_call" | custom-call | bytes 1800000 | tf_op jit(solution)/shard_map/slice_group/pallas_call | solution.py:104
  112.0 3.4 %collective-permute-start.8 = (bf16[192,2304]{1,0:T(8,128)(2,1)}, bf16[192,2304]{1,0:T(8,128)(2,1)S(1)}, u32[]{:S(2)}, u32[]{:S(2)}) collective-permute-start(bf16[192,2304]{1,0:T(8,128)(2,1)} %slice_group.3), channel_id=1, source_target_pairs={{0,1},{1,2},{2,3},{4,5},{5,6},{6,7},{8,9},{9,10},{10,11},{12,13},{... | collective-permute-start | bytes 2654216 | tf_op jit(solution)/shard_map/ppermute | solution.py:412
  115.4 1.5 collective-permute-start.12
  118.5 6.8 %collective-permute-done.10.two = bf16[192,2304]{1,0:T(8,128)(2,1)S(1)} collective-permute-done((bf16[192,2304]{1,0:T(8,128)(2,1)S(1)}, bf16[192,2304]{1,0:T(8,128)(2,1)S(1)}, u32[]{:S(2)}, u32[]{:S(2)}) %collective-permute-start.10) | collective-permute-done | bytes 884768 | tf_op jit(solution)/shard_map/ppermute | solution.py:412
  125.4 5.1 %collective-permute-done.9.minus = bf16[192,2304]{1,0:T(8,128)(2,1)S(1)} collective-permute-done((bf16[192,2304]{1,0:T(8,128)(2,1)}, bf16[192,2304]{1,0:T(8,128)(2,1)S(1)}, u32[]{:S(2)}, u32[]{:S(2)}) %collective-permute-start.9) | collective-permute-done | bytes 884768 | tf_op jit(solution)/shard_map/ppermute | solution.py:412
  130.4 13.0 %collective-permute-done.8.plus = bf16[192,2304]{1,0:T(8,128)(2,1)S(1)} collective-permute-done((bf16[192,2304]{1,0:T(8,128)(2,1)}, bf16[192,2304]{1,0:T(8,128)(2,1)S(1)}, u32[]{:S(2)}, u32[]{:S(2)}) %collective-permute-start.8) | collective-permute-done | bytes 884768 | tf_op jit(solution)/shard_map/ppermute | solution.py:412
  143.4 4.1 %collective-permute-done.12.relay = bf16[192,2304]{1,0:T(8,128)(2,1)S(1)} collective-permute-done((bf16[192,2304]{1,0:T(8,128)(2,1)S(1)}, bf16[192,2304]{1,0:T(8,128)(2,1)S(1)}, u32[]{:S(2)}, u32[]{:S(2)}) %collective-permute-start.12) | collective-permute-done | bytes 884768 | tf_op jit(solution)/shard_map/ppermute | solution.py:412
  148.5 25.6 %attend_stay.1 = (bf16[768,1024]{1,0:T(8,128)(2,1)}, bf16[768,1024]{1,0:T(8,128)(2,1)}, bf16[768,128]{1,0:T(8,128)(2,1)}, bf16[768,128]{1,0:T(8,128)(2,1)}) custom-call(s32[1]{0:T(128)} %bitcast.1.me_ref, bf16[192,4096]{1,0:T(8,128)(2,1)} %q_any.1, bf16[192,512]{1,0:T(8,128)(2,1)} %k_any.1, bf16[192,512]{1,0:T(8,128)(2,1)} %v_any.1, ...), custom_call_target="tpu_custom_call" | custom-call | flops 4076863488 | bytes 6000000 | tf_op jit(solution)/shard_map/attend_stay/pallas_call | solution.py:308
  175.0 6.7 %attend_tail.1 = (bf16[768,1024]{1,0:T(8,128)(2,1)}, bf16[768,1024]{1,0:T(8,128)(2,1)}, bf16[768,128]{1,0:T(8,128)(2,1)}, bf16[768,128]{1,0:T(8,128)(2,1)}) custom-call(bf16[64,56,128]{2,1,0:T(8,128)(2,1)} %copy-done, s32[768,1]{1,0:T(8,128)} %reshape.36.col_ref, ...), custom_call_target="tpu_custom_call", output_to_operand_aliasing={{0}: (3, {}), {1}: (4, {}), {2}: (5, {}), {3}: (6, {})} | custom-call | flops 452984832 | bytes 2000000 | tf_op jit(solution)/shard_map/attend_tail/pallas_call | solution.py:376
  (37 shorter events, 6.6 us)
Async XLA Ops:
  4.5 5.4 %copy-start.10 = (bf16[32,56,128]{2,1,0:T(8,128)(2,1)S(1)}, bf16[32,56,128]{2,1,0:T(8,128)(2,1)}, u32[]{:S(2)}) copy-start(bf16[32,56,128]{2,1,0:T(8,128)(2,1)} %get-tuple-element.27) | copy-start | bytes 1376260
  4.5 12.3 %collective-permute-start.2 = (bf16[32,56,128]{2,1,0:T(8,128)(2,1)}, bf16[32,56,128]{2,1,0:T(8,128)(2,1)}, u32[]{:S(2)}, u32[]{:S(2)}) collective-permute-start(bf16[32,56,128]{2,1,0:T(8,128)(2,1)} %get-tuple-element.23), channel_id=1, source_target_pairs={{3,0},{7,4},{11,8},{15,12},{19,16},{23,20},{27,24},{31,28},{35,32}... | collective-permute-start | bytes 1376264 | tf_op jit(solution)/shard_map/ppermute | solution.py:412
  8.6 18.0 %collective-permute-start = (bf16[32,56,128]{2,1,0:T(8,128)(2,1)}, bf16[32,56,128]{2,1,0:T(8,128)(2,1)S(1)}, u32[]{:S(2)}, u32[]{:S(2)}) collective-permute-start(bf16[32,56,128]{2,1,0:T(8,128)(2,1)} %get-tuple-element.21), channel_id=1, source_target_pairs={{3,0},{7,4},{11,8},{15,12},{19,16},{23,20},{27,24},{31,28},{35,32}... | collective-permute-start | bytes 1376264 | tf_op jit(solution)/shard_map/ppermute | solution.py:412
  9.9 17.4 %collective-permute-start.6 = (bf16[32,56,128]{2,1,0:T(8,128)(2,1)S(1)}, bf16[32,56,128]{2,1,0:T(8,128)(2,1)}, u32[]{:S(2)}, u32[]{:S(2)}) collective-permute-start(bf16[32,56,128]{2,1,0:T(8,128)(2,1)S(1)} %copy-done.10), channel_id=1, source_target_pairs={{3,2},{7,6},{11,10},{15,14},{19,18},{23,22},{27,26},{31,30},{35,34... | collective-permute-start | bytes 1376264 | tf_op jit(solution)/shard_map/ppermute | solution.py:412
  14.0 16.6 %collective-permute-start.1 = (bf16[32,56,128]{2,1,0:T(8,128)(2,1)}, bf16[32,56,128]{2,1,0:T(8,128)(2,1)S(1)}, u32[]{:S(2)}, u32[]{:S(2)}) collective-permute-start(bf16[32,56,128]{2,1,0:T(8,128)(2,1)} %get-tuple-element.22), channel_id=1, source_target_pairs={{3,2},{7,6},{11,10},{15,14},{19,18},{23,22},{27,26},{31,30},{35,34... | collective-permute-start | bytes 1376264 | tf_op jit(solution)/shard_map/ppermute | solution.py:412
  16.8 13.8 %collective-permute-start.3 = (bf16[32,56,128]{2,1,0:T(8,128)(2,1)}, bf16[32,56,128]{2,1,0:T(8,128)(2,1)S(1)}, u32[]{:S(2)}, u32[]{:S(2)}) collective-permute-start(bf16[32,56,128]{2,1,0:T(8,128)(2,1)} %collective-permute-done.2), channel_id=1, source_target_pairs={{0,1},{4,5},{8,9},{12,13},{16,17},{20,21},{24,25},{28,29},{32,33},... | collective-permute-start | bytes 1376264 | tf_op jit(solution)/shard_map/ppermute | solution.py:412
  18.2 18.1 %collective-permute-start.4 = (bf16[32,56,128]{2,1,0:T(8,128)(2,1)}, bf16[32,56,128]{2,1,0:T(8,128)(2,1)S(1)}, u32[]{:S(2)}, u32[]{:S(2)}) collective-permute-start(bf16[32,56,128]{2,1,0:T(8,128)(2,1)} %get-tuple-element.25), channel_id=1, source_target_pairs={{3,0},{7,4},{11,8},{15,12},{19,16},{23,20},{27,24},{31,28},{35,32}... | collective-permute-start | bytes 1376264 | tf_op jit(solution)/shard_map/ppermute | solution.py:412
  26.6 9.8 %collective-permute-start.5 = (bf16[32,56,128]{2,1,0:T(8,128)(2,1)}, bf16[32,56,128]{2,1,0:T(8,128)(2,1)S(1)}, u32[]{:S(2)}, u32[]{:S(2)}) collective-permute-start(bf16[32,56,128]{2,1,0:T(8,128)(2,1)} %get-tuple-element.26), channel_id=1, source_target_pairs={{3,2},{7,6},{11,10},{15,14},{19,18},{23,22},{27,26},{31,30},{35,34... | collective-permute-start | bytes 1376264 | tf_op jit(solution)/shard_map/ppermute | solution.py:412
  27.3 9.1 %collective-permute-start.7 = (bf16[32,56,128]{2,1,0:T(8,128)(2,1)}, bf16[32,56,128]{2,1,0:T(8,128)(2,1)S(1)}, u32[]{:S(2)}, u32[]{:S(2)}) collective-permute-start(bf16[32,56,128]{2,1,0:T(8,128)(2,1)} %collective-permute-done.6), channel_id=1, source_target_pairs={{2,1},{6,5},{10,9},{14,13},{18,17},{22,21},{26,25},{30,29},{34,33}... | collective-permute-start | bytes 1376264 | tf_op jit(solution)/shard_map/ppermute | solution.py:412
  30.6 5.8 %copy-start.3 = (bf16[32,56,128]{2,1,0:T(8,128)(2,1)S(1)}, bf16[32,56,128]{2,1,0:T(8,128)(2,1)}, u32[]{:S(2)}) copy-start(bf16[32,56,128]{2,1,0:T(8,128)(2,1)} %get-tuple-element.24) | copy-start | bytes 1376260
  37.5 42.4 %all-to-all-start = ((bf16[64,56,128]{2,1,0:T(8,128)(2,1)}), bf16[64,56,128]{2,1,0:T(8,128)(2,1)S(1)}, u32[]{:S(2)}, u32[]{:S(2)}) async-start(bf16[64,56,128]{2,1,0:T(8,128)(2,1)} %pad_maximum_fusion), calls=%async_computation | async-start | bytes 1835008 | tf_op jit(solution)/shard_map/all_to_all | solution.py:431
  56.3 59.1 %collective-permute-start.11 = (bf16[192,2304]{1,0:T(8,128)(2,1)}, bf16[192,2304]{1,0:T(8,128)(2,1)S(1)}, u32[]{:S(2)}, u32[]{:S(2)}) collective-permute-start(bf16[192,2304]{1,0:T(8,128)(2,1)} %slice_group.5), channel_id=1, source_target_pairs={{1,0},{5,4},{9,8},{13,12},{17,16},{21,20},{25,24},{29,28},{33,32},... | collective-permute-start | bytes 2654216 | tf_op jit(solution)/shard_map/ppermute | solution.py:412
  79.9 0.9 copy-start.1
  90.4 6.4 %copy-start.2 = (bf16[192,2304]{1,0:T(8,128)(2,1)S(1)}, bf16[192,2304]{1,0:T(8,128)(2,1)}, u32[]{:S(2)}) copy-start(bf16[192,2304]{1,0:T(8,128)(2,1)} %slice_group.5) | copy-start | bytes 2654212
  90.4 83.7 %all-to-all-start.1 = ((bf16[64,56,128]{2,1,0:T(8,128)(2,1)}), bf16[64,56,128]{2,1,0:T(8,128)(2,1)S(1)}, u32[]{:S(2)}, u32[]{:S(2)}) async-start(bf16[64,56,128]{2,1,0:T(8,128)(2,1)} %route.1), calls=%async_computation.1 | async-start | bytes 1835008 | tf_op jit(solution)/shard_map/all_to_all | solution.py:442
  96.8 28.6 %collective-permute-start.10 = (bf16[192,2304]{1,0:T(8,128)(2,1)S(1)}, bf16[192,2304]{1,0:T(8,128)(2,1)S(1)}, u32[]{:S(2)}, u32[]{:S(2)}) collective-permute-start(bf16[192,2304]{1,0:T(8,128)(2,1)S(1)} %copy-done.2), channel_id=1, source_target_pairs={{0,2},{2,0},{4,6},{6,4},{8,10},{10,8},{12,14},{14,12},{16,18},{18,... | collective-permute-start | bytes 2654216 | tf_op jit(solution)/shard_map/ppermute | solution.py:412
  107.9 22.5 %collective-permute-start.9 = (bf16[192,2304]{1,0:T(8,128)(2,1)}, bf16[192,2304]{1,0:T(8,128)(2,1)S(1)}, u32[]{:S(2)}, u32[]{:S(2)}) collective-permute-start(bf16[192,2304]{1,0:T(8,128)(2,1)} %slice_group.4), channel_id=1, source_target_pairs={{1,0},{2,1},{0,3},{5,4},{6,5},{4,7},{9,8},{10,9},{8,11},{13,12},{1... | collective-permute-start | bytes 2654216 | tf_op jit(solution)/shard_map/ppermute | solution.py:412
  109.8 7.1 %copy-start.4 = (s32[768]{0:T(1024)S(1)}, s32[768]{0:T(1024)}, u32[]{:S(2)}) copy-start(s32[768]{0:T(1024)} %param.11) | copy-start | bytes 9220
  112.0 31.4 %collective-permute-start.8 = (bf16[192,2304]{1,0:T(8,128)(2,1)}, bf16[192,2304]{1,0:T(8,128)(2,1)S(1)}, u32[]{:S(2)}, u32[]{:S(2)}) collective-permute-start(bf16[192,2304]{1,0:T(8,128)(2,1)} %slice_group.3), channel_id=1, source_target_pairs={{0,1},{1,2},{2,3},{4,5},{5,6},{6,7},{8,9},{9,10},{10,11},{12,13},{... | collective-permute-start | bytes 2654216 | tf_op jit(solution)/shard_map/ppermute | solution.py:412
  115.4 32.1 %collective-permute-start.12 = (bf16[192,2304]{1,0:T(8,128)(2,1)S(1)}, bf16[192,2304]{1,0:T(8,128)(2,1)S(1)}, u32[]{:S(2)}, u32[]{:S(2)}) collective-permute-start(bf16[192,2304]{1,0:T(8,128)(2,1)S(1)} %collective-permute-done.11), channel_id=1, source_target_pairs={{0,3},{4,7},{8,11},{12,15},{16,19},{20,23},{24,27},{28,31},{32,35}... | collective-permute-start | bytes 2654216 | tf_op jit(solution)/shard_map/ppermute | solution.py:412
  117.9 29.7 %copy-start.5 = (s32[1,768]{1,0:T(1,128)}, s32[1,768]{1,0:T(1,128)S(1)}, u32[]{:S(2)}) copy-start(s32[1,768]{1,0:T(1,128)S(1)} %reshape.31.row_ref) | copy-start | bytes 9220
  125.4 22.2 %copy-start.6 = (bf16[192,2304]{1,0:T(8,128)(2,1)}, bf16[192,2304]{1,0:T(8,128)(2,1)S(1)}, u32[]{:S(2)}) copy-start(bf16[192,2304]{1,0:T(8,128)(2,1)S(1)} %collective-permute-done.10.two) | copy-start | bytes 2654212
  130.4 17.1 %copy-start.7 = (bf16[192,2304]{1,0:T(8,128)(2,1)}, bf16[192,2304]{1,0:T(8,128)(2,1)S(1)}, u32[]{:S(2)}) copy-start(bf16[192,2304]{1,0:T(8,128)(2,1)S(1)} %collective-permute-done.9.minus) | copy-start | bytes 2654212
  143.4 4.1 %copy-start.8 = (bf16[192,2304]{1,0:T(8,128)(2,1)}, bf16[192,2304]{1,0:T(8,128)(2,1)S(1)}, u32[]{:S(2)}) copy-start(bf16[192,2304]{1,0:T(8,128)(2,1)S(1)} %collective-permute-done.8.plus) | copy-start | bytes 2654212
  147.5 0.9 copy-start.9
  174.1 0.9 copy-start

commit v2 on v1

v2 whole, which is shorter than its diff:
```python
import math

import jax
import jax.numpy as jnp
from jax import lax
from jax.experimental import pallas as pl
from jax.experimental.pallas import tpu as pltpu
from jax.sharding import PartitionSpec as P

DH = 128
GROUP = 8
QW = GROUP * DH
ROWS = 768
QUART = 192
STAY = 576
BLK = 4
NBLK = 48
SEQ = 64
WIDE = 2 * QW + 2 * DH
FIRST = 16
REST = NBLK - FIRST
SLOT_A = FIRST + 8
SLOT = NBLK + 8
INV = 1.0 / math.sqrt(DH)
LOG2E = math.log2(math.e)
NEG = -1e30
F32 = jnp.float32
BF16 = jnp.bfloat16
VMEM_LIMIT = 56 * 1024 * 1024


def params():
    return pltpu.CompilerParams(vmem_limit_bytes=VMEM_LIMIT)


def cost(flops, bytes_accessed, transcendentals=0):
    return pl.CostEstimate(
        flops=flops, bytes_accessed=bytes_accessed, transcendentals=transcendentals
    )


def iota(shape, axis):
    return lax.broadcasted_iota(jnp.int32, shape, axis)


def swap_groups(x):
    sub = iota(x.shape, 1)
    grp = iota(x.shape, 2) // 16
    for bit in (1, 2, 4):
        s_on = (sub & bit) != 0
        l_on = (grp & bit) != 0
        up = pltpu.roll(pltpu.roll(x, 8 - bit, 1), 16 * bit, 2)
        down = pltpu.roll(pltpu.roll(x, bit, 1), 128 - 16 * bit, 2)
        x = jnp.where(s_on == l_on, x, jnp.where(l_on, up, down))
    return x


def split_rows(src, dst, first, count, qs):
    for n in range(GROUP):
        qs[n] = src[:, n * DH : (n + 1) * DH].astype(F32)
        for t in range(BLK):
            rows = qs[n, pl.ds(first * BLK + t, count, stride=BLK), :]
            dst[t * GROUP + n, 0:count, :] = rows.astype(BF16)


ORDER = (1, 0, 2, 3)


def pack_a_kernel(q_ref, k_ref, v_ref, g_ref, plan_ref, o1, o0, o2, o3, qs, ks, small):
    half = SEQ // 2
    plan = jnp.concatenate([plan_ref[...], jnp.zeros((1, DH - NBLK), jnp.int32)], axis=1)
    small[:, 6, :] = jnp.broadcast_to((plan // 64).astype(F32), (SEQ, DH))
    small[:, 7, :] = jnp.broadcast_to((plan % 64).astype(F32), (SEQ, DH))
    for group, out in zip(ORDER, (o1, o0, o2, o3)):
        thin = slice(group * DH, (group + 1) * DH)
        wide = slice(group * QW, (group + 1) * QW)
        ks[0] = k_ref[:, thin].astype(F32)
        ks[1] = v_ref[:, thin].astype(F32)
        pieces = []
        for r in range(8):
            rows = ks[r // 4, pl.ds(r % 4, NBLK, stride=BLK), :]
            pieces.append(rows.reshape(6, 8, DH))
        mixed = swap_groups(jnp.concatenate(pieces, axis=0))
        for r in range(8):
            for b in range(6):
                small[pl.ds(r * 8, 8), b, :] = mixed[r * 6 + b]
        for src, dst, start in ((q_ref, out.at[0:half], 0), (g_ref, out.at[half:SEQ], half)):
            split_rows(src.at[:, wide], dst, 0, FIRST, qs)
            dst[:, FIRST:SLOT_A, :] = small[pl.ds(start, half)].astype(BF16)


def pack_b_kernel(q_ref, g_ref, o1, o0, o2, o3, qs):
    half = SEQ // 2
    for group, out in zip(ORDER, (o1, o0, o2, o3)):
        wide = slice(group * QW, (group + 1) * QW)
        split_rows(q_ref.at[:, wide], out.at[0:half], FIRST, REST, qs)
        split_rows(g_ref.at[:, wide], out.at[half:SEQ], FIRST, REST, qs)


def packed_shapes(rows):
    return [jax.ShapeDtypeStruct((SEQ, rows, DH), BF16)] * 4


def pack_a(queries, key_rows, value_rows, out_grad, plan_row):
    shapes = packed_shapes(SLOT_A)
    top = lambda i: (0, 0)
    return pl.pallas_call(
        pack_a_kernel,
        grid=(1,),
        in_specs=[
            pl.BlockSpec((FIRST * BLK, 4 * QW), top),
            pl.BlockSpec((QUART, 4 * DH), top),
            pl.BlockSpec((QUART, 4 * DH), top),
            pl.BlockSpec((FIRST * BLK, 4 * QW), top),
            pl.BlockSpec((1, NBLK), top),
        ],
        out_specs=[pl.BlockSpec(x.shape, lambda i: (0, 0, 0)) for x in shapes],
        out_shape=shapes,
        scratch_shapes=[
            pltpu.VMEM((GROUP, FIRST * BLK, DH), F32),
            pltpu.VMEM((2, QUART, DH), F32),
            pltpu.VMEM((SEQ, 8, DH), F32),
        ],
        compiler_params=params(),
        cost_estimate=cost(0, 3_000_000),
        name="pack_a",
    )(queries, key_rows, value_rows, out_grad, plan_row)


def pack_b(queries, out_grad):
    shapes = packed_shapes(REST)
    return pl.pallas_call(
        pack_b_kernel,
        grid=(1,),
        in_specs=[pl.BlockSpec((QUART, 4 * QW), lambda i: (0, 0))] * 2,
        out_specs=[pl.BlockSpec(x.shape, lambda i: (0, 0, 0)) for x in shapes],
        out_shape=shapes,
        scratch_shapes=[pltpu.VMEM((GROUP, QUART, DH), F32)],
        compiler_params=params(),
        cost_estimate=cost(0, 5_000_000),
        name="pack_b",
    )(queries, out_grad)


def slice_kernel(me_ref, q_ref, k_ref, v_ref, g_ref, o_ref):
    o_ref[:, 0:QW] = q_ref[...]
    o_ref[:, QW : 2 * QW] = g_ref[...]
    o_ref[:, 2 * QW : 2 * QW + DH] = k_ref[...]
    o_ref[:, 2 * QW + DH : WIDE] = v_ref[...]


def slice_group(queries, key_rows, value_rows, out_grad, group):
    column = lambda i, g: (0, g[0])
    return pl.pallas_call(
        slice_kernel,
        grid_spec=pltpu.PrefetchScalarGridSpec(
            num_scalar_prefetch=1,
            grid=(1,),
            in_specs=[
                pl.BlockSpec((QUART, QW), column),
                pl.BlockSpec((QUART, DH), column),
                pl.BlockSpec((QUART, DH), column),
                pl.BlockSpec((QUART, QW), column),
            ],
            out_specs=pl.BlockSpec((QUART, WIDE), lambda i, g: (0, 0)),
        ),
        out_shape=jax.ShapeDtypeStruct((QUART, WIDE), BF16),
        compiler_params=params(),
        cost_estimate=cost(0, 1_800_000),
        name="slice_group",
    )(group.reshape(1), queries, key_rows, value_rows, out_grad)


def plan_lines(tail, first, count):
    total = SEQ * count
    col = iota((1, total), 1).astype(F32)
    owner = jnp.floor((col + 0.5) * (1.0 / count))
    place = col - owner * count + first
    pick = (iota((DH, total), 0).astype(F32) == place).astype(BF16)
    mine = iota((SEQ, total), 0).astype(F32) == owner
    lines = []
    for row in (6, 7):
        spread = jnp.dot(tail[:, row, :].astype(BF16), pick, preferred_element_type=F32)
        lines.append(jnp.sum(jnp.where(mine, spread, 0.0), axis=0, keepdims=True))
    return lines


def low_choice(line):
    return (iota((64, line.shape[1]), 0).astype(F32) == line).astype(BF16)


def choose(sel, low, line, first, runs):
    for k in range(runs):
        row = jnp.where(line == float(first + k), 1.0, 0.0).astype(BF16)
        sel[k * 64 : (k + 1) * 64, :] = low * row


PARTS = 4
TILE = SEQ * NBLK // PARTS
RUNS = TILE // 64
SHARDS = TILE // NBLK


def merge(got, here, shard, out_ref, part_ref=None):
    out = got[:, 0:DH].astype(BF16)
    kept = jnp.where(here, got[:, DH : 2 * DH], 0.0)
    sums = [jnp.sum(kept[b * 8 : b * 8 + 8], axis=0, keepdims=True) for b in range(6)]
    packed = jnp.concatenate(sums + [jnp.zeros((2, DH), F32)], axis=0).astype(BF16)
    if part_ref is not None:
        out += part_ref[shard, 0:NBLK, :]
        packed += part_ref[shard, NBLK:SLOT, :]
    out_ref[shard, 0:NBLK, :] = out
    out_ref[shard, NBLK:SLOT, :] = packed


def lane_is_row():
    return iota((NBLK, DH), 1) // 16 == iota((NBLK, DH), 0) % 8


def route_a_kernel(in_ref, out_ref, line_ref, low_ref, rest_ref, xs, ks, sel, low_a):
    tail = in_ref[:, FIRST:SLOT_A, :].astype(F32)
    high_a, digits_a = plan_lines(tail, 0, FIRST)
    high_b, digits_b = plan_lines(tail, FIRST, REST)
    line_ref[...] = jnp.broadcast_to(high_b, line_ref.shape)
    low_ref[...] = low_choice(digits_b)
    low_a[...] = low_choice(digits_a)

    here = lane_is_row()
    fold = (iota((DH, DH), 0) % 16 == iota((DH, DH), 1) % 16).astype(BF16)
    for s in range(SEQ):
        xs[s * FIRST : (s + 1) * FIRST, 0:DH] = in_ref[s, 0:FIRST, :]
        rows = [jnp.broadcast_to(tail[s, b : b + 1, :], (8, DH)) for b in range(6)]
        wide = jnp.where(here, jnp.concatenate(rows, axis=0), 0.0).astype(BF16)
        ks[s * FIRST : (s + 1) * FIRST, :] = wide[0:FIRST]
        rest_ref[s * REST : (s + 1) * REST, :] = wide[FIRST:NBLK]
    xs[:, DH : 2 * DH] = jnp.dot(ks[...], fold, preferred_element_type=F32).astype(BF16)
    rest_ref[...] = jnp.dot(rest_ref[...], fold, preferred_element_type=F32).astype(BF16)
    for p in range(PARTS):
        choose(sel.at[p % 2], low_a[...], high_a, p * RUNS, RUNS)
        got = jnp.dot(sel[p % 2], xs[...], preferred_element_type=F32)
        for d in range(SHARDS):
            merge(got[d * NBLK : (d + 1) * NBLK], here, p * SHARDS + d, out_ref)


def route_a(slots):
    vmem = pl.BlockSpec(memory_space=pltpu.VMEM)
    return pl.pallas_call(
        route_a_kernel,
        in_specs=[vmem],
        out_specs=[vmem] * 4,
        out_shape=[
            jax.ShapeDtypeStruct((SEQ, SLOT, DH), BF16),
            jax.ShapeDtypeStruct((8, SEQ * REST), F32),
            jax.ShapeDtypeStruct((64, SEQ * REST), BF16),
            jax.ShapeDtypeStruct((SEQ * REST, DH), BF16),
        ],
        scratch_shapes=[
            pltpu.VMEM((SEQ * FIRST, 2 * DH), BF16),
            pltpu.VMEM((SEQ * FIRST, DH), BF16),
            pltpu.VMEM((2, TILE, SEQ * FIRST), BF16),
            pltpu.VMEM((64, SEQ * FIRST), BF16),
        ],
        compiler_params=params(),
        cost_estimate=cost(4 * SEQ * NBLK * SEQ * FIRST * DH, 2_000_000),
        name="route_a",
    )(slots)


def route_b_kernel(in_ref, part_ref, line_ref, low_ref, rest_ref, out_ref, xs, sel):
    xs[:, 0:DH] = in_ref[...].reshape(SEQ * REST, DH)
    xs[:, DH : 2 * DH] = rest_ref[...]
    here = lane_is_row()
    line = line_ref[0:1, :]
    for p in range(PARTS):
        choose(sel.at[p % 2], low_ref[...], line, p * RUNS, RUNS)
        got = jnp.dot(sel[p % 2], xs[...], preferred_element_type=F32)
        for d in range(SHARDS):
            merge(got[d * NBLK : (d + 1) * NBLK], here, p * SHARDS + d, out_ref, part_ref)


def route_b(slots, part, line, low, rest):
    vmem = pl.BlockSpec(memory_space=pltpu.VMEM)
    return pl.pallas_call(
        route_b_kernel,
        in_specs=[vmem] * 5,
        out_specs=vmem,
        out_shape=jax.ShapeDtypeStruct((SEQ, SLOT, DH), BF16),
        scratch_shapes=[
            pltpu.VMEM((SEQ * REST, 2 * DH), BF16),
            pltpu.VMEM((2, TILE, SEQ * REST), BF16),
        ],
        compiler_params=params(),
        cost_estimate=cost(4 * SEQ * NBLK * SEQ * REST * DH, 3_000_000),
        name="route_b",
    )(slots, part, line, low, rest)


def dot(a, b, dims):
    return lax.dot_general(a, b, (dims, ((), ())), preferred_element_type=F32)


NT = ((1,), (1,))
NN = ((1,), (0,))


def attend(q, g, k, v, k_cols, v_cols, allowed):
    scores = jnp.where(allowed, dot(k, q, NT) * (INV * LOG2E), NEG)
    weights = jnp.exp2(scores - jnp.max(scores, axis=0, keepdims=True))
    probs = weights * (1.0 / jnp.sum(weights, axis=0, keepdims=True))
    probs_low = probs.astype(BF16)
    grad_probs = dot(v, g, NT)
    centre = jnp.sum(probs * grad_probs, axis=0, keepdims=True)
    grad_scores = (probs * (grad_probs - centre) * INV).astype(BF16)
    out_cols = dot(v_cols, probs_low, NN)
    dq_cols = dot(k_cols, grad_scores, NN)
    return out_cols, dq_cols, dot(grad_scores, q, NN), dot(probs_low, g, NN)


def causal(seg_col, seg_row, first):
    j = iota((seg_col.shape[0], DH), 0)
    i = iota((seg_col.shape[0], DH), 1) + first
    return (seg_col == seg_row) & (j <= i)


PAD = 640
PAIR = 2


def stay_kernel(
    me_ref, q_any, k_any, v_any, g_any, plus, minus, two, col_ref, row_ref,
    out_ref, dq_ref, dk_ref, dv_ref, rows, kt, vt, dk, dv, sems,
):
    me = me_ref[0]

    def fetch(src, part):
        pltpu.make_async_copy(src, rows.at[pl.ds(part * QUART, QUART), :], sems.at[part]).start()

    wide = pl.ds(pl.multiple_of(me * QW, QW), QW)
    thin = pl.ds(pl.multiple_of(me * DH, DH), DH)

    def own(part):
        there = pl.ds(part * QUART, QUART)
        columns = (0, QW, 2 * QW, 2 * QW + DH, WIDE)
        for n, (src, at) in enumerate(((q_any, wide), (g_any, wide), (k_any, thin), (v_any, thin))):
            pltpu.make_async_copy(
                src.at[:, at], rows.at[there, columns[n] : columns[n + 1]], sems.at[part]
            ).start()

    @pl.when(me == 0)
    def _():
        own(0)
        fetch(minus, 1)
        fetch(two, 2)

    @pl.when(me == 1)
    def _():
        fetch(plus, 0)
        own(1)
        fetch(minus, 2)

    @pl.when(me == 2)
    def _():
        fetch(two, 0)
        fetch(plus, 1)
        own(2)

    @pl.when(me == 3)
    def _():
        fetch(minus, 0)
        fetch(two, 1)
        fetch(plus, 2)

    dk[...] = jnp.zeros_like(dk)
    dv[...] = jnp.zeros_like(dv)
    rows[STAY:PAD, :] = jnp.zeros((PAD - STAY, WIDE), BF16)
    for part in range(3):
        pltpu.make_async_copy(plus, rows.at[pl.ds(part * QUART, QUART), :], sems.at[part]).wait()
    kt[...] = rows[:, 2 * QW : 2 * QW + DH].astype(F32).T.astype(BF16)
    vt[...] = rows[:, 2 * QW + DH : WIDE].astype(F32).T.astype(BF16)

    for tile in range(PAD // DH):
        width = (tile + 1) * DH
        there = slice(tile * DH, width)
        count = min(DH, STAY - tile * DH)
        allowed = causal(col_ref[0:width, :], row_ref[:, there], tile * DH)
        allowed = jnp.concatenate([allowed] * PAIR, axis=1)

        for first in range(0, GROUP, PAIR):
            heads = range(first, first + PAIR)
            q = [rows[there, n * DH : (n + 1) * DH] for n in heads]
            g = [rows[there, QW + n * DH : QW + (n + 1) * DH] for n in heads]
            out, dq, dk_part, dv_part = attend(
                jnp.concatenate(q, axis=0),
                jnp.concatenate(g, axis=0),
                rows[0:width, 2 * QW : 2 * QW + DH],
                rows[0:width, 2 * QW + DH : WIDE],
                kt[:, 0:width],
                vt[:, 0:width],
                allowed,
            )
            for h, n in enumerate(heads):
                at = slice(n * DH, (n + 1) * DH)
                columns = slice(h * DH, (h + 1) * DH)
                out_ref[tile * DH : tile * DH + count, at] = out[:, columns].T[0:count].astype(BF16)
                dq_ref[tile * DH : tile * DH + count, at] = dq[:, columns].T[0:count].astype(BF16)
            dk[0:width, :] += dk_part
            dv[0:width, :] += dv_part

    dk_ref[...] = dk[0:STAY, :].astype(BF16)
    dv_ref[...] = dv[0:STAY, :].astype(BF16)


OUT_SHAPES = [
    jax.ShapeDtypeStruct((ROWS, QW), BF16),
    jax.ShapeDtypeStruct((ROWS, QW), BF16),
    jax.ShapeDtypeStruct((ROWS, DH), BF16),
    jax.ShapeDtypeStruct((ROWS, DH), BF16),
]


def attend_stay(me, held, received, seg_col, seg_row):
    any_spec = pl.BlockSpec(memory_space=pl.ANY)
    top = lambda n, m: (0, 0)
    return pl.pallas_call(
        stay_kernel,
        grid_spec=pltpu.PrefetchScalarGridSpec(
            num_scalar_prefetch=1,
            grid=(1,),
            in_specs=[any_spec] * 7 + [pl.BlockSpec((ROWS, 1), top), pl.BlockSpec((1, ROWS), top)],
            out_specs=[
                pl.BlockSpec((STAY, QW), top),
                pl.BlockSpec((STAY, QW), top),
                pl.BlockSpec((STAY, DH), top),
                pl.BlockSpec((STAY, DH), top),
            ],
            scratch_shapes=[
                pltpu.VMEM((PAD, WIDE), BF16),
                pltpu.VMEM((DH, PAD), BF16),
                pltpu.VMEM((DH, PAD), BF16),
                pltpu.VMEM((PAD, DH), F32),
                pltpu.VMEM((PAD, DH), F32),
                pltpu.SemaphoreType.DMA((3,)),
            ],
        ),
        out_shape=OUT_SHAPES,
        compiler_params=params(),
        cost_estimate=cost(60 * 2 * GROUP * STAY * STAY * DH, 6_000_000, GROUP * STAY * STAY),
        name="attend_stay",
    )(me.reshape(1), *held, *received, seg_col, seg_row)


SPAN = 2 * DH


def tail_kernel(
    slots, col_ref, row_ref, a0, a1, a2, a3, out_ref, dq_ref, dk_ref, dv_ref, qs, gs, ks, small
):
    pad = jnp.zeros((SPAN - QUART, DH), F32)
    for n in range(GROUP):
        qs[n, QUART:SPAN, :] = pad
        gs[n, QUART:SPAN, :] = pad
        for t in range(BLK):
            there = pl.ds(t, NBLK, stride=BLK)
            qs[n, there, :] = slots[t * GROUP + n, 0:NBLK, :].astype(F32)
            gs[n, there, :] = slots[SEQ // 2 + t * GROUP + n, 0:NBLK, :].astype(F32)
    small[...] = slots[:, NBLK:SLOT, :].astype(F32)
    pieces = [small[pl.ds(r * 8, 8), b, :][None] for r in range(8) for b in range(6)]
    plain = swap_groups(jnp.concatenate(pieces, axis=0))
    for r in range(8):
        ks[r // 4, pl.ds(r % 4, NBLK, stride=BLK), :] = plain[r * 6 : r * 6 + 6].reshape(NBLK, DH)
    for half in range(2):
        ks[half, QUART:SPAN, :] = pad
    for tile in range(2):
        first = tile * DH
        count = min(DH, QUART - first)
        there = slice(first, first + DH)
        k, v = ks[0, there, :], ks[1, there, :]
        allowed = causal(col_ref[there, :], row_ref[:, there], 0)
        out, dq, dk, dv = attend(
            qs[:, there, :].astype(BF16).reshape(QW, DH),
            gs[:, there, :].astype(BF16).reshape(QW, DH),
            k.astype(BF16),
            v.astype(BF16),
            k.T.astype(BF16),
            v.T.astype(BF16),
            jnp.concatenate([allowed] * GROUP, axis=1),
        )
        for n in range(GROUP):
            at = slice(n * DH, (n + 1) * DH)
            out_ref[first : first + count, at] = out[:, at].T[0:count].astype(BF16)
            dq_ref[first : first + count, at] = dq[:, at].T[0:count].astype(BF16)
        dk_ref[first : first + count, :] = dk[0:count].astype(BF16)
        dv_ref[first : first + count, :] = dv[0:count].astype(BF16)


def attend_tail(slots, seg_col, seg_row, partial):
    any_spec = pl.BlockSpec(memory_space=pl.ANY)
    last = lambda i: (3, 0)
    return pl.pallas_call(
        tail_kernel,
        grid=(1,),
        in_specs=[
            pl.BlockSpec((SEQ, SLOT, DH), lambda i: (0, 0, 0)),
            pl.BlockSpec((SPAN, 1), lambda i: (0, 0)),
            pl.BlockSpec((1, SPAN), lambda i: (0, 0)),
        ]
        + [any_spec] * 4,
        out_specs=[
            pl.BlockSpec((QUART, QW), last),
            pl.BlockSpec((QUART, QW), last),
            pl.BlockSpec((QUART, DH), last),
            pl.BlockSpec((QUART, DH), last),
        ],
        out_shape=OUT_SHAPES,
        input_output_aliases={3: 0, 4: 1, 5: 2, 6: 3},
        scratch_shapes=[
            pltpu.VMEM((GROUP, SPAN, DH), F32),
            pltpu.VMEM((GROUP, SPAN, DH), F32),
            pltpu.VMEM((2, SPAN, DH), F32),
            pltpu.VMEM((SEQ, 8, DH), F32),
        ],
        compiler_params=params(),
        cost_estimate=cost(6 * 2 * GROUP * QUART * DH * DH, 2_000_000, GROUP * QUART * DH),
        name="attend_tail",
    )(slots, seg_col, seg_row, *partial)


def after(values, *others):
    return lax.optimization_barrier((tuple(values), others))[0]


def on_device(queries, key_rows, value_rows, out_grad, mover_dest, segment_ids):
    me = lax.axis_index("head").astype(jnp.int32)
    held = (queries, key_rows, value_rows, out_grad)
    send = lambda x, *pairs: lax.ppermute(x, "head", list(pairs))
    exchange = lambda x: lax.all_to_all(x, "seq", split_axis=0, concat_axis=0, tiled=True)

    def scatter(one, zero, two, three):
        parts = (send(one, (3, 1)), send(zero, (3, 0)), send(two, (3, 2)))
        other = jnp.where(me == 0, parts[1], jnp.where(me == 2, parts[2], parts[0]))
        return jnp.where(me == 3, three, other), parts

    slots_a, sent_a = scatter(*pack_a(*held, mover_dest.reshape(1, NBLK)))
    part = lambda shift: slice_group(*held, (me + shift) % 4)
    slices = (part(1), part(3), part(2))
    slots_b, _ = scatter(*after(pack_b(queries, out_grad), *sent_a, *slices))

    pieces_a = exchange(slots_a)
    (next_b,) = after([slots_b], pieces_a)
    pieces_b = exchange(next_b)
    routed_a = route_a(pieces_a)

    ahead, behind, across = after(slices, slots_b)
    two = send(across, (0, 2), (2, 0), (1, 3))
    plus = send(ahead, (0, 1), (1, 2), (2, 3))
    minus = send(behind, (1, 0), (2, 1), (0, 3))

    routed = route_b(pieces_b, *routed_a)
    stay = after((plus, minus, two), routed)
    seg_col = segment_ids.reshape(ROWS, 1)
    seg_row = segment_ids.reshape(1, ROWS)
    tail_seg = jnp.pad(segment_ids[STAY:], (0, SPAN - QUART), constant_values=-1)
    partial = attend_stay(me, held, stay, seg_col, seg_row)
    arrived = exchange(routed)
    return attend_tail(arrived, tail_seg.reshape(SPAN, 1), tail_seg.reshape(1, SPAN), partial)


def solution(mesh):
    rows = P(("seq", "head"), None)
    spread = P("seq", "head")
    return jax.shard_map(
        on_device,
        mesh=mesh,
        in_specs=(rows, rows, rows, rows, P("seq"), P("seq")),
        out_specs=(spread, spread, spread, spread),
        check_vma=False,
    )
```

time: 183 us -> 137 us (0.75)
  waiting for transfers between devices: 66.1 us -> 25.7 us
  Pallas kernels: 59.1 us -> 45 us
  starting transfers between devices: 48.9 us -> 56.7 us
    ppermute x13 -> x9, waiting for transfers between devices: 43.8 us -> 10.9 us  [on_device(): send = lambda x, *pairs: lax.ppermute(x, 'head', list(pairs))]
    pallas_call x1, Pallas kernels: 25.6 us -> 15.8 us  [attend_stay(): pl.pallas_call(stay_kernel, grid_spec=pltpu.PrefetchScalarGridSpec(num_sc...]
    all_to_all x2 -> x3, starting transfers between devices: 22.9 us -> 30.7 us  [on_device(): lax.all_to_all(x, 'seq', split_axis=0, concat_axis=0, tiled=True)]
    all_to_all x2 -> x3, waiting for transfers between devices: 22.3 us -> 14.8 us  [on_device(): lax.all_to_all(x, 'seq', split_axis=0, concat_axis=0, tiled=True)]
    select_n x2, other arithmetic: 0.18 us -> 2.92 us  [scatter(): return (jnp.where(me == 3, three, other), parts)]
    pallas_call x1, Pallas kernels: 6.71 us -> 4.02 us  [attend_tail(): pl.pallas_call(tail_kernel, grid=(1,), in_specs=[pl.BlockSpec((SEQ, SLOT,...]
    pallas_call x5 -> x4, Pallas kernels: 20.4 us -> 18.7 us  [the longest x1 6.33 us: route_b(): pl.pallas_call(route_b_kernel, in_specs=[vmem] * 5, out_specs=vmem, out_s...]
    ppermute x13 -> x9, starting transfers between devices: 26 us -> 26 us  [on_device(): send = lambda x, *pairs: lax.ppermute(x, 'head', list(pairs))]
  transfers between devices with their start and end apart: 15 -> 12, of which waited for: 8 -> 5; matrix products, arithmetic and copies ran while one was open for 1% -> 4% of each run, Pallas kernels for 27% -> 27%
where the time goes in v2:
time: 137 us; the launch traced here: 135 us
  starting transfers between devices  56.7 us (41%)
  Pallas kernels  45 us (33%)
  waiting for transfers between devices  25.7 us (19%)
  local copies, waits for them, and re-layouts  4.17 us (3%)
  other arithmetic  2.92 us (2%)
    all_to_all x3, starting transfers between devices, on_device(): lax.all_to_all(x, 'seq', split_axis=0, concat_axis=0, tiled=True)  30.7 us
    ppermute x9, starting transfers between devices, on_device(): send = lambda x, *pairs: lax.ppermute(x, 'head', list(pairs))  26 us
    pallas_call x1, Pallas kernels, attend_stay(): pl.pallas_call(stay_kernel, grid_spec=pltpu.PrefetchScalarGridSpec(num_sc...  15.8 us
    all_to_all x3, waiting for transfers between devices, on_device(): lax.all_to_all(x, 'seq', split_axis=0, concat_axis=0, tiled=True)  14.8 us
    ppermute x9, waiting for transfers between devices, on_device(): send = lambda x, *pairs: lax.ppermute(x, 'head', list(pairs))  10.9 us
    pallas_call x3, Pallas kernels, slice_group(): pl.pallas_call(slice_kernel, grid_spec=pltpu.PrefetchScalarGridSpec(num_s...  6.54 us
    pallas_call x1, Pallas kernels, route_b(): pl.pallas_call(route_b_kernel, in_specs=[vmem] * 5, out_specs=vmem, out_s...  6.33 us
    pallas_call x1, Pallas kernels, route_a(): pl.pallas_call(route_a_kernel, in_specs=[vmem], out_specs=[vmem] * 4, out...  4.62 us
  transfers between devices with their start and end apart: 12, of which 5 were waited for; matrix products, arithmetic and copies ran while one was open for 4% of the time, Pallas kernels for 27%

profile of v2, /device:TPU:1, one launch (start us, length us, event | category | flops | bytes accessed | tf_op | source)
XLA Modules:
  0.0 135.3 jit_solution(16355139437733326311)
XLA Ops:
  0.6 4.3 %pack_a.1 = (bf16[64,24,128]{2,1,0:T(8,128)(2,1)}, bf16[64,24,128]{2,1,0:T(8,128)(2,1)}, bf16[64,24,128]{2,1,0:T(8,128)(2,1)}, bf16[64,24,128]{2,1,0:T(8,128)(2,1)}) custom-call(bf16[192,4096]{1,0:T(8,128)(2,1)} %q_any.1, bf16[192,512]{1,0:T(8,128)(2,1)} %k_any.1, bf16[192,512]{1,0:T(8,128)(2,1)} %v_any.1, bf16[192,4096]{1,0:T(8,128)(2,1)} %g_any.1, ...), custom_call_target="tpu_custom_call" | custom-call | bytes 3000000 | tf_op jit(solution)/shard_map/pack_a/pallas_call | solution.py:107
  4.9 0.7 collective-permute-start
  5.6 1.3 collective-permute-start.1
  6.9 0.7 collective-permute-start.2
  7.6 3.5 %pack_b.1 = (bf16[64,32,128]{2,1,0:T(8,128)(2,1)}, bf16[64,32,128]{2,1,0:T(8,128)(2,1)}, bf16[64,32,128]{2,1,0:T(8,128)(2,1)}, bf16[64,32,128]{2,1,0:T(8,128)(2,1)}) custom-call(bf16[192,4096]{1,0:T(8,128)(2,1)} %q_any.1, bf16[192,4096]{1,0:T(8,128)(2,1)} %g_any.1), custom_call_target="tpu_custom_call" | custom-call | bytes 5000000 | tf_op jit(solution)/shard_map/pack_b/pallas_call | solution.py:132
  11.1 2.2 %slice_group.3 = bf16[192,2304]{1,0:T(8,128)(2,1)} custom-call(s32[1]{0:T(128)} %bitcast.1.me_ref, bf16[192,4096]{1,0:T(8,128)(2,1)} %q_any.1, bf16[192,512]{1,0:T(8,128)(2,1)} %k_any.1, bf16[192,512]{1,0:T(8,128)(2,1)} %v_any.1, bf16[192,4096]{1,0:T(8,128)(2,1)} %g_any.1), custom_call_target="tpu_custom_call" | custom-call | bytes 1800000 | tf_op jit(solution)/shard_map/slice_group/pallas_call | solution.py:154
  13.2 2.2 %slice_group.4 = bf16[192,2304]{1,0:T(8,128)(2,1)} custom-call(s32[1]{0:T(128)} %bitcast.2.me_ref, bf16[192,4096]{1,0:T(8,128)(2,1)} %q_any.1, bf16[192,512]{1,0:T(8,128)(2,1)} %k_any.1, bf16[192,512]{1,0:T(8,128)(2,1)} %v_any.1, bf16[192,4096]{1,0:T(8,128)(2,1)} %g_any.1), custom_call_target="tpu_custom_call" | custom-call | bytes 1800000 | tf_op jit(solution)/shard_map/slice_group/pallas_call | solution.py:154
  15.4 2.2 %slice_group.5 = bf16[192,2304]{1,0:T(8,128)(2,1)} custom-call(s32[1]{0:T(128)} %bitcast.3.me_ref, bf16[192,4096]{1,0:T(8,128)(2,1)} %q_any.1, bf16[192,512]{1,0:T(8,128)(2,1)} %k_any.1, bf16[192,512]{1,0:T(8,128)(2,1)} %v_any.1, bf16[192,4096]{1,0:T(8,128)(2,1)} %g_any.1), custom_call_target="tpu_custom_call" | custom-call | bytes 1800000 | tf_op jit(solution)/shard_map/slice_group/pallas_call | solution.py:154
  17.6 3.4 %collective-permute-done.1 = bf16[64,24,128]{2,1,0:T(8,128)(2,1)S(1)} collective-permute-done((bf16[64,24,128]{2,1,0:T(8,128)(2,1)}, bf16[64,24,128]{2,1,0:T(8,128)(2,1)S(1)}, u32[]{:S(2)}, u32[]{:S(2)}) %collective-permute-start.1) | collective-permute-done | bytes 393248 | tf_op jit(solution)/shard_map/ppermute | solution.py:535
  21.1 1.3 collective-permute-start.3
  22.3 1.5 %collective-permute-start.4 = (bf16[64,32,128]{2,1,0:T(8,128)(2,1)}, bf16[64,32,128]{2,1,0:T(8,128)(2,1)}, u32[]{:S(2)}, u32[]{:S(2)}) collective-permute-start(bf16[64,32,128]{2,1,0:T(8,128)(2,1)} %get-tuple-element.40), channel_id=1, source_target_pairs={{3,2},{7,6},{11,10},{15,14},{19,18},{23,22},{27,26},{31,30},{35,34... | collective-permute-start | bytes 1572872 | tf_op jit(solution)/shard_map/ppermute | solution.py:535
  23.8 1.5 %collective-permute-start.5 = (bf16[64,32,128]{2,1,0:T(8,128)(2,1)}, bf16[64,32,128]{2,1,0:T(8,128)(2,1)}, u32[]{:S(2)}, u32[]{:S(2)}) collective-permute-start(bf16[64,32,128]{2,1,0:T(8,128)(2,1)} %get-tuple-element.41), channel_id=1, source_target_pairs={{3,1},{7,5},{11,9},{15,13},{19,17},{23,21},{27,25},{31,29},{35,33}... | collective-permute-start | bytes 1572872 | tf_op jit(solution)/shard_map/ppermute | solution.py:535
  25.3 0.8 select_select_fusion.1
  26.1 13.4 %all-to-all-start = ((bf16[64,24,128]{2,1,0:T(8,128)(2,1)}), bf16[64,24,128]{2,1,0:T(8,128)(2,1)S(1)}, u32[]{:S(2)}, u32[]{:S(2)}) async-start(bf16[64,24,128]{2,1,0:T(8,128)(2,1)} %select_select_fusion.1), calls=%async_computation | async-start | bytes 786432 | tf_op jit(solution)/shard_map/all_to_all | solution.py:536
  39.9 2.1 %select_select_fusion = bf16[64,32,128]{2,1,0:T(8,128)(2,1)} fusion(bf16[64,32,128]{2,1,0:T(8,128)(2,1)S(1)} %copy-done.4, bf16[64,32,128]{2,1,0:T(8,128)(2,1)S(1)} %collective-permute-done.3, bf16[64,32,128]{2,1,0:T(8,128)(2,1)} %collective-permute-done.4, bf16[64,32,128]{2,1,0:T(8,128)(2,1)} %collective-permute-done.5, pred[]{:T(512)S(6)} %eq.18, ...), kind=kLoop, calls=%fused_computation | loop fusion | flops 786432 | bytes 2621443 | tf_op jit(solution)/shard_map/jit(_where)/select_n | solution.py:541
  42.0 12.1 %all-to-all-done.in_ref = bf16[64,24,128]{2,1,0:T(8,128)(2,1)S(1)} async-done(((bf16[64,24,128]{2,1,0:T(8,128)(2,1)}), bf16[64,24,128]{2,1,0:T(8,128)(2,1)S(1)}, u32[]{:S(2)}, u32[]{:S(2)}) %all-to-all-start) | async-done | bytes 393248 | tf_op jit(solution)/shard_map/all_to_all | solution.py:536
  54.1 6.2 %all-to-all-start.1 = ((bf16[64,32,128]{2,1,0:T(8,128)(2,1)}), bf16[64,32,128]{2,1,0:T(8,128)(2,1)S(1)}, u32[]{:S(2)}, u32[]{:S(2)}) async-start(bf16[64,32,128]{2,1,0:T(8,128)(2,1)} %select_select_fusion), calls=%async_computation.1 | async-start | bytes 1048576 | tf_op jit(solution)/shard_map/all_to_all | solution.py:536
  60.3 13.5 %collective-permute-start.6 = (bf16[192,2304]{1,0:T(8,128)(2,1)S(1)}, bf16[192,2304]{1,0:T(8,128)(2,1)}, u32[]{:S(2)}, u32[]{:S(2)}) collective-permute-start(bf16[192,2304]{1,0:T(8,128)(2,1)S(1)} %copy-done.1), channel_id=1, source_target_pairs={{0,1},{1,2},{2,3},{4,5},{5,6},{6,7},{8,9},{9,10},{10,11},{12,13},{... | collective-permute-start | bytes 2654216 | tf_op jit(solution)/shard_map/ppermute | solution.py:535
  73.9 1.9 %collective-permute-start.7 = (bf16[192,2304]{1,0:T(8,128)(2,1)S(1)}, bf16[192,2304]{1,0:T(8,128)(2,1)}, u32[]{:S(2)}, u32[]{:S(2)}) collective-permute-start(bf16[192,2304]{1,0:T(8,128)(2,1)S(1)} %copy-done.2), channel_id=1, source_target_pairs={{1,0},{2,1},{0,3},{5,4},{6,5},{4,7},{9,8},{10,9},{8,11},{13,12},{1... | collective-permute-start | bytes 2654216 | tf_op jit(solution)/shard_map/ppermute | solution.py:535
  75.8 3.7 %collective-permute-start.8 = (bf16[192,2304]{1,0:T(8,128)(2,1)}, bf16[192,2304]{1,0:T(8,128)(2,1)}, u32[]{:S(2)}, u32[]{:S(2)}) collective-permute-start(bf16[192,2304]{1,0:T(8,128)(2,1)} %slice_group.5), channel_id=1, source_target_pairs={{0,2},{2,0},{1,3},{4,6},{6,4},{5,7},{8,10},{10,8},{9,11},{12,14},{... | collective-permute-start | bytes 2654216 | tf_op jit(solution)/shard_map/ppermute | solution.py:535
  79.5 0.9 reshape.44.col_ref
  80.4 0.6 reshape.43.row_ref
  81.1 0.8 copy.15.col_ref
  81.9 4.6 %route_a.1 = (bf16[64,56,128]{2,1,0:T(8,128)(2,1)}, f32[8,2048]{1,0:T(8,128)}, bf16[64,2048]{1,0:T(8,128)(2,1)}, bf16[2048,128]{1,0:T(8,128)(2,1)}) custom-call(bf16[64,24,128]{2,1,0:T(8,128)(2,1)} %copy-done.5), custom_call_target="tpu_custom_call" | custom-call | flops 1610612736 | bytes 2000000 | tf_op jit(solution)/shard_map/route_a/pallas_call | solution.py:247
  86.6 0.8 copy-done.3
  87.3 6.3 %route_b.1 = bf16[64,56,128]{2,1,0:T(8,128)(2,1)} custom-call(bf16[64,32,128]{2,1,0:T(8,128)(2,1)} %copy-done.3, bf16[64,56,128]{2,1,0:T(8,128)(2,1)} %get-tuple-element.44.part_ref, f32[8,2048]{1,0:T(8,128)} %get-tuple-element.45.line_ref, bf16[64,2048]{1,0:T(8,128)(2,1)} %get-tuple-element.46.low_ref, bf16[2048,128]{1,0:T(8,128)(2,1)} %get-tuple-element.47.rest_ref), custom_call_target="tpu_custom_call" | custom-call | flops 3221225472 | bytes 3000000 | tf_op jit(solution)/shard_map/route_b/pallas_call | solution.py:283
  93.7 11.1 %all-to-all-start.2 = ((bf16[64,56,128]{2,1,0:T(8,128)(2,1)}), bf16[64,56,128]{2,1,0:T(8,128)(2,1)S(1)}, u32[]{:S(2)}, u32[]{:S(2)}) async-start(bf16[64,56,128]{2,1,0:T(8,128)(2,1)} %route_b.1), calls=%async_computation.2 | async-start | bytes 1835008 | tf_op jit(solution)/shard_map/all_to_all | solution.py:536
  104.8 7.1 %collective-permute-done.8.two = bf16[192,2304]{1,0:T(8,128)(2,1)} collective-permute-done((bf16[192,2304]{1,0:T(8,128)(2,1)}, bf16[192,2304]{1,0:T(8,128)(2,1)}, u32[]{:S(2)}, u32[]{:S(2)}) %collective-permute-start.8) | collective-permute-done | bytes 884768 | tf_op jit(solution)/shard_map/ppermute | solution.py:535
  111.9 15.8 %attend_stay.1 = (bf16[768,1024]{1,0:T(8,128)(2,1)}, bf16[768,1024]{1,0:T(8,128)(2,1)}, bf16[768,128]{1,0:T(8,128)(2,1)}, bf16[768,128]{1,0:T(8,128)(2,1)}) custom-call(s32[1]{0:T(128)} %bitcast.6.me_ref, bf16[192,4096]{1,0:T(8,128)(2,1)} %q_any.1, bf16[192,512]{1,0:T(8,128)(2,1)} %k_any.1, bf16[192,512]{1,0:T(8,128)(2,1)} %v_any.1, ...), custom_call_target="tpu_custom_call" | custom-call | flops 40768634880 | bytes 6000000 | tf_op jit(solution)/shard_map/attend_stay/pallas_call | solution.py:424
  127.7 2.6 %all-to-all-done.2.slots = bf16[64,56,128]{2,1,0:T(8,128)(2,1)S(1)} async-done(((bf16[64,56,128]{2,1,0:T(8,128)(2,1)}), bf16[64,56,128]{2,1,0:T(8,128)(2,1)S(1)}, u32[]{:S(2)}, u32[]{:S(2)}) %all-to-all-start.2) | async-done | bytes 917536 | tf_op jit(solution)/shard_map/all_to_all | solution.py:536
  130.3 0.9 copy-done
  131.3 4.0 %attend_tail.1 = (bf16[768,1024]{1,0:T(8,128)(2,1)}, bf16[768,1024]{1,0:T(8,128)(2,1)}, bf16[768,128]{1,0:T(8,128)(2,1)}, bf16[768,128]{1,0:T(8,128)(2,1)}) custom-call(bf16[64,56,128]{2,1,0:T(8,128)(2,1)} %copy-done, s32[256,1]{1,0:T(8,128)} %copy.15.col_ref, ...), custom_call_target="tpu_custom_call", output_to_operand_aliasing={{0}: (3, {}), {1}: (4, {}), {2}: (5, {}), {3}: (6, {})} | custom-call | flops 301989888 | bytes 2000000 | tf_op jit(solution)/shard_map/attend_tail/pallas_call | solution.py:499
  (26 shorter events, 0.5 us)
Async XLA Ops:
  4.9 12.7 %collective-permute-start = (bf16[64,24,128]{2,1,0:T(8,128)(2,1)}, bf16[64,24,128]{2,1,0:T(8,128)(2,1)S(1)}, u32[]{:S(2)}, u32[]{:S(2)}) collective-permute-start(bf16[64,24,128]{2,1,0:T(8,128)(2,1)} %get-tuple-element.35), channel_id=1, source_target_pairs={{3,1},{7,5},{11,9},{15,13},{19,17},{23,21},{27,25},{31,29},{35,33}... | collective-permute-start | bytes 1179656 | tf_op jit(solution)/shard_map/ppermute | solution.py:535
  5.6 15.5 %collective-permute-start.1 = (bf16[64,24,128]{2,1,0:T(8,128)(2,1)}, bf16[64,24,128]{2,1,0:T(8,128)(2,1)S(1)}, u32[]{:S(2)}, u32[]{:S(2)}) collective-permute-start(bf16[64,24,128]{2,1,0:T(8,128)(2,1)} %get-tuple-element.36), channel_id=1, source_target_pairs={{3,0},{7,4},{11,8},{15,12},{19,16},{23,20},{27,24},{31,28},{35,32}... | collective-permute-start | bytes 1179656 | tf_op jit(solution)/shard_map/ppermute | solution.py:535
  6.9 14.2 %collective-permute-start.2 = (bf16[64,24,128]{2,1,0:T(8,128)(2,1)}, bf16[64,24,128]{2,1,0:T(8,128)(2,1)S(1)}, u32[]{:S(2)}, u32[]{:S(2)}) collective-permute-start(bf16[64,24,128]{2,1,0:T(8,128)(2,1)} %get-tuple-element.37), channel_id=1, source_target_pairs={{3,2},{7,6},{11,10},{15,14},{19,18},{23,22},{27,26},{31,30},{35,34... | collective-permute-start | bytes 1179656 | tf_op jit(solution)/shard_map/ppermute | solution.py:535
  15.4 9.9 %copy-start.6 = (bf16[64,24,128]{2,1,0:T(8,128)(2,1)S(1)}, bf16[64,24,128]{2,1,0:T(8,128)(2,1)}, u32[]{:S(2)}) copy-start(bf16[64,24,128]{2,1,0:T(8,128)(2,1)} %get-tuple-element.42) | copy-start | bytes 1179652
  17.6 22.3 %copy-start.4 = (bf16[64,32,128]{2,1,0:T(8,128)(2,1)S(1)}, bf16[64,32,128]{2,1,0:T(8,128)(2,1)}, u32[]{:S(2)}) copy-start(bf16[64,32,128]{2,1,0:T(8,128)(2,1)} %get-tuple-element.38) | copy-start | bytes 1572868
  21.1 18.8 %collective-permute-start.3 = (bf16[64,32,128]{2,1,0:T(8,128)(2,1)}, bf16[64,32,128]{2,1,0:T(8,128)(2,1)S(1)}, u32[]{:S(2)}, u32[]{:S(2)}) collective-permute-start(bf16[64,32,128]{2,1,0:T(8,128)(2,1)} %get-tuple-element.39), channel_id=1, source_target_pairs={{3,0},{7,4},{11,8},{15,12},{19,16},{23,20},{27,24},{31,28},{35,32}... | collective-permute-start | bytes 1572872 | tf_op jit(solution)/shard_map/ppermute | solution.py:535
  22.3 17.6 %collective-permute-start.4 = (bf16[64,32,128]{2,1,0:T(8,128)(2,1)}, bf16[64,32,128]{2,1,0:T(8,128)(2,1)}, u32[]{:S(2)}, u32[]{:S(2)}) collective-permute-start(bf16[64,32,128]{2,1,0:T(8,128)(2,1)} %get-tuple-element.40), channel_id=1, source_target_pairs={{3,2},{7,6},{11,10},{15,14},{19,18},{23,22},{27,26},{31,30},{35,34... | collective-permute-start | bytes 1572872 | tf_op jit(solution)/shard_map/ppermute | solution.py:535
  23.8 16.1 %collective-permute-start.5 = (bf16[64,32,128]{2,1,0:T(8,128)(2,1)}, bf16[64,32,128]{2,1,0:T(8,128)(2,1)}, u32[]{:S(2)}, u32[]{:S(2)}) collective-permute-start(bf16[64,32,128]{2,1,0:T(8,128)(2,1)} %get-tuple-element.41), channel_id=1, source_target_pairs={{3,1},{7,5},{11,9},{15,13},{19,17},{23,21},{27,25},{31,29},{35,33}... | collective-permute-start | bytes 1572872 | tf_op jit(solution)/shard_map/ppermute | solution.py:535
  26.1 28.0 %all-to-all-start = ((bf16[64,24,128]{2,1,0:T(8,128)(2,1)}), bf16[64,24,128]{2,1,0:T(8,128)(2,1)S(1)}, u32[]{:S(2)}, u32[]{:S(2)}) async-start(bf16[64,24,128]{2,1,0:T(8,128)(2,1)} %select_select_fusion.1), calls=%async_computation | async-start | bytes 786432 | tf_op jit(solution)/shard_map/all_to_all | solution.py:536
  39.5 20.8 %copy-start.1 = (bf16[192,2304]{1,0:T(8,128)(2,1)S(1)}, bf16[192,2304]{1,0:T(8,128)(2,1)}, u32[]{:S(2)}) copy-start(bf16[192,2304]{1,0:T(8,128)(2,1)} %slice_group.3) | copy-start | bytes 2654212
  39.5 34.4 %copy-start.2 = (bf16[192,2304]{1,0:T(8,128)(2,1)S(1)}, bf16[192,2304]{1,0:T(8,128)(2,1)}, u32[]{:S(2)}) copy-start(bf16[192,2304]{1,0:T(8,128)(2,1)} %slice_group.4) | copy-start | bytes 2654212
  39.5 40.0 %copy-start.7 = (s32[768]{0:T(1024)S(1)}, s32[768]{0:T(1024)}, u32[]{:S(2)}) copy-start(s32[768]{0:T(1024)} %param.11) | copy-start | bytes 9220
  54.1 27.8 %copy-start.5 = (bf16[64,24,128]{2,1,0:T(8,128)(2,1)}, bf16[64,24,128]{2,1,0:T(8,128)(2,1)S(1)}, u32[]{:S(2)}) copy-start(bf16[64,24,128]{2,1,0:T(8,128)(2,1)S(1)} %all-to-all-done.in_ref) | copy-start | bytes 1179652
  54.1 32.4 %all-to-all-start.1 = ((bf16[64,32,128]{2,1,0:T(8,128)(2,1)}), bf16[64,32,128]{2,1,0:T(8,128)(2,1)S(1)}, u32[]{:S(2)}, u32[]{:S(2)}) async-start(bf16[64,32,128]{2,1,0:T(8,128)(2,1)} %select_select_fusion), calls=%async_computation.1 | async-start | bytes 1048576 | tf_op jit(solution)/shard_map/all_to_all | solution.py:536
  60.3 44.4 %collective-permute-start.6 = (bf16[192,2304]{1,0:T(8,128)(2,1)S(1)}, bf16[192,2304]{1,0:T(8,128)(2,1)}, u32[]{:S(2)}, u32[]{:S(2)}) collective-permute-start(bf16[192,2304]{1,0:T(8,128)(2,1)S(1)} %copy-done.1), channel_id=1, source_target_pairs={{0,1},{1,2},{2,3},{4,5},{5,6},{6,7},{8,9},{9,10},{10,11},{12,13},{... | collective-permute-start | bytes 2654216 | tf_op jit(solution)/shard_map/ppermute | solution.py:535
  73.9 30.9 %collective-permute-start.7 = (bf16[192,2304]{1,0:T(8,128)(2,1)S(1)}, bf16[192,2304]{1,0:T(8,128)(2,1)}, u32[]{:S(2)}, u32[]{:S(2)}) collective-permute-start(bf16[192,2304]{1,0:T(8,128)(2,1)S(1)} %copy-done.2), channel_id=1, source_target_pairs={{1,0},{2,1},{0,3},{5,4},{6,5},{4,7},{9,8},{10,9},{8,11},{13,12},{1... | collective-permute-start | bytes 2654216 | tf_op jit(solution)/shard_map/ppermute | solution.py:535
  75.8 36.1 %collective-permute-start.8 = (bf16[192,2304]{1,0:T(8,128)(2,1)}, bf16[192,2304]{1,0:T(8,128)(2,1)}, u32[]{:S(2)}, u32[]{:S(2)}) collective-permute-start(bf16[192,2304]{1,0:T(8,128)(2,1)} %slice_group.5), channel_id=1, source_target_pairs={{0,2},{2,0},{1,3},{4,6},{6,4},{5,7},{8,10},{10,8},{9,11},{12,14},{... | collective-permute-start | bytes 2654216 | tf_op jit(solution)/shard_map/ppermute | solution.py:535
  81.1 5.4 %copy-start.8 = (s32[256]{0:T(256)}, s32[256]{0:T(256)S(1)}, u32[]{:S(2)}) copy-start(s32[256]{0:T(256)S(1)} %pad.4) | copy-start | bytes 3076
  86.5 0.8 copy-start.3
  93.7 36.6 %all-to-all-start.2 = ((bf16[64,56,128]{2,1,0:T(8,128)(2,1)}), bf16[64,56,128]{2,1,0:T(8,128)(2,1)S(1)}, u32[]{:S(2)}, u32[]{:S(2)}) async-start(bf16[64,56,128]{2,1,0:T(8,128)(2,1)} %route_b.1), calls=%async_computation.2 | async-start | bytes 1835008 | tf_op jit(solution)/shard_map/all_to_all | solution.py:536
  130.3 0.9 copy-start

commit v3 on v2

--- a/solution.py
+++ b/solution.py
@@ -17,9 +17,6 @@
 NBLK = 48
 SEQ = 64
 WIDE = 2 * QW + 2 * DH
-FIRST = 16
-REST = NBLK - FIRST
-SLOT_A = FIRST + 8
 SLOT = NBLK + 8
 INV = 1.0 / math.sqrt(DH)
 LOG2E = math.log2(math.e)
@@ -55,91 +52,71 @@
     return x
 
 
-def split_rows(src, dst, first, count, qs):
-    for n in range(GROUP):
-        qs[n] = src[:, n * DH : (n + 1) * DH].astype(F32)
-        for t in range(BLK):
-            rows = qs[n, pl.ds(first * BLK + t, count, stride=BLK), :]
-            dst[t * GROUP + n, 0:count, :] = rows.astype(BF16)
-
-
-ORDER = (1, 0, 2, 3)
-
-
-def pack_a_kernel(q_ref, k_ref, v_ref, g_ref, plan_ref, o1, o0, o2, o3, qs, ks, small):
+def pack_group(group, q_ref, k_ref, v_ref, g_ref, out, qs, ks, small):
     half = SEQ // 2
+    thin = slice(group * DH, (group + 1) * DH)
+    ks[0] = k_ref[:, thin].astype(F32)
+    ks[1] = v_ref[:, thin].astype(F32)
+    pieces = []
+    for r in range(8):
+        rows = ks[r // 4, pl.ds(r % 4, NBLK, stride=BLK), :]
+        pieces.append(rows.reshape(6, 8, DH))
+    mixed = swap_groups(jnp.concatenate(pieces, axis=0))
+    for r in range(8):
+        for b in range(6):
+            small[pl.ds(r * 8, 8), b, :] = mixed[r * 6 + b]
+    for which, src in enumerate((q_ref, g_ref)):
+        dst = out[which]
+        for n in range(GROUP):
+            qs[n] = src[:, group * QW + n * DH : group * QW + (n + 1) * DH].astype(F32)
+            for t in range(BLK):
+                rows = qs[n, pl.ds(t, NBLK, stride=BLK), :]
+                dst[t * GROUP + n, 0:NBLK, :] = rows.astype(BF16)
+        dst[:, NBLK:SLOT, :] = small[pl.ds(which * half, half)].astype(BF16)
+
+
+def put_plan(plan_ref, small):
     plan = jnp.concatenate([plan_ref[...], jnp.zeros((1, DH - NBLK), jnp.int32)], axis=1)
     small[:, 6, :] = jnp.broadcast_to((plan // 64).astype(F32), (SEQ, DH))
     small[:, 7, :] = jnp.broadcast_to((plan % 64).astype(F32), (SEQ, DH))
-    for group, out in zip(ORDER, (o1, o0, o2, o3)):
-        thin = slice(group * DH, (group + 1) * DH)
-        wide = slice(group * QW, (group + 1) * QW)
-        ks[0] = k_ref[:, thin].astype(F32)
-        ks[1] = v_ref[:, thin].astype(F32)
-        pieces = []
-        for r in range(8):
-            rows = ks[r // 4, pl.ds(r % 4, NBLK, stride=BLK), :]
-            pieces.append(rows.reshape(6, 8, DH))
-        mixed = swap_groups(jnp.concatenate(pieces, axis=0))
-        for r in range(8):
-            for b in range(6):
-                small[pl.ds(r * 8, 8), b, :] = mixed[r * 6 + b]
-        for src, dst, start in ((q_ref, out.at[0:half], 0), (g_ref, out.at[half:SEQ], half)):
-            split_rows(src.at[:, wide], dst, 0, FIRST, qs)
-            dst[:, FIRST:SLOT_A, :] = small[pl.ds(start, half)].astype(BF16)
-
-
-def pack_b_kernel(q_ref, g_ref, o1, o0, o2, o3, qs):
+
+
+def pack_one_kernel(q_ref, k_ref, v_ref, g_ref, plan_ref, lo_ref, hi_ref, qs, ks, small):
+    put_plan(plan_ref, small)
+    pack_group(0, q_ref, k_ref, v_ref, g_ref, (lo_ref, hi_ref), qs, ks, small)
+
+
+def pack_rest_kernel(q_ref, k_ref, v_ref, g_ref, plan_ref, o0, o2, o3, qs, ks, small):
     half = SEQ // 2
-    for group, out in zip(ORDER, (o1, o0, o2, o3)):
-        wide = slice(group * QW, (group + 1) * QW)
-        split_rows(q_ref.at[:, wide], out.at[0:half], FIRST, REST, qs)
-        split_rows(g_ref.at[:, wide], out.at[half:SEQ], FIRST, REST, qs)
-
-
-def packed_shapes(rows):
-    return [jax.ShapeDtypeStruct((SEQ, rows, DH), BF16)] * 4
-
-
-def pack_a(queries, key_rows, value_rows, out_grad, plan_row):
-    shapes = packed_shapes(SLOT_A)
-    top = lambda i: (0, 0)
+    put_plan(plan_ref, small)
+    for group, out in ((0, o0), (2, o2), (3, o3)):
+        halves = (out.at[0:half], out.at[half:SEQ])
+        pack_group(group, q_ref, k_ref, v_ref, g_ref, halves, qs, ks, small)
+
+
+def pack(kernel, name, width, first, shapes, queries, key_rows, value_rows, out_grad, plan_row):
+    at = lambda i: (0, first)
     return pl.pallas_call(
-        pack_a_kernel,
+        kernel,
         grid=(1,),
         in_specs=[
-            pl.BlockSpec((FIRST * BLK, 4 * QW), top),
-            pl.BlockSpec((QUART, 4 * DH), top),
-            pl.BlockSpec((QUART, 4 * DH), top),
-            pl.BlockSpec((FIRST * BLK, 4 * QW), top),
-            pl.BlockSpec((1, NBLK), top),
+            pl.BlockSpec((QUART, width * QW), at),
+            pl.BlockSpec((QUART, width * DH), at),
+            pl.BlockSpec((QUART, width * DH), at),
+            pl.BlockSpec((QUART, width * QW), at),
+            pl.BlockSpec((1, NBLK), lambda i: (0, 0)),
         ],
-        out_specs=[pl.BlockSpec(x.shape, lambda i: (0, 0, 0)) for x in shapes],
-        out_shape=shapes,
+        out_specs=[pl.BlockSpec(x, lambda i: (0, 0, 0)) for x in shapes],
+        out_shape=[jax.ShapeDtypeStruct(x, BF16) for x in shapes],
         scratch_shapes=[
-            pltpu.VMEM((GROUP, FIRST * BLK, DH), F32),
+            pltpu.VMEM((GROUP, QUART, DH), F32),
             pltpu.VMEM((2, QUART, DH), F32),
             pltpu.VMEM((SEQ, 8, DH), F32),
         ],
         compiler_params=params(),
-        cost_estimate=cost(0, 3_000_000),
-        name="pack_a",
+        cost_estimate=cost(0, 2_000_000 * len(shapes)),
+        name=name,
     )(queries, key_rows, value_rows, out_grad, plan_row)
-
-
-def pack_b(queries, out_grad):
-    shapes = packed_shapes(REST)
-    return pl.pallas_call(
-        pack_b_kernel,
-        grid=(1,),
-        in_specs=[pl.BlockSpec((QUART, 4 * QW), lambda i: (0, 0))] * 2,
-        out_specs=[pl.BlockSpec(x.shape, lambda i: (0, 0, 0)) for x in shapes],
-        out_shape=shapes,
-        scratch_shapes=[pltpu.VMEM((GROUP, QUART, DH), F32)],
-        compiler_params=params(),
-        cost_estimate=cost(0, 5_000_000),
-        name="pack_b",
-    )(queries, out_grad)
 
 
 def slice_kernel(me_ref, q_ref, k_ref, v_ref, g_ref, o_ref):
@@ -171,11 +148,11 @@
     )(group.reshape(1), queries, key_rows, value_rows, out_grad)
 
 
-def plan_lines(tail, first, count):
-    total = SEQ * count
+def plan_lines(tail):
+    total = SEQ * NBLK
     col = iota((1, total), 1).astype(F32)
-    owner = jnp.floor((col + 0.5) * (1.0 / count))
-    place = col - owner * count + first
+    owner = jnp.floor((col + 0.5) * (1.0 / NBLK))
+    place = col - owner * NBLK
     pick = (iota((DH, total), 0).astype(F32) == place).astype(BF16)
     mine = iota((SEQ, total), 0).astype(F32) == owner
     lines = []
@@ -201,98 +178,47 @@
 SHARDS = TILE // NBLK
 
 
-def merge(got, here, shard, out_ref, part_ref=None):
-    out = got[:, 0:DH].astype(BF16)
-    kept = jnp.where(here, got[:, DH : 2 * DH], 0.0)
-    sums = [jnp.sum(kept[b * 8 : b * 8 + 8], axis=0, keepdims=True) for b in range(6)]
-    packed = jnp.concatenate(sums + [jnp.zeros((2, DH), F32)], axis=0).astype(BF16)
-    if part_ref is not None:
-        out += part_ref[shard, 0:NBLK, :]
-        packed += part_ref[shard, NBLK:SLOT, :]
-    out_ref[shard, 0:NBLK, :] = out
-    out_ref[shard, NBLK:SLOT, :] = packed
-
-
-def lane_is_row():
-    return iota((NBLK, DH), 1) // 16 == iota((NBLK, DH), 0) % 8
-
-
-def route_a_kernel(in_ref, out_ref, line_ref, low_ref, rest_ref, xs, ks, sel, low_a):
-    tail = in_ref[:, FIRST:SLOT_A, :].astype(F32)
-    high_a, digits_a = plan_lines(tail, 0, FIRST)
-    high_b, digits_b = plan_lines(tail, FIRST, REST)
-    line_ref[...] = jnp.broadcast_to(high_b, line_ref.shape)
-    low_ref[...] = low_choice(digits_b)
-    low_a[...] = low_choice(digits_a)
-
-    here = lane_is_row()
+def route_kernel(in_ref, out_ref, xs, ks, sel, low):
+    tail = in_ref[:, NBLK:SLOT, :].astype(F32)
+    high, digits = plan_lines(tail)
+    low[...] = low_choice(digits)
+    here = iota((NBLK, DH), 1) // 16 == iota((NBLK, DH), 0) % 8
     fold = (iota((DH, DH), 0) % 16 == iota((DH, DH), 1) % 16).astype(BF16)
+    xs[:, 0:DH] = in_ref[:, 0:NBLK, :].reshape(SEQ * NBLK, DH)
     for s in range(SEQ):
-        xs[s * FIRST : (s + 1) * FIRST, 0:DH] = in_ref[s, 0:FIRST, :]
         rows = [jnp.broadcast_to(tail[s, b : b + 1, :], (8, DH)) for b in range(6)]
         wide = jnp.where(here, jnp.concatenate(rows, axis=0), 0.0).astype(BF16)
-        ks[s * FIRST : (s + 1) * FIRST, :] = wide[0:FIRST]
-        rest_ref[s * REST : (s + 1) * REST, :] = wide[FIRST:NBLK]
+        ks[s * NBLK : (s + 1) * NBLK, :] = wide
     xs[:, DH : 2 * DH] = jnp.dot(ks[...], fold, preferred_element_type=F32).astype(BF16)
-    rest_ref[...] = jnp.dot(rest_ref[...], fold, preferred_element_type=F32).astype(BF16)
     for p in range(PARTS):
-        choose(sel.at[p % 2], low_a[...], high_a, p * RUNS, RUNS)
+        choose(sel.at[p % 2], low[...], high, p * RUNS, RUNS)
         got = jnp.dot(sel[p % 2], xs[...], preferred_element_type=F32)
         for d in range(SHARDS):
-            merge(got[d * NBLK : (d + 1) * NBLK], here, p * SHARDS + d, out_ref)
-
-
-def route_a(slots):
+            part = got[d * NBLK : (d + 1) * NBLK]
+            kept = jnp.where(here, part[:, DH : 2 * DH], 0.0)
+            sums = [jnp.sum(kept[b * 8 : b * 8 + 8], axis=0, keepdims=True) for b in range(6)]
+            sums.append(jnp.zeros((2, DH), F32))
+            out_ref[p * SHARDS + d, 0:NBLK, :] = part[:, 0:DH].astype(BF16)
+            out_ref[p * SHARDS + d, NBLK:SLOT, :] = jnp.concatenate(sums, axis=0).astype(BF16)
+
+
+def route(slots):
     vmem = pl.BlockSpec(memory_space=pltpu.VMEM)
     return pl.pallas_call(
-        route_a_kernel,
+        route_kernel,
         in_specs=[vmem],
-        out_specs=[vmem] * 4,
-        out_shape=[
-            jax.ShapeDtypeStruct((SEQ, SLOT, DH), BF16),
-            jax.ShapeDtypeStruct((8, SEQ * REST), F32),
-            jax.ShapeDtypeStruct((64, SEQ * REST), BF16),
-            jax.ShapeDtypeStruct((SEQ * REST, DH), BF16),
-        ],
-        scratch_shapes=[
-            pltpu.VMEM((SEQ * FIRST, 2 * DH), BF16),
-            pltpu.VMEM((SEQ * FIRST, DH), BF16),
-            pltpu.VMEM((2, TILE, SEQ * FIRST), BF16),
-            pltpu.VMEM((64, SEQ * FIRST), BF16),
-        ],
-        compiler_params=params(),
-        cost_estimate=cost(4 * SEQ * NBLK * SEQ * FIRST * DH, 2_000_000),
-        name="route_a",
-    )(slots)
-
-
-def route_b_kernel(in_ref, part_ref, line_ref, low_ref, rest_ref, out_ref, xs, sel):
-    xs[:, 0:DH] = in_ref[...].reshape(SEQ * REST, DH)
-    xs[:, DH : 2 * DH] = rest_ref[...]
-    here = lane_is_row()
-    line = line_ref[0:1, :]
-    for p in range(PARTS):
-        choose(sel.at[p % 2], low_ref[...], line, p * RUNS, RUNS)
-        got = jnp.dot(sel[p % 2], xs[...], preferred_element_type=F32)
-        for d in range(SHARDS):
-            merge(got[d * NBLK : (d + 1) * NBLK], here, p * SHARDS + d, out_ref, part_ref)
-
-
-def route_b(slots, part, line, low, rest):
-    vmem = pl.BlockSpec(memory_space=pltpu.VMEM)
-    return pl.pallas_call(
-        route_b_kernel,
-        in_specs=[vmem] * 5,
         out_specs=vmem,
         out_shape=jax.ShapeDtypeStruct((SEQ, SLOT, DH), BF16),
         scratch_shapes=[
-            pltpu.VMEM((SEQ * REST, 2 * DH), BF16),
-            pltpu.VMEM((2, TILE, SEQ * REST), BF16),
+            pltpu.VMEM((SEQ * NBLK, 2 * DH), BF16),
+            pltpu.VMEM((SEQ * NBLK, DH), BF16),
+            pltpu.VMEM((2, TILE, SEQ * NBLK), BF16),
+            pltpu.VMEM((64, SEQ * NBLK), BF16),
         ],
         compiler_params=params(),
-        cost_estimate=cost(4 * SEQ * NBLK * SEQ * REST * DH, 3_000_000),
-        name="route_b",
-    )(slots, part, line, low, rest)
+        cost_estimate=cost(4 * SEQ * NBLK * SEQ * NBLK * DH, 2_000_000),
+        name="route",
+    )(slots)
 
 
 def dot(a, b, dims):
@@ -535,27 +461,27 @@
     send = lambda x, *pairs: lax.ppermute(x, "head", list(pairs))
     exchange = lambda x: lax.all_to_all(x, "seq", split_axis=0, concat_axis=0, tiled=True)
 
-    def scatter(one, zero, two, three):
-        parts = (send(one, (3, 1)), send(zero, (3, 0)), send(two, (3, 2)))
-        other = jnp.where(me == 0, parts[1], jnp.where(me == 2, parts[2], parts[0]))
-        return jnp.where(me == 3, three, other), parts
-
-    slots_a, sent_a = scatter(*pack_a(*held, mover_dest.reshape(1, NBLK)))
+    plan_row = mover_dest.reshape(1, NBLK)
+    half = (SEQ // 2, SLOT, DH)
+    one_lo, one_hi = pack(pack_one_kernel, "pack_one", 1, 1, [half] * 2, *held, plan_row)
+    at_zero = send(one_lo, (3, 0))
+    at_two = send(one_hi, (3, 2))
+    rest = pack(pack_rest_kernel, "pack_rest", 4, 0, [(SEQ, SLOT, DH)] * 3, *held, plan_row)
+    to_zero, to_two = send(rest[0], (3, 0)), send(rest[1], (3, 2))
+    lo, hi = send(at_zero, (0, 1)), send(at_two, (2, 1))
+    other = jnp.where(me == 3, rest[2], jnp.where(me == 0, to_zero, to_two))
+    slots = jnp.where(me == 1, jnp.concatenate([lo, hi], axis=0), other)
     part = lambda shift: slice_group(*held, (me + shift) % 4)
-    slices = (part(1), part(3), part(2))
-    slots_b, _ = scatter(*after(pack_b(queries, out_grad), *sent_a, *slices))
-
-    pieces_a = exchange(slots_a)
-    (next_b,) = after([slots_b], pieces_a)
-    pieces_b = exchange(next_b)
-    routed_a = route_a(pieces_a)
-
-    ahead, behind, across = after(slices, slots_b)
+    (slots, *slices) = after((slots, part(1), part(3), part(2)))
+
+    pieces = exchange(slots)
+
+    ahead, behind, across = after(slices, slots)
     two = send(across, (0, 2), (2, 0), (1, 3))
     plus = send(ahead, (0, 1), (1, 2), (2, 3))
     minus = send(behind, (1, 0), (2, 1), (0, 3))
 
-    routed = route_b(pieces_b, *routed_a)
+    routed = route(pieces)
     stay = after((plus, minus, two), routed)
     seg_col = segment_ids.reshape(ROWS, 1)
     seg_row = segment_ids.reshape(1, ROWS)

time: 137 us -> 125 us (0.912)
  starting transfers between devices: 56.7 us -> 39.2 us
  waiting for transfers between devices: 25.7 us -> 36.9 us
  Pallas kernels: 45 us -> 42.1 us
  other arithmetic: 2.92 us -> 1.09 us
    all_to_all x3 -> x2, starting transfers between devices: 30.7 us -> 21.9 us  [on_device(): lax.all_to_all(x, 'seq', split_axis=0, concat_axis=0, tiled=True)]
    ppermute x9, starting transfers between devices: 26 us -> 17.3 us  [on_device(): send = lambda x, *pairs: lax.ppermute(x, 'head', list(pairs))]
    ppermute x9, waiting for transfers between devices: 10.9 us -> 16.6 us  [on_device(): send = lambda x, *pairs: lax.ppermute(x, 'head', list(pairs))]
    all_to_all x3 -> x2, waiting for transfers between devices: 14.8 us -> 20.4 us  [on_device(): lax.all_to_all(x, 'seq', split_axis=0, concat_axis=0, tiled=True)]
    pallas_call x4 -> x3, Pallas kernels: 18.7 us -> 15.8 us  [the longest x1 7.91 us: route(): pl.pallas_call(route_kernel, in_specs=[vmem], out_specs=vmem, out_shape=j...]
    select_n x2 -> x1, other arithmetic: 2.92 us -> 1.09 us  [on_device(): slots = jnp.where(me == 1, jnp.concatenate([lo, hi], axis=0), other)]
  transfers between devices with their start and end apart: 12 -> 11, of which waited for: 5 -> 5; matrix products, arithmetic and copies ran while one was open for 4% -> 2% of each run, Pallas kernels for 27% -> 28%
where the time goes in v3:
time: 125 us; the launch traced here: 124 us
  Pallas kernels  42.1 us (34%)
  starting transfers between devices  39.2 us (31%)
  waiting for transfers between devices  36.9 us (30%)
  local copies, waits for them, and re-layouts  4.31 us (3%)
    all_to_all x2, starting transfers between devices, on_device(): lax.all_to_all(x, 'seq', split_axis=0, concat_axis=0, tiled=True)  21.9 us
    all_to_all x2, waiting for transfers between devices, on_device(): lax.all_to_all(x, 'seq', split_axis=0, concat_axis=0, tiled=True)  20.4 us
    ppermute x9, starting transfers between devices, on_device(): send = lambda x, *pairs: lax.ppermute(x, 'head', list(pairs))  17.3 us
    ppermute x9, waiting for transfers between devices, on_device(): send = lambda x, *pairs: lax.ppermute(x, 'head', list(pairs))  16.6 us
    pallas_call x1, Pallas kernels, attend_stay(): pl.pallas_call(stay_kernel, grid_spec=pltpu.PrefetchScalarGridSpec(num_sc...  15.7 us
    pallas_call x1, Pallas kernels, route(): pl.pallas_call(route_kernel, in_specs=[vmem], out_specs=vmem, out_shape=j...  7.91 us
    pallas_call x2, Pallas kernels, pack(): pl.pallas_call(kernel, grid=(1,), in_specs=[pl.BlockSpec((QUART, width *...  7.9 us
    pallas_call x3, Pallas kernels, slice_group(): pl.pallas_call(slice_kernel, grid_spec=pltpu.PrefetchScalarGridSpec(num_s...  6.58 us
  transfers between devices with their start and end apart: 11, of which 5 were waited for; matrix products, arithmetic and copies ran while one was open for 2% of the time, Pallas kernels for 28%

profile of v3, /device:TPU:1, one launch (start us, length us, event | category | flops | bytes accessed | tf_op | source)
XLA Modules:
  0.0 124.5 jit_solution(6281827687198465779)
XLA Ops:
  0.6 2.7 %pack_one.1 = (bf16[32,56,128]{2,1,0:T(8,128)(2,1)}, bf16[32,56,128]{2,1,0:T(8,128)(2,1)}) custom-call(bf16[192,4096]{1,0:T(8,128)(2,1)} %q_any.1, bf16[192,512]{1,0:T(8,128)(2,1)} %k_any.1, bf16[192,512]{1,0:T(8,128)(2,1)} %v_any.1, bf16[192,4096]{1,0:T(8,128)(2,1)} %g_any.1, s32[1,48]{1,0:T(1,128)} %bitcast.9), custom_call_target="tpu_custom_call" | custom-call | bytes 4000000 | tf_op jit(solution)/shard_map/pack_one/pallas_call | solution.py:99
  3.3 1.3 %collective-permute-start = (bf16[32,56,128]{2,1,0:T(8,128)(2,1)}, bf16[32,56,128]{2,1,0:T(8,128)(2,1)S(1)}, u32[]{:S(2)}, u32[]{:S(2)}) collective-permute-start(bf16[32,56,128]{2,1,0:T(8,128)(2,1)} %get-tuple-element.23), channel_id=1, source_target_pairs={{3,0},{7,4},{11,8},{15,12},{19,16},{23,20},{27,24},{31,28},{35,32}... | collective-permute-start | bytes 1376264 | tf_op jit(solution)/shard_map/ppermute | solution.py:461
  4.6 1.4 %collective-permute-start.2 = (bf16[32,56,128]{2,1,0:T(8,128)(2,1)}, bf16[32,56,128]{2,1,0:T(8,128)(2,1)}, u32[]{:S(2)}, u32[]{:S(2)}) collective-permute-start(bf16[32,56,128]{2,1,0:T(8,128)(2,1)} %get-tuple-element.24), channel_id=1, source_target_pairs={{3,2},{7,6},{11,10},{15,14},{19,18},{23,22},{27,26},{31,30},{35,34... | collective-permute-start | bytes 1376264 | tf_op jit(solution)/shard_map/ppermute | solution.py:461
  6.1 5.2 %pack_rest.1 = (bf16[64,56,128]{2,1,0:T(8,128)(2,1)}, bf16[64,56,128]{2,1,0:T(8,128)(2,1)}, bf16[64,56,128]{2,1,0:T(8,128)(2,1)}) custom-call(bf16[192,4096]{1,0:T(8,128)(2,1)} %q_any.1, bf16[192,512]{1,0:T(8,128)(2,1)} %k_any.1, bf16[192,512]{1,0:T(8,128)(2,1)} %v_any.1, bf16[192,4096]{1,0:T(8,128)(2,1)} %g_any.1, s32[1,48]{1,0:T(1,128)} %bitcast.10), custom_call_target="tpu_custom_call" | custom-call | bytes 6000000 | tf_op jit(solution)/shard_map/pack_rest/pallas_call | solution.py:99
  11.3 1.3 %collective-permute-start.4 = (bf16[64,56,128]{2,1,0:T(8,128)(2,1)}, bf16[64,56,128]{2,1,0:T(8,128)(2,1)S(1)}, u32[]{:S(2)}, u32[]{:S(2)}) collective-permute-start(bf16[64,56,128]{2,1,0:T(8,128)(2,1)} %get-tuple-element.26), channel_id=1, source_target_pairs={{3,0},{7,4},{11,8},{15,12},{19,16},{23,20},{27,24},{31,28},{35,32}... | collective-permute-start | bytes 2752520 | tf_op jit(solution)/shard_map/ppermute | solution.py:461
  12.6 0.7 collective-permute-start.5
  13.3 2.2 %collective-permute-done = bf16[32,56,128]{2,1,0:T(8,128)(2,1)S(1)} collective-permute-done((bf16[32,56,128]{2,1,0:T(8,128)(2,1)}, bf16[32,56,128]{2,1,0:T(8,128)(2,1)S(1)}, u32[]{:S(2)}, u32[]{:S(2)}) %collective-permute-start) | collective-permute-done | bytes 458784 | tf_op jit(solution)/shard_map/ppermute | solution.py:461
  15.4 1.3 %collective-permute-start.1 = (bf16[32,56,128]{2,1,0:T(8,128)(2,1)S(1)}, bf16[32,56,128]{2,1,0:T(8,128)(2,1)S(1)}, u32[]{:S(2)}, u32[]{:S(2)}) collective-permute-start(bf16[32,56,128]{2,1,0:T(8,128)(2,1)S(1)} %collective-permute-done), channel_id=1, source_target_pairs={{0,1},{4,5},{8,9},{12,13},{16,17},{20,21},{24,25},{28,29},{32,33},... | collective-permute-start | bytes 1376264 | tf_op jit(solution)/shard_map/ppermute | solution.py:461
  16.8 0.0 collective-permute-done.2
  16.8 0.7 collective-permute-start.3
  17.5 2.2 %slice_group.4 = bf16[192,2304]{1,0:T(8,128)(2,1)} custom-call(s32[1]{0:T(128)} %bitcast.2.me_ref, bf16[192,4096]{1,0:T(8,128)(2,1)} %q_any.1, bf16[192,512]{1,0:T(8,128)(2,1)} %k_any.1, bf16[192,512]{1,0:T(8,128)(2,1)} %v_any.1, bf16[192,4096]{1,0:T(8,128)(2,1)} %g_any.1), custom_call_target="tpu_custom_call" | custom-call | bytes 1800000 | tf_op jit(solution)/shard_map/slice_group/pallas_call | solution.py:131
  19.7 2.2 %slice_group.3 = bf16[192,2304]{1,0:T(8,128)(2,1)} custom-call(s32[1]{0:T(128)} %bitcast.1.me_ref, bf16[192,4096]{1,0:T(8,128)(2,1)} %q_any.1, bf16[192,512]{1,0:T(8,128)(2,1)} %k_any.1, bf16[192,512]{1,0:T(8,128)(2,1)} %v_any.1, bf16[192,4096]{1,0:T(8,128)(2,1)} %g_any.1), custom_call_target="tpu_custom_call" | custom-call | bytes 1800000 | tf_op jit(solution)/shard_map/slice_group/pallas_call | solution.py:131
  21.8 2.3 %slice_group.5 = bf16[192,2304]{1,0:T(8,128)(2,1)} custom-call(s32[1]{0:T(128)} %bitcast.3.me_ref, bf16[192,4096]{1,0:T(8,128)(2,1)} %q_any.1, bf16[192,512]{1,0:T(8,128)(2,1)} %k_any.1, bf16[192,512]{1,0:T(8,128)(2,1)} %v_any.1, bf16[192,4096]{1,0:T(8,128)(2,1)} %g_any.1), custom_call_target="tpu_custom_call" | custom-call | bytes 1800000 | tf_op jit(solution)/shard_map/slice_group/pallas_call | solution.py:131
  24.1 12.3 %collective-permute-done.4 = bf16[64,56,128]{2,1,0:T(8,128)(2,1)S(1)} collective-permute-done((bf16[64,56,128]{2,1,0:T(8,128)(2,1)}, bf16[64,56,128]{2,1,0:T(8,128)(2,1)S(1)}, u32[]{:S(2)}, u32[]{:S(2)}) %collective-permute-start.4) | collective-permute-done | bytes 917536 | tf_op jit(solution)/shard_map/ppermute | solution.py:461
  36.4 1.1 maximum_select_fusion
  37.5 15.5 %all-to-all-start = ((bf16[64,56,128]{2,1,0:T(8,128)(2,1)}), bf16[64,56,128]{2,1,0:T(8,128)(2,1)S(1)}, u32[]{:S(2)}, u32[]{:S(2)}) async-start(bf16[64,56,128]{2,1,0:T(8,128)(2,1)} %maximum_select_fusion), calls=%async_computation | async-start | bytes 1835008 | tf_op jit(solution)/shard_map/all_to_all | solution.py:462
  53.0 2.2 %collective-permute-start.6 = (bf16[192,2304]{1,0:T(8,128)(2,1)S(1)}, bf16[192,2304]{1,0:T(8,128)(2,1)}, u32[]{:S(2)}, u32[]{:S(2)}) collective-permute-start(bf16[192,2304]{1,0:T(8,128)(2,1)S(1)} %copy-done.4), channel_id=1, source_target_pairs={{0,1},{1,2},{2,3},{4,5},{5,6},{6,7},{8,9},{9,10},{10,11},{12,13},{... | collective-permute-start | bytes 2654216 | tf_op jit(solution)/shard_map/ppermute | solution.py:461
  55.2 1.9 %collective-permute-start.7 = (bf16[192,2304]{1,0:T(8,128)(2,1)S(1)}, bf16[192,2304]{1,0:T(8,128)(2,1)}, u32[]{:S(2)}, u32[]{:S(2)}) collective-permute-start(bf16[192,2304]{1,0:T(8,128)(2,1)S(1)} %copy-done.3), channel_id=1, source_target_pairs={{1,0},{2,1},{0,3},{5,4},{6,5},{4,7},{9,8},{10,9},{8,11},{13,12},{1... | collective-permute-start | bytes 2654216 | tf_op jit(solution)/shard_map/ppermute | solution.py:461
  57.1 6.5 %collective-permute-start.8 = (bf16[192,2304]{1,0:T(8,128)(2,1)}, bf16[192,2304]{1,0:T(8,128)(2,1)}, u32[]{:S(2)}, u32[]{:S(2)}) collective-permute-start(bf16[192,2304]{1,0:T(8,128)(2,1)} %slice_group.5), channel_id=1, source_target_pairs={{0,2},{2,0},{1,3},{4,6},{6,4},{5,7},{8,10},{10,8},{9,11},{12,14},{... | collective-permute-start | bytes 2654216 | tf_op jit(solution)/shard_map/ppermute | solution.py:461
  63.6 0.1 slice.3
  63.7 0.6 reshape.43.row_ref
  64.3 0.9 reshape.44.col_ref
  65.2 0.8 copy.15.col_ref
  66.1 12.7 %all-to-all-done.in_ref = bf16[64,56,128]{2,1,0:T(8,128)(2,1)S(1)} async-done(((bf16[64,56,128]{2,1,0:T(8,128)(2,1)}), bf16[64,56,128]{2,1,0:T(8,128)(2,1)S(1)}, u32[]{:S(2)}, u32[]{:S(2)}) %all-to-all-start) | async-done | bytes 917536 | tf_op jit(solution)/shard_map/all_to_all | solution.py:462
  78.7 0.9 copy-done.1
  79.6 7.9 %route.1 = bf16[64,56,128]{2,1,0:T(8,128)(2,1)} custom-call(bf16[64,56,128]{2,1,0:T(8,128)(2,1)} %copy-done.1), custom_call_target="tpu_custom_call" | custom-call | flops 4831838208 | bytes 2000000 | tf_op jit(solution)/shard_map/route/pallas_call | solution.py:207
  87.5 6.4 %all-to-all-start.1 = ((bf16[64,56,128]{2,1,0:T(8,128)(2,1)}), bf16[64,56,128]{2,1,0:T(8,128)(2,1)S(1)}, u32[]{:S(2)}, u32[]{:S(2)}) async-start(bf16[64,56,128]{2,1,0:T(8,128)(2,1)} %route.1), calls=%async_computation.1 | async-start | bytes 1835008 | tf_op jit(solution)/shard_map/all_to_all | solution.py:462
  94.0 2.1 %collective-permute-done.8.two = bf16[192,2304]{1,0:T(8,128)(2,1)} collective-permute-done((bf16[192,2304]{1,0:T(8,128)(2,1)}, bf16[192,2304]{1,0:T(8,128)(2,1)}, u32[]{:S(2)}, u32[]{:S(2)}) %collective-permute-start.8) | collective-permute-done | bytes 884768 | tf_op jit(solution)/shard_map/ppermute | solution.py:461
  96.1 15.7 %attend_stay.1 = (bf16[768,1024]{1,0:T(8,128)(2,1)}, bf16[768,1024]{1,0:T(8,128)(2,1)}, bf16[768,128]{1,0:T(8,128)(2,1)}, bf16[768,128]{1,0:T(8,128)(2,1)}) custom-call(s32[1]{0:T(128)} %bitcast.6.me_ref, bf16[192,4096]{1,0:T(8,128)(2,1)} %q_any.1, bf16[192,512]{1,0:T(8,128)(2,1)} %k_any.1, bf16[192,512]{1,0:T(8,128)(2,1)} %v_any.1, ...), custom_call_target="tpu_custom_call" | custom-call | flops 40768634880 | bytes 6000000 | tf_op jit(solution)/shard_map/attend_stay/pallas_call | solution.py:350
  111.8 7.7 %all-to-all-done.1.slots = bf16[64,56,128]{2,1,0:T(8,128)(2,1)S(1)} async-done(((bf16[64,56,128]{2,1,0:T(8,128)(2,1)}), bf16[64,56,128]{2,1,0:T(8,128)(2,1)S(1)}, u32[]{:S(2)}, u32[]{:S(2)}) %all-to-all-start.1) | async-done | bytes 917536 | tf_op jit(solution)/shard_map/all_to_all | solution.py:462
  119.5 0.9 copy-done
  120.4 4.0 %attend_tail.1 = (bf16[768,1024]{1,0:T(8,128)(2,1)}, bf16[768,1024]{1,0:T(8,128)(2,1)}, bf16[768,128]{1,0:T(8,128)(2,1)}, bf16[768,128]{1,0:T(8,128)(2,1)}) custom-call(bf16[64,56,128]{2,1,0:T(8,128)(2,1)} %copy-done, s32[256,1]{1,0:T(8,128)} %copy.15.col_ref, ...), custom_call_target="tpu_custom_call", output_to_operand_aliasing={{0}: (3, {}), {1}: (4, {}), {2}: (5, {}), {3}: (6, {})} | custom-call | flops 301989888 | bytes 2000000 | tf_op jit(solution)/shard_map/attend_tail/pallas_call | solution.py:425
  (18 shorter events, 0.0 us)
Async XLA Ops:
  3.3 12.1 %collective-permute-start = (bf16[32,56,128]{2,1,0:T(8,128)(2,1)}, bf16[32,56,128]{2,1,0:T(8,128)(2,1)S(1)}, u32[]{:S(2)}, u32[]{:S(2)}) collective-permute-start(bf16[32,56,128]{2,1,0:T(8,128)(2,1)} %get-tuple-element.23), channel_id=1, source_target_pairs={{3,0},{7,4},{11,8},{15,12},{19,16},{23,20},{27,24},{31,28},{35,32}... | collective-permute-start | bytes 1376264 | tf_op jit(solution)/shard_map/ppermute | solution.py:461
  4.6 12.1 %collective-permute-start.2 = (bf16[32,56,128]{2,1,0:T(8,128)(2,1)}, bf16[32,56,128]{2,1,0:T(8,128)(2,1)}, u32[]{:S(2)}, u32[]{:S(2)}) collective-permute-start(bf16[32,56,128]{2,1,0:T(8,128)(2,1)} %get-tuple-element.24), channel_id=1, source_target_pairs={{3,2},{7,6},{11,10},{15,14},{19,18},{23,22},{27,26},{31,30},{35,34... | collective-permute-start | bytes 1376264 | tf_op jit(solution)/shard_map/ppermute | solution.py:461
  11.3 25.1 %collective-permute-start.4 = (bf16[64,56,128]{2,1,0:T(8,128)(2,1)}, bf16[64,56,128]{2,1,0:T(8,128)(2,1)S(1)}, u32[]{:S(2)}, u32[]{:S(2)}) collective-permute-start(bf16[64,56,128]{2,1,0:T(8,128)(2,1)} %get-tuple-element.26), channel_id=1, source_target_pairs={{3,0},{7,4},{11,8},{15,12},{19,16},{23,20},{27,24},{31,28},{35,32}... | collective-permute-start | bytes 2752520 | tf_op jit(solution)/shard_map/ppermute | solution.py:461
  12.6 23.8 %collective-permute-start.5 = (bf16[64,56,128]{2,1,0:T(8,128)(2,1)}, bf16[64,56,128]{2,1,0:T(8,128)(2,1)S(1)}, u32[]{:S(2)}, u32[]{:S(2)}) collective-permute-start(bf16[64,56,128]{2,1,0:T(8,128)(2,1)} %get-tuple-element.27), channel_id=1, source_target_pairs={{3,2},{7,6},{11,10},{15,14},{19,18},{23,22},{27,26},{31,30},{35,34... | collective-permute-start | bytes 2752520 | tf_op jit(solution)/shard_map/ppermute | solution.py:461
  15.4 8.6 %collective-permute-start.1 = (bf16[32,56,128]{2,1,0:T(8,128)(2,1)S(1)}, bf16[32,56,128]{2,1,0:T(8,128)(2,1)S(1)}, u32[]{:S(2)}, u32[]{:S(2)}) collective-permute-start(bf16[32,56,128]{2,1,0:T(8,128)(2,1)S(1)} %collective-permute-done), channel_id=1, source_target_pairs={{0,1},{4,5},{8,9},{12,13},{16,17},{20,21},{24,25},{28,29},{32,33},... | collective-permute-start | bytes 1376264 | tf_op jit(solution)/shard_map/ppermute | solution.py:461
  16.8 7.3 %collective-permute-start.3 = (bf16[32,56,128]{2,1,0:T(8,128)(2,1)}, bf16[32,56,128]{2,1,0:T(8,128)(2,1)S(1)}, u32[]{:S(2)}, u32[]{:S(2)}) collective-permute-start(bf16[32,56,128]{2,1,0:T(8,128)(2,1)} %collective-permute-done.2), channel_id=1, source_target_pairs={{2,1},{6,5},{10,9},{14,13},{18,17},{22,21},{26,25},{30,29},{34,33}... | collective-permute-start | bytes 1376264 | tf_op jit(solution)/shard_map/ppermute | solution.py:461
  21.8 14.5 %copy-start.2 = (bf16[64,56,128]{2,1,0:T(8,128)(2,1)S(1)}, bf16[64,56,128]{2,1,0:T(8,128)(2,1)}, u32[]{:S(2)}) copy-start(bf16[64,56,128]{2,1,0:T(8,128)(2,1)} %get-tuple-element.25) | copy-start | bytes 2752516
  37.5 15.5 %copy-start.4 = (bf16[192,2304]{1,0:T(8,128)(2,1)S(1)}, bf16[192,2304]{1,0:T(8,128)(2,1)}, u32[]{:S(2)}) copy-start(bf16[192,2304]{1,0:T(8,128)(2,1)} %slice_group.3) | copy-start | bytes 2654212
  37.5 17.7 %copy-start.3 = (bf16[192,2304]{1,0:T(8,128)(2,1)S(1)}, bf16[192,2304]{1,0:T(8,128)(2,1)}, u32[]{:S(2)}) copy-start(bf16[192,2304]{1,0:T(8,128)(2,1)} %slice_group.4) | copy-start | bytes 2654212
  37.5 26.2 %copy-start.5 = (s32[768]{0:T(1024)S(1)}, s32[768]{0:T(1024)}, u32[]{:S(2)}) copy-start(s32[768]{0:T(1024)} %param.11) | copy-start | bytes 9220
  37.5 41.2 %all-to-all-start = ((bf16[64,56,128]{2,1,0:T(8,128)(2,1)}), bf16[64,56,128]{2,1,0:T(8,128)(2,1)S(1)}, u32[]{:S(2)}, u32[]{:S(2)}) async-start(bf16[64,56,128]{2,1,0:T(8,128)(2,1)} %maximum_select_fusion), calls=%async_computation | async-start | bytes 1835008 | tf_op jit(solution)/shard_map/all_to_all | solution.py:462
  53.0 41.0 %collective-permute-start.6 = (bf16[192,2304]{1,0:T(8,128)(2,1)S(1)}, bf16[192,2304]{1,0:T(8,128)(2,1)}, u32[]{:S(2)}, u32[]{:S(2)}) collective-permute-start(bf16[192,2304]{1,0:T(8,128)(2,1)S(1)} %copy-done.4), channel_id=1, source_target_pairs={{0,1},{1,2},{2,3},{4,5},{5,6},{6,7},{8,9},{9,10},{10,11},{12,13},{... | collective-permute-start | bytes 2654216 | tf_op jit(solution)/shard_map/ppermute | solution.py:461
  55.2 38.8 %collective-permute-start.7 = (bf16[192,2304]{1,0:T(8,128)(2,1)S(1)}, bf16[192,2304]{1,0:T(8,128)(2,1)}, u32[]{:S(2)}, u32[]{:S(2)}) collective-permute-start(bf16[192,2304]{1,0:T(8,128)(2,1)S(1)} %copy-done.3), channel_id=1, source_target_pairs={{1,0},{2,1},{0,3},{5,4},{6,5},{4,7},{9,8},{10,9},{8,11},{13,12},{1... | collective-permute-start | bytes 2654216 | tf_op jit(solution)/shard_map/ppermute | solution.py:461
  57.1 39.0 %collective-permute-start.8 = (bf16[192,2304]{1,0:T(8,128)(2,1)}, bf16[192,2304]{1,0:T(8,128)(2,1)}, u32[]{:S(2)}, u32[]{:S(2)}) collective-permute-start(bf16[192,2304]{1,0:T(8,128)(2,1)} %slice_group.5), channel_id=1, source_target_pairs={{0,2},{2,0},{1,3},{4,6},{6,4},{5,7},{8,10},{10,8},{9,11},{12,14},{... | collective-permute-start | bytes 2654216 | tf_op jit(solution)/shard_map/ppermute | solution.py:461
  65.2 22.3 %copy-start.6 = (s32[256]{0:T(256)}, s32[256]{0:T(256)S(1)}, u32[]{:S(2)}) copy-start(s32[256]{0:T(256)S(1)} %pad.4) | copy-start | bytes 3076
  78.7 0.9 copy-start.1
  87.5 32.0 %all-to-all-start.1 = ((bf16[64,56,128]{2,1,0:T(8,128)(2,1)}), bf16[64,56,128]{2,1,0:T(8,128)(2,1)S(1)}, u32[]{:S(2)}, u32[]{:S(2)}) async-start(bf16[64,56,128]{2,1,0:T(8,128)(2,1)} %route.1), calls=%async_computation.1 | async-start | bytes 1835008 | tf_op jit(solution)/shard_map/all_to_all | solution.py:462
  119.5 0.9 copy-start

commit v4 on v3

--- a/solution.py
+++ b/solution.py
@@ -24,10 +24,11 @@
 F32 = jnp.float32
 BF16 = jnp.bfloat16
 VMEM_LIMIT = 56 * 1024 * 1024
-
-
-def params():
-    return pltpu.CompilerParams(vmem_limit_bytes=VMEM_LIMIT)
+SMALL_LIMIT = 24 * 1024 * 1024
+
+
+def params(limit=VMEM_LIMIT):
+    return pltpu.CompilerParams(vmem_limit_bytes=limit)
 
 
 def cost(flops, bytes_accessed, transcendentals=0):
@@ -208,14 +209,14 @@
         route_kernel,
         in_specs=[vmem],
         out_specs=vmem,
-        out_shape=jax.ShapeDtypeStruct((SEQ, SLOT, DH), BF16),
+        out_shape=pltpu.HBM((SEQ, SLOT, DH), BF16),
         scratch_shapes=[
             pltpu.VMEM((SEQ * NBLK, 2 * DH), BF16),
             pltpu.VMEM((SEQ * NBLK, DH), BF16),
             pltpu.VMEM((2, TILE, SEQ * NBLK), BF16),
             pltpu.VMEM((64, SEQ * NBLK), BF16),
         ],
-        compiler_params=params(),
+        compiler_params=params(SMALL_LIMIT),
         cost_estimate=cost(4 * SEQ * NBLK * SEQ * NBLK * DH, 2_000_000),
         name="route",
     )(slots)
@@ -445,7 +446,7 @@
             pltpu.VMEM((2, SPAN, DH), F32),
             pltpu.VMEM((SEQ, 8, DH), F32),
         ],
-        compiler_params=params(),
+        compiler_params=params(SMALL_LIMIT),
         cost_estimate=cost(6 * 2 * GROUP * QUART * DH * DH, 2_000_000, GROUP * QUART * DH),
         name="attend_tail",
     )(slots, seg_col, seg_row, *partial)

time: 125 us -> 121 us (0.968)
  local copies, waits for them, and re-layouts: 4.31 us -> 1.74 us
  Pallas kernels: 42.1 us -> 39.7 us
    ppermute x9, waiting for transfers between devices: 16.6 us -> 18.7 us  [on_device(): send = lambda x, *pairs: lax.ppermute(x, 'head', list(pairs))]
    unnamed x14 -> x8, local copies, waits for them, and re-layouts: 1.88 us -> 0.01 us
    all_to_all x2, waiting for transfers between devices: 20.4 us -> 18.9 us  [on_device(): lax.all_to_all(x, 'seq', split_axis=0, concat_axis=0, tiled=True)]
  transfers between devices with their start and end apart: 11 -> 11, of which waited for: 5 -> 5; matrix products, arithmetic and copies ran while one was open for 2% -> 1% of each run, Pallas kernels for 28% -> 28%
where the time goes in v4:
time: 121 us; the launch traced here: 120 us
  Pallas kernels  39.7 us (33%)
  starting transfers between devices  39.2 us (32%)
  waiting for transfers between devices  37.6 us (31%)
  local copies, waits for them, and re-layouts  1.74 us (1%)
    all_to_all x2, starting transfers between devices, on_device(): lax.all_to_all(x, 'seq', split_axis=0, concat_axis=0, tiled=True)  21.9 us
    all_to_all x2, waiting for transfers between devices, on_device(): lax.all_to_all(x, 'seq', split_axis=0, concat_axis=0, tiled=True)  18.9 us
    ppermute x9, waiting for transfers between devices, on_device(): send = lambda x, *pairs: lax.ppermute(x, 'head', list(pairs))  18.7 us
    ppermute x9, starting transfers between devices, on_device(): send = lambda x, *pairs: lax.ppermute(x, 'head', list(pairs))  17.3 us
    pallas_call x1, Pallas kernels, attend_stay(): pl.pallas_call(stay_kernel, grid_spec=pltpu.PrefetchScalarGridSpec(num_sc...  15.7 us
    pallas_call x2, Pallas kernels, pack(): pl.pallas_call(kernel, grid=(1,), in_specs=[pl.BlockSpec((QUART, width *...  7.87 us
    pallas_call x1, Pallas kernels, route(): pl.pallas_call(route_kernel, in_specs=[vmem], out_specs=vmem, out_shape=p...  6.71 us
    pallas_call x3, Pallas kernels, slice_group(): pl.pallas_call(slice_kernel, grid_spec=pltpu.PrefetchScalarGridSpec(num_s...  6.6 us
  transfers between devices with their start and end apart: 11, of which 5 were waited for; matrix products, arithmetic and copies ran while one was open for 1% of the time, Pallas kernels for 28%

profile of v4, /device:TPU:1, one launch (start us, length us, event | category | flops | bytes accessed | tf_op | source)
XLA Modules:
  0.0 120.2 jit_solution(6229831743585434312)
XLA Ops:
  0.6 2.7 %pack_one.1 = (bf16[32,56,128]{2,1,0:T(8,128)(2,1)}, bf16[32,56,128]{2,1,0:T(8,128)(2,1)}) custom-call(bf16[192,4096]{1,0:T(8,128)(2,1)} %q_any.1, bf16[192,512]{1,0:T(8,128)(2,1)} %k_any.1, bf16[192,512]{1,0:T(8,128)(2,1)} %v_any.1, bf16[192,4096]{1,0:T(8,128)(2,1)} %g_any.1, s32[1,48]{1,0:T(1,128)} %bitcast.9), custom_call_target="tpu_custom_call" | custom-call | bytes 4000000 | tf_op jit(solution)/shard_map/pack_one/pallas_call | solution.py:100
  3.3 1.3 %collective-permute-start = (bf16[32,56,128]{2,1,0:T(8,128)(2,1)}, bf16[32,56,128]{2,1,0:T(8,128)(2,1)S(1)}, u32[]{:S(2)}, u32[]{:S(2)}) collective-permute-start(bf16[32,56,128]{2,1,0:T(8,128)(2,1)} %get-tuple-element.23), channel_id=1, source_target_pairs={{3,0},{7,4},{11,8},{15,12},{19,16},{23,20},{27,24},{31,28},{35,32}... | collective-permute-start | bytes 1376264 | tf_op jit(solution)/shard_map/ppermute | solution.py:462
  4.6 1.4 %collective-permute-start.2 = (bf16[32,56,128]{2,1,0:T(8,128)(2,1)}, bf16[32,56,128]{2,1,0:T(8,128)(2,1)}, u32[]{:S(2)}, u32[]{:S(2)}) collective-permute-start(bf16[32,56,128]{2,1,0:T(8,128)(2,1)} %get-tuple-element.24), channel_id=1, source_target_pairs={{3,2},{7,6},{11,10},{15,14},{19,18},{23,22},{27,26},{31,30},{35,34... | collective-permute-start | bytes 1376264 | tf_op jit(solution)/shard_map/ppermute | solution.py:462
  6.0 5.2 %pack_rest.1 = (bf16[64,56,128]{2,1,0:T(8,128)(2,1)}, bf16[64,56,128]{2,1,0:T(8,128)(2,1)}, bf16[64,56,128]{2,1,0:T(8,128)(2,1)}) custom-call(bf16[192,4096]{1,0:T(8,128)(2,1)} %q_any.1, bf16[192,512]{1,0:T(8,128)(2,1)} %k_any.1, bf16[192,512]{1,0:T(8,128)(2,1)} %v_any.1, bf16[192,4096]{1,0:T(8,128)(2,1)} %g_any.1, s32[1,48]{1,0:T(1,128)} %bitcast.10), custom_call_target="tpu_custom_call" | custom-call | bytes 6000000 | tf_op jit(solution)/shard_map/pack_rest/pallas_call | solution.py:100
  11.2 1.3 %collective-permute-start.4 = (bf16[64,56,128]{2,1,0:T(8,128)(2,1)}, bf16[64,56,128]{2,1,0:T(8,128)(2,1)S(1)}, u32[]{:S(2)}, u32[]{:S(2)}) collective-permute-start(bf16[64,56,128]{2,1,0:T(8,128)(2,1)} %get-tuple-element.26), channel_id=1, source_target_pairs={{3,0},{7,4},{11,8},{15,12},{19,16},{23,20},{27,24},{31,28},{35,32}... | collective-permute-start | bytes 2752520 | tf_op jit(solution)/shard_map/ppermute | solution.py:462
  12.5 0.7 collective-permute-start.5
  13.2 2.2 %collective-permute-done = bf16[32,56,128]{2,1,0:T(8,128)(2,1)S(1)} collective-permute-done((bf16[32,56,128]{2,1,0:T(8,128)(2,1)}, bf16[32,56,128]{2,1,0:T(8,128)(2,1)S(1)}, u32[]{:S(2)}, u32[]{:S(2)}) %collective-permute-start) | collective-permute-done | bytes 458784 | tf_op jit(solution)/shard_map/ppermute | solution.py:462
  15.4 1.3 %collective-permute-start.1 = (bf16[32,56,128]{2,1,0:T(8,128)(2,1)S(1)}, bf16[32,56,128]{2,1,0:T(8,128)(2,1)S(1)}, u32[]{:S(2)}, u32[]{:S(2)}) collective-permute-start(bf16[32,56,128]{2,1,0:T(8,128)(2,1)S(1)} %collective-permute-done), channel_id=1, source_target_pairs={{0,1},{4,5},{8,9},{12,13},{16,17},{20,21},{24,25},{28,29},{32,33},... | collective-permute-start | bytes 1376264 | tf_op jit(solution)/shard_map/ppermute | solution.py:462
  16.7 0.0 collective-permute-done.2
  16.8 0.7 collective-permute-start.3
  17.5 2.2 %slice_group.4 = bf16[192,2304]{1,0:T(8,128)(2,1)} custom-call(s32[1]{0:T(128)} %bitcast.2.me_ref, bf16[192,4096]{1,0:T(8,128)(2,1)} %q_any.1, bf16[192,512]{1,0:T(8,128)(2,1)} %k_any.1, bf16[192,512]{1,0:T(8,128)(2,1)} %v_any.1, bf16[192,4096]{1,0:T(8,128)(2,1)} %g_any.1), custom_call_target="tpu_custom_call" | custom-call | bytes 1800000 | tf_op jit(solution)/shard_map/slice_group/pallas_call | solution.py:132
  19.7 2.1 %slice_group.3 = bf16[192,2304]{1,0:T(8,128)(2,1)} custom-call(s32[1]{0:T(128)} %bitcast.1.me_ref, bf16[192,4096]{1,0:T(8,128)(2,1)} %q_any.1, bf16[192,512]{1,0:T(8,128)(2,1)} %k_any.1, bf16[192,512]{1,0:T(8,128)(2,1)} %v_any.1, bf16[192,4096]{1,0:T(8,128)(2,1)} %g_any.1), custom_call_target="tpu_custom_call" | custom-call | bytes 1800000 | tf_op jit(solution)/shard_map/slice_group/pallas_call | solution.py:132
  21.8 2.3 %slice_group.5 = bf16[192,2304]{1,0:T(8,128)(2,1)} custom-call(s32[1]{0:T(128)} %bitcast.3.me_ref, bf16[192,4096]{1,0:T(8,128)(2,1)} %q_any.1, bf16[192,512]{1,0:T(8,128)(2,1)} %k_any.1, bf16[192,512]{1,0:T(8,128)(2,1)} %v_any.1, bf16[192,4096]{1,0:T(8,128)(2,1)} %g_any.1), custom_call_target="tpu_custom_call" | custom-call | bytes 1800000 | tf_op jit(solution)/shard_map/slice_group/pallas_call | solution.py:132
  24.1 0.0 collective-permute-done.1
  24.1 0.0 collective-permute-done.3
  24.1 12.3 %collective-permute-done.4 = bf16[64,56,128]{2,1,0:T(8,128)(2,1)S(1)} collective-permute-done((bf16[64,56,128]{2,1,0:T(8,128)(2,1)}, bf16[64,56,128]{2,1,0:T(8,128)(2,1)S(1)}, u32[]{:S(2)}, u32[]{:S(2)}) %collective-permute-start.4) | collective-permute-done | bytes 917536 | tf_op jit(solution)/shard_map/ppermute | solution.py:462
  36.4 1.1 maximum_select_fusion
  37.5 15.5 %all-to-all-start = ((bf16[64,56,128]{2,1,0:T(8,128)(2,1)}), bf16[64,56,128]{2,1,0:T(8,128)(2,1)S(1)}, u32[]{:S(2)}, u32[]{:S(2)}) async-start(bf16[64,56,128]{2,1,0:T(8,128)(2,1)} %maximum_select_fusion), calls=%async_computation | async-start | bytes 1835008 | tf_op jit(solution)/shard_map/all_to_all | solution.py:463
  52.9 2.2 %collective-permute-start.6 = (bf16[192,2304]{1,0:T(8,128)(2,1)S(1)}, bf16[192,2304]{1,0:T(8,128)(2,1)}, u32[]{:S(2)}, u32[]{:S(2)}) collective-permute-start(bf16[192,2304]{1,0:T(8,128)(2,1)S(1)} %copy-done.2), channel_id=1, source_target_pairs={{0,1},{1,2},{2,3},{4,5},{5,6},{6,7},{8,9},{9,10},{10,11},{12,13},{... | collective-permute-start | bytes 2654216 | tf_op jit(solution)/shard_map/ppermute | solution.py:462
  55.2 1.9 %collective-permute-start.7 = (bf16[192,2304]{1,0:T(8,128)(2,1)S(1)}, bf16[192,2304]{1,0:T(8,128)(2,1)}, u32[]{:S(2)}, u32[]{:S(2)}) collective-permute-start(bf16[192,2304]{1,0:T(8,128)(2,1)S(1)} %copy-done.1), channel_id=1, source_target_pairs={{1,0},{2,1},{0,3},{5,4},{6,5},{4,7},{9,8},{10,9},{8,11},{13,12},{1... | collective-permute-start | bytes 2654216 | tf_op jit(solution)/shard_map/ppermute | solution.py:462
  57.1 6.5 %collective-permute-start.8 = (bf16[192,2304]{1,0:T(8,128)(2,1)}, bf16[192,2304]{1,0:T(8,128)(2,1)}, u32[]{:S(2)}, u32[]{:S(2)}) collective-permute-start(bf16[192,2304]{1,0:T(8,128)(2,1)} %slice_group.5), channel_id=1, source_target_pairs={{0,2},{2,0},{1,3},{4,6},{6,4},{5,7},{8,10},{10,8},{9,11},{12,14},{... | collective-permute-start | bytes 2654216 | tf_op jit(solution)/shard_map/ppermute | solution.py:462
  63.6 0.1 slice.3
  63.7 0.6 reshape.43.row_ref
  64.3 0.9 reshape.44.col_ref
  65.2 0.1 copy.15.col_ref
  65.3 13.3 %all-to-all-done.in_ref = bf16[64,56,128]{2,1,0:T(8,128)(2,1)S(1)} async-done(((bf16[64,56,128]{2,1,0:T(8,128)(2,1)}), bf16[64,56,128]{2,1,0:T(8,128)(2,1)S(1)}, u32[]{:S(2)}, u32[]{:S(2)}) %all-to-all-start) | async-done | bytes 917536 | tf_op jit(solution)/shard_map/all_to_all | solution.py:463
  78.7 6.7 %route.1 = bf16[64,56,128]{2,1,0:T(8,128)(2,1)} custom-call(bf16[64,56,128]{2,1,0:T(8,128)(2,1)S(1)} %all-to-all-done.in_ref), custom_call_target="tpu_custom_call" | custom-call | flops 4831838208 | bytes 2000000 | tf_op jit(solution)/shard_map/route/pallas_call | solution.py:208
  85.4 6.4 %all-to-all-start.1 = ((bf16[64,56,128]{2,1,0:T(8,128)(2,1)}), bf16[64,56,128]{2,1,0:T(8,128)(2,1)S(1)}, u32[]{:S(2)}, u32[]{:S(2)}) async-start(bf16[64,56,128]{2,1,0:T(8,128)(2,1)} %route.1), calls=%async_computation.1 | async-start | bytes 1835008 | tf_op jit(solution)/shard_map/all_to_all | solution.py:463
  91.8 4.2 %collective-permute-done.8.two = bf16[192,2304]{1,0:T(8,128)(2,1)} collective-permute-done((bf16[192,2304]{1,0:T(8,128)(2,1)}, bf16[192,2304]{1,0:T(8,128)(2,1)}, u32[]{:S(2)}, u32[]{:S(2)}) %collective-permute-start.8) | collective-permute-done | bytes 884768 | tf_op jit(solution)/shard_map/ppermute | solution.py:462
  96.0 15.7 %attend_stay.1 = (bf16[768,1024]{1,0:T(8,128)(2,1)}, bf16[768,1024]{1,0:T(8,128)(2,1)}, bf16[768,128]{1,0:T(8,128)(2,1)}, bf16[768,128]{1,0:T(8,128)(2,1)}) custom-call(s32[1]{0:T(128)} %bitcast.6.me_ref, bf16[192,4096]{1,0:T(8,128)(2,1)} %q_any.1, bf16[192,512]{1,0:T(8,128)(2,1)} %k_any.1, bf16[192,512]{1,0:T(8,128)(2,1)} %v_any.1, ...), custom_call_target="tpu_custom_call" | custom-call | flops 40768634880 | bytes 6000000 | tf_op jit(solution)/shard_map/attend_stay/pallas_call | solution.py:351
  111.8 5.6 %all-to-all-done.1.slots = bf16[64,56,128]{2,1,0:T(8,128)(2,1)S(1)} async-done(((bf16[64,56,128]{2,1,0:T(8,128)(2,1)}), bf16[64,56,128]{2,1,0:T(8,128)(2,1)S(1)}, u32[]{:S(2)}, u32[]{:S(2)}) %all-to-all-start.1) | async-done | bytes 917536 | tf_op jit(solution)/shard_map/all_to_all | solution.py:463
  117.4 2.8 %attend_tail.1 = (bf16[768,1024]{1,0:T(8,128)(2,1)}, bf16[768,1024]{1,0:T(8,128)(2,1)}, bf16[768,128]{1,0:T(8,128)(2,1)}, bf16[768,128]{1,0:T(8,128)(2,1)}) custom-call(bf16[64,56,128]{2,1,0:T(8,128)(2,1)S(1)} %all-to-all-done.1.slots, s32[256,1]{1,0:T(8,128)S(1)} %copy.15.col_ref, ...), custom_call_target="tpu_custom_call", output_to_operand_aliasing={{0}: (3, {}), {1}: (4, {}), {2}: (5, {}), {3}: (6, {})} | custom-call | flops 301989888 | bytes 2000000 | tf_op jit(solution)/shard_map/attend_tail/pallas_call | solution.py:426
  (12 shorter events, 0.0 us)
Async XLA Ops:
  3.3 12.1 %collective-permute-start = (bf16[32,56,128]{2,1,0:T(8,128)(2,1)}, bf16[32,56,128]{2,1,0:T(8,128)(2,1)S(1)}, u32[]{:S(2)}, u32[]{:S(2)}) collective-permute-start(bf16[32,56,128]{2,1,0:T(8,128)(2,1)} %get-tuple-element.23), channel_id=1, source_target_pairs={{3,0},{7,4},{11,8},{15,12},{19,16},{23,20},{27,24},{31,28},{35,32}... | collective-permute-start | bytes 1376264 | tf_op jit(solution)/shard_map/ppermute | solution.py:462
  4.6 12.1 %collective-permute-start.2 = (bf16[32,56,128]{2,1,0:T(8,128)(2,1)}, bf16[32,56,128]{2,1,0:T(8,128)(2,1)}, u32[]{:S(2)}, u32[]{:S(2)}) collective-permute-start(bf16[32,56,128]{2,1,0:T(8,128)(2,1)} %get-tuple-element.24), channel_id=1, source_target_pairs={{3,2},{7,6},{11,10},{15,14},{19,18},{23,22},{27,26},{31,30},{35,34... | collective-permute-start | bytes 1376264 | tf_op jit(solution)/shard_map/ppermute | solution.py:462
  11.2 25.1 %collective-permute-start.4 = (bf16[64,56,128]{2,1,0:T(8,128)(2,1)}, bf16[64,56,128]{2,1,0:T(8,128)(2,1)S(1)}, u32[]{:S(2)}, u32[]{:S(2)}) collective-permute-start(bf16[64,56,128]{2,1,0:T(8,128)(2,1)} %get-tuple-element.26), channel_id=1, source_target_pairs={{3,0},{7,4},{11,8},{15,12},{19,16},{23,20},{27,24},{31,28},{35,32}... | collective-permute-start | bytes 2752520 | tf_op jit(solution)/shard_map/ppermute | solution.py:462
  12.5 23.9 %collective-permute-start.5 = (bf16[64,56,128]{2,1,0:T(8,128)(2,1)}, bf16[64,56,128]{2,1,0:T(8,128)(2,1)S(1)}, u32[]{:S(2)}, u32[]{:S(2)}) collective-permute-start(bf16[64,56,128]{2,1,0:T(8,128)(2,1)} %get-tuple-element.27), channel_id=1, source_target_pairs={{3,2},{7,6},{11,10},{15,14},{19,18},{23,22},{27,26},{31,30},{35,34... | collective-permute-start | bytes 2752520 | tf_op jit(solution)/shard_map/ppermute | solution.py:462
  15.4 8.7 %collective-permute-start.1 = (bf16[32,56,128]{2,1,0:T(8,128)(2,1)S(1)}, bf16[32,56,128]{2,1,0:T(8,128)(2,1)S(1)}, u32[]{:S(2)}, u32[]{:S(2)}) collective-permute-start(bf16[32,56,128]{2,1,0:T(8,128)(2,1)S(1)} %collective-permute-done), channel_id=1, source_target_pairs={{0,1},{4,5},{8,9},{12,13},{16,17},{20,21},{24,25},{28,29},{32,33},... | collective-permute-start | bytes 1376264 | tf_op jit(solution)/shard_map/ppermute | solution.py:462
  16.8 7.3 %collective-permute-start.3 = (bf16[32,56,128]{2,1,0:T(8,128)(2,1)}, bf16[32,56,128]{2,1,0:T(8,128)(2,1)S(1)}, u32[]{:S(2)}, u32[]{:S(2)}) collective-permute-start(bf16[32,56,128]{2,1,0:T(8,128)(2,1)} %collective-permute-done.2), channel_id=1, source_target_pairs={{2,1},{6,5},{10,9},{14,13},{18,17},{22,21},{26,25},{30,29},{34,33}... | collective-permute-start | bytes 1376264 | tf_op jit(solution)/shard_map/ppermute | solution.py:462
  21.8 14.6 %copy-start = (bf16[64,56,128]{2,1,0:T(8,128)(2,1)S(1)}, bf16[64,56,128]{2,1,0:T(8,128)(2,1)}, u32[]{:S(2)}) copy-start(bf16[64,56,128]{2,1,0:T(8,128)(2,1)} %get-tuple-element.25) | copy-start | bytes 2752516
  37.5 15.5 %copy-start.2 = (bf16[192,2304]{1,0:T(8,128)(2,1)S(1)}, bf16[192,2304]{1,0:T(8,128)(2,1)}, u32[]{:S(2)}) copy-start(bf16[192,2304]{1,0:T(8,128)(2,1)} %slice_group.3) | copy-start | bytes 2654212
  37.5 17.7 %copy-start.1 = (bf16[192,2304]{1,0:T(8,128)(2,1)S(1)}, bf16[192,2304]{1,0:T(8,128)(2,1)}, u32[]{:S(2)}) copy-start(bf16[192,2304]{1,0:T(8,128)(2,1)} %slice_group.4) | copy-start | bytes 2654212
  37.5 26.1 %copy-start.3 = (s32[768]{0:T(1024)S(1)}, s32[768]{0:T(1024)}, u32[]{:S(2)}) copy-start(s32[768]{0:T(1024)} %param.11) | copy-start | bytes 9220
  37.5 41.2 %all-to-all-start = ((bf16[64,56,128]{2,1,0:T(8,128)(2,1)}), bf16[64,56,128]{2,1,0:T(8,128)(2,1)S(1)}, u32[]{:S(2)}, u32[]{:S(2)}) async-start(bf16[64,56,128]{2,1,0:T(8,128)(2,1)} %maximum_select_fusion), calls=%async_computation | async-start | bytes 1835008 | tf_op jit(solution)/shard_map/all_to_all | solution.py:463
  52.9 38.9 %collective-permute-start.6 = (bf16[192,2304]{1,0:T(8,128)(2,1)S(1)}, bf16[192,2304]{1,0:T(8,128)(2,1)}, u32[]{:S(2)}, u32[]{:S(2)}) collective-permute-start(bf16[192,2304]{1,0:T(8,128)(2,1)S(1)} %copy-done.2), channel_id=1, source_target_pairs={{0,1},{1,2},{2,3},{4,5},{5,6},{6,7},{8,9},{9,10},{10,11},{12,13},{... | collective-permute-start | bytes 2654216 | tf_op jit(solution)/shard_map/ppermute | solution.py:462
  55.2 36.7 %collective-permute-start.7 = (bf16[192,2304]{1,0:T(8,128)(2,1)S(1)}, bf16[192,2304]{1,0:T(8,128)(2,1)}, u32[]{:S(2)}, u32[]{:S(2)}) collective-permute-start(bf16[192,2304]{1,0:T(8,128)(2,1)S(1)} %copy-done.1), channel_id=1, source_target_pairs={{1,0},{2,1},{0,3},{5,4},{6,5},{4,7},{9,8},{10,9},{8,11},{13,12},{1... | collective-permute-start | bytes 2654216 | tf_op jit(solution)/shard_map/ppermute | solution.py:462
  57.1 39.0 %collective-permute-start.8 = (bf16[192,2304]{1,0:T(8,128)(2,1)}, bf16[192,2304]{1,0:T(8,128)(2,1)}, u32[]{:S(2)}, u32[]{:S(2)}) collective-permute-start(bf16[192,2304]{1,0:T(8,128)(2,1)} %slice_group.5), channel_id=1, source_target_pairs={{0,2},{2,0},{1,3},{4,6},{6,4},{5,7},{8,10},{10,8},{9,11},{12,14},{... | collective-permute-start | bytes 2654216 | tf_op jit(solution)/shard_map/ppermute | solution.py:462
  85.4 32.0 %all-to-all-start.1 = ((bf16[64,56,128]{2,1,0:T(8,128)(2,1)}), bf16[64,56,128]{2,1,0:T(8,128)(2,1)S(1)}, u32[]{:S(2)}, u32[]{:S(2)}) async-start(bf16[64,56,128]{2,1,0:T(8,128)(2,1)} %route.1), calls=%async_computation.1 | async-start | bytes 1835008 | tf_op jit(solution)/shard_map/all_to_all | solution.py:463

commit v5 on v4

--- a/solution.py
+++ b/solution.py
@@ -250,7 +250,7 @@
 
 
 PAD = 640
-PAIR = 2
+PAIR = 8
 
 
 def stay_kernel(

time: 121 us -> 121 us (level)
  waiting for transfers between devices: 37.6 us -> 40.9 us
  Pallas kernels: 39.7 us -> 36.6 us
    all_to_all x2, waiting for transfers between devices: 18.9 us -> 22 us  [on_device(): lax.all_to_all(x, 'seq', split_axis=0, concat_axis=0, tiled=True)]
    pallas_call x1, Pallas kernels: 15.7 us -> 12.6 us  [attend_stay(): pl.pallas_call(stay_kernel, grid_spec=pltpu.PrefetchScalarGridSpec(num_sc...]
  transfers between devices with their start and end apart: 11 -> 11, of which waited for: 5 -> 5; matrix products, arithmetic and copies ran while one was open for 1% -> 1% of each run, Pallas kernels for 28% -> 26%
where the time goes in v5:
time: 121 us; the launch traced here: 120 us
  waiting for transfers between devices  40.9 us (34%)
  starting transfers between devices  39 us (32%)
  Pallas kernels  36.6 us (30%)
  local copies, waits for them, and re-layouts  1.74 us (1%)
    all_to_all x2, waiting for transfers between devices, on_device(): lax.all_to_all(x, 'seq', split_axis=0, concat_axis=0, tiled=True)  22 us
    all_to_all x2, starting transfers between devices, on_device(): lax.all_to_all(x, 'seq', split_axis=0, concat_axis=0, tiled=True)  21.7 us
    ppermute x9, waiting for transfers between devices, on_device(): send = lambda x, *pairs: lax.ppermute(x, 'head', list(pairs))  18.9 us
    ppermute x9, starting transfers between devices, on_device(): send = lambda x, *pairs: lax.ppermute(x, 'head', list(pairs))  17.3 us
    pallas_call x1, Pallas kernels, attend_stay(): pl.pallas_call(stay_kernel, grid_spec=pltpu.PrefetchScalarGridSpec(num_sc...  12.6 us
    pallas_call x2, Pallas kernels, pack(): pl.pallas_call(kernel, grid=(1,), in_specs=[pl.BlockSpec((QUART, width *...  7.87 us
    pallas_call x1, Pallas kernels, route(): pl.pallas_call(route_kernel, in_specs=[vmem], out_specs=vmem, out_shape=p...  6.71 us
    pallas_call x3, Pallas kernels, slice_group(): pl.pallas_call(slice_kernel, grid_spec=pltpu.PrefetchScalarGridSpec(num_s...  6.6 us
  transfers between devices with their start and end apart: 11, of which 5 were waited for; matrix products, arithmetic and copies ran while one was open for 1% of the time, Pallas kernels for 26%

profile of v5, /device:TPU:1, one launch (start us, length us, event | category | flops | bytes accessed | tf_op | source)
XLA Modules:
  0.0 120.2 jit_solution(6713704745634741128)
XLA Ops:
  0.6 2.7 %pack_one.1 = (bf16[32,56,128]{2,1,0:T(8,128)(2,1)}, bf16[32,56,128]{2,1,0:T(8,128)(2,1)}) custom-call(bf16[192,4096]{1,0:T(8,128)(2,1)} %q_any.1, bf16[192,512]{1,0:T(8,128)(2,1)} %k_any.1, bf16[192,512]{1,0:T(8,128)(2,1)} %v_any.1, bf16[192,4096]{1,0:T(8,128)(2,1)} %g_any.1, s32[1,48]{1,0:T(1,128)} %bitcast.9), custom_call_target="tpu_custom_call" | custom-call | bytes 4000000 | tf_op jit(solution)/shard_map/pack_one/pallas_call | solution.py:100
  3.3 1.3 %collective-permute-start = (bf16[32,56,128]{2,1,0:T(8,128)(2,1)}, bf16[32,56,128]{2,1,0:T(8,128)(2,1)S(1)}, u32[]{:S(2)}, u32[]{:S(2)}) collective-permute-start(bf16[32,56,128]{2,1,0:T(8,128)(2,1)} %get-tuple-element.23), channel_id=1, source_target_pairs={{3,0},{7,4},{11,8},{15,12},{19,16},{23,20},{27,24},{31,28},{35,32}... | collective-permute-start | bytes 1376264 | tf_op jit(solution)/shard_map/ppermute | solution.py:462
  4.6 1.4 %collective-permute-start.2 = (bf16[32,56,128]{2,1,0:T(8,128)(2,1)}, bf16[32,56,128]{2,1,0:T(8,128)(2,1)}, u32[]{:S(2)}, u32[]{:S(2)}) collective-permute-start(bf16[32,56,128]{2,1,0:T(8,128)(2,1)} %get-tuple-element.24), channel_id=1, source_target_pairs={{3,2},{7,6},{11,10},{15,14},{19,18},{23,22},{27,26},{31,30},{35,34... | collective-permute-start | bytes 1376264 | tf_op jit(solution)/shard_map/ppermute | solution.py:462
  6.0 5.2 %pack_rest.1 = (bf16[64,56,128]{2,1,0:T(8,128)(2,1)}, bf16[64,56,128]{2,1,0:T(8,128)(2,1)}, bf16[64,56,128]{2,1,0:T(8,128)(2,1)}) custom-call(bf16[192,4096]{1,0:T(8,128)(2,1)} %q_any.1, bf16[192,512]{1,0:T(8,128)(2,1)} %k_any.1, bf16[192,512]{1,0:T(8,128)(2,1)} %v_any.1, bf16[192,4096]{1,0:T(8,128)(2,1)} %g_any.1, s32[1,48]{1,0:T(1,128)} %bitcast.10), custom_call_target="tpu_custom_call" | custom-call | bytes 6000000 | tf_op jit(solution)/shard_map/pack_rest/pallas_call | solution.py:100
  11.2 1.3 %collective-permute-start.4 = (bf16[64,56,128]{2,1,0:T(8,128)(2,1)}, bf16[64,56,128]{2,1,0:T(8,128)(2,1)S(1)}, u32[]{:S(2)}, u32[]{:S(2)}) collective-permute-start(bf16[64,56,128]{2,1,0:T(8,128)(2,1)} %get-tuple-element.26), channel_id=1, source_target_pairs={{3,0},{7,4},{11,8},{15,12},{19,16},{23,20},{27,24},{31,28},{35,32}... | collective-permute-start | bytes 2752520 | tf_op jit(solution)/shard_map/ppermute | solution.py:462
  12.5 0.7 collective-permute-start.5
  13.2 2.2 %collective-permute-done = bf16[32,56,128]{2,1,0:T(8,128)(2,1)S(1)} collective-permute-done((bf16[32,56,128]{2,1,0:T(8,128)(2,1)}, bf16[32,56,128]{2,1,0:T(8,128)(2,1)S(1)}, u32[]{:S(2)}, u32[]{:S(2)}) %collective-permute-start) | collective-permute-done | bytes 458784 | tf_op jit(solution)/shard_map/ppermute | solution.py:462
  15.4 1.3 %collective-permute-start.1 = (bf16[32,56,128]{2,1,0:T(8,128)(2,1)S(1)}, bf16[32,56,128]{2,1,0:T(8,128)(2,1)S(1)}, u32[]{:S(2)}, u32[]{:S(2)}) collective-permute-start(bf16[32,56,128]{2,1,0:T(8,128)(2,1)S(1)} %collective-permute-done), channel_id=1, source_target_pairs={{0,1},{4,5},{8,9},{12,13},{16,17},{20,21},{24,25},{28,29},{32,33},... | collective-permute-start | bytes 1376264 | tf_op jit(solution)/shard_map/ppermute | solution.py:462
  16.7 0.0 collective-permute-done.2
  16.8 0.7 collective-permute-start.3
  17.5 2.2 %slice_group.4 = bf16[192,2304]{1,0:T(8,128)(2,1)} custom-call(s32[1]{0:T(128)} %bitcast.2.me_ref, bf16[192,4096]{1,0:T(8,128)(2,1)} %q_any.1, bf16[192,512]{1,0:T(8,128)(2,1)} %k_any.1, bf16[192,512]{1,0:T(8,128)(2,1)} %v_any.1, bf16[192,4096]{1,0:T(8,128)(2,1)} %g_any.1), custom_call_target="tpu_custom_call" | custom-call | bytes 1800000 | tf_op jit(solution)/shard_map/slice_group/pallas_call | solution.py:132
  19.7 2.1 %slice_group.3 = bf16[192,2304]{1,0:T(8,128)(2,1)} custom-call(s32[1]{0:T(128)} %bitcast.1.me_ref, bf16[192,4096]{1,0:T(8,128)(2,1)} %q_any.1, bf16[192,512]{1,0:T(8,128)(2,1)} %k_any.1, bf16[192,512]{1,0:T(8,128)(2,1)} %v_any.1, bf16[192,4096]{1,0:T(8,128)(2,1)} %g_any.1), custom_call_target="tpu_custom_call" | custom-call | bytes 1800000 | tf_op jit(solution)/shard_map/slice_group/pallas_call | solution.py:132
  21.8 2.3 %slice_group.5 = bf16[192,2304]{1,0:T(8,128)(2,1)} custom-call(s32[1]{0:T(128)} %bitcast.3.me_ref, bf16[192,4096]{1,0:T(8,128)(2,1)} %q_any.1, bf16[192,512]{1,0:T(8,128)(2,1)} %k_any.1, bf16[192,512]{1,0:T(8,128)(2,1)} %v_any.1, bf16[192,4096]{1,0:T(8,128)(2,1)} %g_any.1), custom_call_target="tpu_custom_call" | custom-call | bytes 1800000 | tf_op jit(solution)/shard_map/slice_group/pallas_call | solution.py:132
  24.1 0.0 collective-permute-done.1
  24.1 0.0 collective-permute-done.3
  24.1 12.3 %collective-permute-done.4 = bf16[64,56,128]{2,1,0:T(8,128)(2,1)S(1)} collective-permute-done((bf16[64,56,128]{2,1,0:T(8,128)(2,1)}, bf16[64,56,128]{2,1,0:T(8,128)(2,1)S(1)}, u32[]{:S(2)}, u32[]{:S(2)}) %collective-permute-start.4) | collective-permute-done | bytes 917536 | tf_op jit(solution)/shard_map/ppermute | solution.py:462
  36.4 1.1 maximum_select_fusion
  37.5 15.5 %all-to-all-start = ((bf16[64,56,128]{2,1,0:T(8,128)(2,1)}), bf16[64,56,128]{2,1,0:T(8,128)(2,1)S(1)}, u32[]{:S(2)}, u32[]{:S(2)}) async-start(bf16[64,56,128]{2,1,0:T(8,128)(2,1)} %maximum_select_fusion), calls=%async_computation | async-start | bytes 1835008 | tf_op jit(solution)/shard_map/all_to_all | solution.py:463
  52.9 2.2 %collective-permute-start.6 = (bf16[192,2304]{1,0:T(8,128)(2,1)S(1)}, bf16[192,2304]{1,0:T(8,128)(2,1)}, u32[]{:S(2)}, u32[]{:S(2)}) collective-permute-start(bf16[192,2304]{1,0:T(8,128)(2,1)S(1)} %copy-done.2), channel_id=1, source_target_pairs={{0,1},{1,2},{2,3},{4,5},{5,6},{6,7},{8,9},{9,10},{10,11},{12,13},{... | collective-permute-start | bytes 2654216 | tf_op jit(solution)/shard_map/ppermute | solution.py:462
  55.2 1.9 %collective-permute-start.7 = (bf16[192,2304]{1,0:T(8,128)(2,1)S(1)}, bf16[192,2304]{1,0:T(8,128)(2,1)}, u32[]{:S(2)}, u32[]{:S(2)}) collective-permute-start(bf16[192,2304]{1,0:T(8,128)(2,1)S(1)} %copy-done.1), channel_id=1, source_target_pairs={{1,0},{2,1},{0,3},{5,4},{6,5},{4,7},{9,8},{10,9},{8,11},{13,12},{1... | collective-permute-start | bytes 2654216 | tf_op jit(solution)/shard_map/ppermute | solution.py:462
  57.1 6.5 %collective-permute-start.8 = (bf16[192,2304]{1,0:T(8,128)(2,1)}, bf16[192,2304]{1,0:T(8,128)(2,1)}, u32[]{:S(2)}, u32[]{:S(2)}) collective-permute-start(bf16[192,2304]{1,0:T(8,128)(2,1)} %slice_group.5), channel_id=1, source_target_pairs={{0,2},{2,0},{1,3},{4,6},{6,4},{5,7},{8,10},{10,8},{9,11},{12,14},{... | collective-permute-start | bytes 2654216 | tf_op jit(solution)/shard_map/ppermute | solution.py:462
  63.6 0.1 slice.3
  63.7 0.6 reshape.43.row_ref
  64.3 0.9 reshape.44.col_ref
  65.2 0.1 copy.15.col_ref
  65.3 13.3 %all-to-all-done.in_ref = bf16[64,56,128]{2,1,0:T(8,128)(2,1)S(1)} async-done(((bf16[64,56,128]{2,1,0:T(8,128)(2,1)}), bf16[64,56,128]{2,1,0:T(8,128)(2,1)S(1)}, u32[]{:S(2)}, u32[]{:S(2)}) %all-to-all-start) | async-done | bytes 917536 | tf_op jit(solution)/shard_map/all_to_all | solution.py:463
  78.7 6.7 %route.1 = bf16[64,56,128]{2,1,0:T(8,128)(2,1)} custom-call(bf16[64,56,128]{2,1,0:T(8,128)(2,1)S(1)} %all-to-all-done.in_ref), custom_call_target="tpu_custom_call" | custom-call | flops 4831838208 | bytes 2000000 | tf_op jit(solution)/shard_map/route/pallas_call | solution.py:208
  85.4 6.2 %all-to-all-start.1 = ((bf16[64,56,128]{2,1,0:T(8,128)(2,1)}), bf16[64,56,128]{2,1,0:T(8,128)(2,1)S(1)}, u32[]{:S(2)}, u32[]{:S(2)}) async-start(bf16[64,56,128]{2,1,0:T(8,128)(2,1)} %route.1), calls=%async_computation.1 | async-start | bytes 1835008 | tf_op jit(solution)/shard_map/all_to_all | solution.py:463
  91.7 4.4 %collective-permute-done.8.two = bf16[192,2304]{1,0:T(8,128)(2,1)} collective-permute-done((bf16[192,2304]{1,0:T(8,128)(2,1)}, bf16[192,2304]{1,0:T(8,128)(2,1)}, u32[]{:S(2)}, u32[]{:S(2)}) %collective-permute-start.8) | collective-permute-done | bytes 884768 | tf_op jit(solution)/shard_map/ppermute | solution.py:462
  96.0 12.6 %attend_stay.1 = (bf16[768,1024]{1,0:T(8,128)(2,1)}, bf16[768,1024]{1,0:T(8,128)(2,1)}, bf16[768,128]{1,0:T(8,128)(2,1)}, bf16[768,128]{1,0:T(8,128)(2,1)}) custom-call(s32[1]{0:T(128)} %bitcast.6.me_ref, bf16[192,4096]{1,0:T(8,128)(2,1)} %q_any.1, bf16[192,512]{1,0:T(8,128)(2,1)} %k_any.1, bf16[192,512]{1,0:T(8,128)(2,1)} %v_any.1, ...), custom_call_target="tpu_custom_call" | custom-call | flops 40768634880 | bytes 6000000 | tf_op jit(solution)/shard_map/attend_stay/pallas_call | solution.py:351
  108.7 8.7 %all-to-all-done.1.slots = bf16[64,56,128]{2,1,0:T(8,128)(2,1)S(1)} async-done(((bf16[64,56,128]{2,1,0:T(8,128)(2,1)}), bf16[64,56,128]{2,1,0:T(8,128)(2,1)S(1)}, u32[]{:S(2)}, u32[]{:S(2)}) %all-to-all-start.1) | async-done | bytes 917536 | tf_op jit(solution)/shard_map/all_to_all | solution.py:463
  117.4 2.8 %attend_tail.1 = (bf16[768,1024]{1,0:T(8,128)(2,1)}, bf16[768,1024]{1,0:T(8,128)(2,1)}, bf16[768,128]{1,0:T(8,128)(2,1)}, bf16[768,128]{1,0:T(8,128)(2,1)}) custom-call(bf16[64,56,128]{2,1,0:T(8,128)(2,1)S(1)} %all-to-all-done.1.slots, s32[256,1]{1,0:T(8,128)S(1)} %copy.15.col_ref, ...), custom_call_target="tpu_custom_call", output_to_operand_aliasing={{0}: (3, {}), {1}: (4, {}), {2}: (5, {}), {3}: (6, {})} | custom-call | flops 301989888 | bytes 2000000 | tf_op jit(solution)/shard_map/attend_tail/pallas_call | solution.py:426
  (12 shorter events, 0.0 us)
Async XLA Ops:
  3.3 12.1 %collective-permute-start = (bf16[32,56,128]{2,1,0:T(8,128)(2,1)}, bf16[32,56,128]{2,1,0:T(8,128)(2,1)S(1)}, u32[]{:S(2)}, u32[]{:S(2)}) collective-permute-start(bf16[32,56,128]{2,1,0:T(8,128)(2,1)} %get-tuple-element.23), channel_id=1, source_target_pairs={{3,0},{7,4},{11,8},{15,12},{19,16},{23,20},{27,24},{31,28},{35,32}... | collective-permute-start | bytes 1376264 | tf_op jit(solution)/shard_map/ppermute | solution.py:462
  4.6 12.1 %collective-permute-start.2 = (bf16[32,56,128]{2,1,0:T(8,128)(2,1)}, bf16[32,56,128]{2,1,0:T(8,128)(2,1)}, u32[]{:S(2)}, u32[]{:S(2)}) collective-permute-start(bf16[32,56,128]{2,1,0:T(8,128)(2,1)} %get-tuple-element.24), channel_id=1, source_target_pairs={{3,2},{7,6},{11,10},{15,14},{19,18},{23,22},{27,26},{31,30},{35,34... | collective-permute-start | bytes 1376264 | tf_op jit(solution)/shard_map/ppermute | solution.py:462
  11.2 25.1 %collective-permute-start.4 = (bf16[64,56,128]{2,1,0:T(8,128)(2,1)}, bf16[64,56,128]{2,1,0:T(8,128)(2,1)S(1)}, u32[]{:S(2)}, u32[]{:S(2)}) collective-permute-start(bf16[64,56,128]{2,1,0:T(8,128)(2,1)} %get-tuple-element.26), channel_id=1, source_target_pairs={{3,0},{7,4},{11,8},{15,12},{19,16},{23,20},{27,24},{31,28},{35,32}... | collective-permute-start | bytes 2752520 | tf_op jit(solution)/shard_map/ppermute | solution.py:462
  12.5 23.9 %collective-permute-start.5 = (bf16[64,56,128]{2,1,0:T(8,128)(2,1)}, bf16[64,56,128]{2,1,0:T(8,128)(2,1)S(1)}, u32[]{:S(2)}, u32[]{:S(2)}) collective-permute-start(bf16[64,56,128]{2,1,0:T(8,128)(2,1)} %get-tuple-element.27), channel_id=1, source_target_pairs={{3,2},{7,6},{11,10},{15,14},{19,18},{23,22},{27,26},{31,30},{35,34... | collective-permute-start | bytes 2752520 | tf_op jit(solution)/shard_map/ppermute | solution.py:462
  15.4 8.7 %collective-permute-start.1 = (bf16[32,56,128]{2,1,0:T(8,128)(2,1)S(1)}, bf16[32,56,128]{2,1,0:T(8,128)(2,1)S(1)}, u32[]{:S(2)}, u32[]{:S(2)}) collective-permute-start(bf16[32,56,128]{2,1,0:T(8,128)(2,1)S(1)} %collective-permute-done), channel_id=1, source_target_pairs={{0,1},{4,5},{8,9},{12,13},{16,17},{20,21},{24,25},{28,29},{32,33},... | collective-permute-start | bytes 1376264 | tf_op jit(solution)/shard_map/ppermute | solution.py:462
  16.8 7.3 %collective-permute-start.3 = (bf16[32,56,128]{2,1,0:T(8,128)(2,1)}, bf16[32,56,128]{2,1,0:T(8,128)(2,1)S(1)}, u32[]{:S(2)}, u32[]{:S(2)}) collective-permute-start(bf16[32,56,128]{2,1,0:T(8,128)(2,1)} %collective-permute-done.2), channel_id=1, source_target_pairs={{2,1},{6,5},{10,9},{14,13},{18,17},{22,21},{26,25},{30,29},{34,33}... | collective-permute-start | bytes 1376264 | tf_op jit(solution)/shard_map/ppermute | solution.py:462
  21.8 14.6 %copy-start = (bf16[64,56,128]{2,1,0:T(8,128)(2,1)S(1)}, bf16[64,56,128]{2,1,0:T(8,128)(2,1)}, u32[]{:S(2)}) copy-start(bf16[64,56,128]{2,1,0:T(8,128)(2,1)} %get-tuple-element.25) | copy-start | bytes 2752516
  37.5 15.5 %copy-start.2 = (bf16[192,2304]{1,0:T(8,128)(2,1)S(1)}, bf16[192,2304]{1,0:T(8,128)(2,1)}, u32[]{:S(2)}) copy-start(bf16[192,2304]{1,0:T(8,128)(2,1)} %slice_group.3) | copy-start | bytes 2654212
  37.5 17.7 %copy-start.1 = (bf16[192,2304]{1,0:T(8,128)(2,1)S(1)}, bf16[192,2304]{1,0:T(8,128)(2,1)}, u32[]{:S(2)}) copy-start(bf16[192,2304]{1,0:T(8,128)(2,1)} %slice_group.4) | copy-start | bytes 2654212
  37.5 26.1 %copy-start.3 = (s32[768]{0:T(1024)S(1)}, s32[768]{0:T(1024)}, u32[]{:S(2)}) copy-start(s32[768]{0:T(1024)} %param.11) | copy-start | bytes 9220
  37.5 41.2 %all-to-all-start = ((bf16[64,56,128]{2,1,0:T(8,128)(2,1)}), bf16[64,56,128]{2,1,0:T(8,128)(2,1)S(1)}, u32[]{:S(2)}, u32[]{:S(2)}) async-start(bf16[64,56,128]{2,1,0:T(8,128)(2,1)} %maximum_select_fusion), calls=%async_computation | async-start | bytes 1835008 | tf_op jit(solution)/shard_map/all_to_all | solution.py:463
  52.9 38.7 %collective-permute-start.6 = (bf16[192,2304]{1,0:T(8,128)(2,1)S(1)}, bf16[192,2304]{1,0:T(8,128)(2,1)}, u32[]{:S(2)}, u32[]{:S(2)}) collective-permute-start(bf16[192,2304]{1,0:T(8,128)(2,1)S(1)} %copy-done.2), channel_id=1, source_target_pairs={{0,1},{1,2},{2,3},{4,5},{5,6},{6,7},{8,9},{9,10},{10,11},{12,13},{... | collective-permute-start | bytes 2654216 | tf_op jit(solution)/shard_map/ppermute | solution.py:462
  55.2 36.5 %collective-permute-start.7 = (bf16[192,2304]{1,0:T(8,128)(2,1)S(1)}, bf16[192,2304]{1,0:T(8,128)(2,1)}, u32[]{:S(2)}, u32[]{:S(2)}) collective-permute-start(bf16[192,2304]{1,0:T(8,128)(2,1)S(1)} %copy-done.1), channel_id=1, source_target_pairs={{1,0},{2,1},{0,3},{5,4},{6,5},{4,7},{9,8},{10,9},{8,11},{13,12},{1... | collective-permute-start | bytes 2654216 | tf_op jit(solution)/shard_map/ppermute | solution.py:462
  57.1 39.0 %collective-permute-start.8 = (bf16[192,2304]{1,0:T(8,128)(2,1)}, bf16[192,2304]{1,0:T(8,128)(2,1)}, u32[]{:S(2)}, u32[]{:S(2)}) collective-permute-start(bf16[192,2304]{1,0:T(8,128)(2,1)} %slice_group.5), channel_id=1, source_target_pairs={{0,2},{2,0},{1,3},{4,6},{6,4},{5,7},{8,10},{10,8},{9,11},{12,14},{... | collective-permute-start | bytes 2654216 | tf_op jit(solution)/shard_map/ppermute | solution.py:462
  85.4 32.0 %all-to-all-start.1 = ((bf16[64,56,128]{2,1,0:T(8,128)(2,1)}), bf16[64,56,128]{2,1,0:T(8,128)(2,1)S(1)}, u32[]{:S(2)}, u32[]{:S(2)}) async-start(bf16[64,56,128]{2,1,0:T(8,128)(2,1)} %route.1), calls=%async_computation.1 | async-start | bytes 1835008 | tf_op jit(solution)/shard_map/all_to_all | solution.py:463

commit v6 on v5

--- a/solution.py
+++ b/solution.py
@@ -56,8 +56,8 @@
 def pack_group(group, q_ref, k_ref, v_ref, g_ref, out, qs, ks, small):
     half = SEQ // 2
     thin = slice(group * DH, (group + 1) * DH)
-    ks[0] = k_ref[:, thin].astype(F32)
-    ks[1] = v_ref[:, thin].astype(F32)
+    ks[0, 0:QUART, :] = k_ref[:, thin].astype(F32)
+    ks[1, 0:QUART, :] = v_ref[:, thin].astype(F32)
     pieces = []
     for r in range(8):
         rows = ks[r // 4, pl.ds(r % 4, NBLK, stride=BLK), :]
@@ -69,7 +69,7 @@
     for which, src in enumerate((q_ref, g_ref)):
         dst = out[which]
         for n in range(GROUP):
-            qs[n] = src[:, group * QW + n * DH : group * QW + (n + 1) * DH].astype(F32)
+            qs[n, 0:QUART, :] = src[:, group * QW + n * DH : group * QW + (n + 1) * DH].astype(F32)
             for t in range(BLK):
                 rows = qs[n, pl.ds(t, NBLK, stride=BLK), :]
                 dst[t * GROUP + n, 0:NBLK, :] = rows.astype(BF16)
@@ -110,8 +110,8 @@
         out_specs=[pl.BlockSpec(x, lambda i: (0, 0, 0)) for x in shapes],
         out_shape=[jax.ShapeDtypeStruct(x, BF16) for x in shapes],
         scratch_shapes=[
-            pltpu.VMEM((GROUP, QUART, DH), F32),
-            pltpu.VMEM((2, QUART, DH), F32),
+            pltpu.VMEM((GROUP, QUART + 8, DH), F32),
+            pltpu.VMEM((2, QUART + 8, DH), F32),
             pltpu.VMEM((SEQ, 8, DH), F32),
         ],
         compiler_params=params(),

time: 121 us -> 121 us (level)
  no operation moved by 1% of the time
where the time goes in v6:
time: 121 us; the launch traced here: 120 us
  waiting for transfers between devices  40.9 us (34%)
  starting transfers between devices  39 us (32%)
  Pallas kernels  36.6 us (30%)
  local copies, waits for them, and re-layouts  1.74 us (1%)
    all_to_all x2, waiting for transfers between devices, on_device(): lax.all_to_all(x, 'seq', split_axis=0, concat_axis=0, tiled=True)  22 us
    all_to_all x2, starting transfers between devices, on_device(): lax.all_to_all(x, 'seq', split_axis=0, concat_axis=0, tiled=True)  21.7 us
    ppermute x9, waiting for transfers between devices, on_device(): send = lambda x, *pairs: lax.ppermute(x, 'head', list(pairs))  18.9 us
    ppermute x9, starting transfers between devices, on_device(): send = lambda x, *pairs: lax.ppermute(x, 'head', list(pairs))  17.3 us
    pallas_call x1, Pallas kernels, attend_stay(): pl.pallas_call(stay_kernel, grid_spec=pltpu.PrefetchScalarGridSpec(num_sc...  12.6 us
    pallas_call x2, Pallas kernels, pack(): pl.pallas_call(kernel, grid=(1,), in_specs=[pl.BlockSpec((QUART, width *...  7.87 us
    pallas_call x1, Pallas kernels, route(): pl.pallas_call(route_kernel, in_specs=[vmem], out_specs=vmem, out_shape=p...  6.71 us
    pallas_call x3, Pallas kernels, slice_group(): pl.pallas_call(slice_kernel, grid_spec=pltpu.PrefetchScalarGridSpec(num_s...  6.6 us
  transfers between devices with their start and end apart: 11, of which 5 were waited for; matrix products, arithmetic and copies ran while one was open for 1% of the time, Pallas kernels for 26%

profile of v6, /device:TPU:1, one launch (start us, length us, event | category | flops | bytes accessed | tf_op | source)
XLA Modules:
  0.0 120.2 jit_solution(14476610649210861948)
XLA Ops:
  0.6 2.7 %pack_one.1 = (bf16[32,56,128]{2,1,0:T(8,128)(2,1)}, bf16[32,56,128]{2,1,0:T(8,128)(2,1)}) custom-call(bf16[192,4096]{1,0:T(8,128)(2,1)} %q_any.1, bf16[192,512]{1,0:T(8,128)(2,1)} %k_any.1, bf16[192,512]{1,0:T(8,128)(2,1)} %v_any.1, bf16[192,4096]{1,0:T(8,128)(2,1)} %g_any.1, s32[1,48]{1,0:T(1,128)} %bitcast.9), custom_call_target="tpu_custom_call" | custom-call | bytes 4000000 | tf_op jit(solution)/shard_map/pack_one/pallas_call | solution.py:100
  3.3 1.3 %collective-permute-start = (bf16[32,56,128]{2,1,0:T(8,128)(2,1)}, bf16[32,56,128]{2,1,0:T(8,128)(2,1)S(1)}, u32[]{:S(2)}, u32[]{:S(2)}) collective-permute-start(bf16[32,56,128]{2,1,0:T(8,128)(2,1)} %get-tuple-element.23), channel_id=1, source_target_pairs={{3,0},{7,4},{11,8},{15,12},{19,16},{23,20},{27,24},{31,28},{35,32}... | collective-permute-start | bytes 1376264 | tf_op jit(solution)/shard_map/ppermute | solution.py:462
  4.6 1.4 %collective-permute-start.2 = (bf16[32,56,128]{2,1,0:T(8,128)(2,1)}, bf16[32,56,128]{2,1,0:T(8,128)(2,1)}, u32[]{:S(2)}, u32[]{:S(2)}) collective-permute-start(bf16[32,56,128]{2,1,0:T(8,128)(2,1)} %get-tuple-element.24), channel_id=1, source_target_pairs={{3,2},{7,6},{11,10},{15,14},{19,18},{23,22},{27,26},{31,30},{35,34... | collective-permute-start | bytes 1376264 | tf_op jit(solution)/shard_map/ppermute | solution.py:462
  6.0 5.2 %pack_rest.1 = (bf16[64,56,128]{2,1,0:T(8,128)(2,1)}, bf16[64,56,128]{2,1,0:T(8,128)(2,1)}, bf16[64,56,128]{2,1,0:T(8,128)(2,1)}) custom-call(bf16[192,4096]{1,0:T(8,128)(2,1)} %q_any.1, bf16[192,512]{1,0:T(8,128)(2,1)} %k_any.1, bf16[192,512]{1,0:T(8,128)(2,1)} %v_any.1, bf16[192,4096]{1,0:T(8,128)(2,1)} %g_any.1, s32[1,48]{1,0:T(1,128)} %bitcast.10), custom_call_target="tpu_custom_call" | custom-call | bytes 6000000 | tf_op jit(solution)/shard_map/pack_rest/pallas_call | solution.py:100
  11.2 1.3 %collective-permute-start.4 = (bf16[64,56,128]{2,1,0:T(8,128)(2,1)}, bf16[64,56,128]{2,1,0:T(8,128)(2,1)S(1)}, u32[]{:S(2)}, u32[]{:S(2)}) collective-permute-start(bf16[64,56,128]{2,1,0:T(8,128)(2,1)} %get-tuple-element.26), channel_id=1, source_target_pairs={{3,0},{7,4},{11,8},{15,12},{19,16},{23,20},{27,24},{31,28},{35,32}... | collective-permute-start | bytes 2752520 | tf_op jit(solution)/shard_map/ppermute | solution.py:462
  12.5 0.7 collective-permute-start.5
  13.2 2.2 %collective-permute-done = bf16[32,56,128]{2,1,0:T(8,128)(2,1)S(1)} collective-permute-done((bf16[32,56,128]{2,1,0:T(8,128)(2,1)}, bf16[32,56,128]{2,1,0:T(8,128)(2,1)S(1)}, u32[]{:S(2)}, u32[]{:S(2)}) %collective-permute-start) | collective-permute-done | bytes 458784 | tf_op jit(solution)/shard_map/ppermute | solution.py:462
  15.4 1.3 %collective-permute-start.1 = (bf16[32,56,128]{2,1,0:T(8,128)(2,1)S(1)}, bf16[32,56,128]{2,1,0:T(8,128)(2,1)S(1)}, u32[]{:S(2)}, u32[]{:S(2)}) collective-permute-start(bf16[32,56,128]{2,1,0:T(8,128)(2,1)S(1)} %collective-permute-done), channel_id=1, source_target_pairs={{0,1},{4,5},{8,9},{12,13},{16,17},{20,21},{24,25},{28,29},{32,33},... | collective-permute-start | bytes 1376264 | tf_op jit(solution)/shard_map/ppermute | solution.py:462
  16.8 0.7 collective-permute-start.3
  17.5 2.2 %slice_group.4 = bf16[192,2304]{1,0:T(8,128)(2,1)} custom-call(s32[1]{0:T(128)} %bitcast.2.me_ref, bf16[192,4096]{1,0:T(8,128)(2,1)} %q_any.1, bf16[192,512]{1,0:T(8,128)(2,1)} %k_any.1, bf16[192,512]{1,0:T(8,128)(2,1)} %v_any.1, bf16[192,4096]{1,0:T(8,128)(2,1)} %g_any.1), custom_call_target="tpu_custom_call" | custom-call | bytes 1800000 | tf_op jit(solution)/shard_map/slice_group/pallas_call | solution.py:132
  19.7 2.1 %slice_group.3 = bf16[192,2304]{1,0:T(8,128)(2,1)} custom-call(s32[1]{0:T(128)} %bitcast.1.me_ref, bf16[192,4096]{1,0:T(8,128)(2,1)} %q_any.1, bf16[192,512]{1,0:T(8,128)(2,1)} %k_any.1, bf16[192,512]{1,0:T(8,128)(2,1)} %v_any.1, bf16[192,4096]{1,0:T(8,128)(2,1)} %g_any.1), custom_call_target="tpu_custom_call" | custom-call | bytes 1800000 | tf_op jit(solution)/shard_map/slice_group/pallas_call | solution.py:132
  21.8 2.3 %slice_group.5 = bf16[192,2304]{1,0:T(8,128)(2,1)} custom-call(s32[1]{0:T(128)} %bitcast.3.me_ref, bf16[192,4096]{1,0:T(8,128)(2,1)} %q_any.1, bf16[192,512]{1,0:T(8,128)(2,1)} %k_any.1, bf16[192,512]{1,0:T(8,128)(2,1)} %v_any.1, bf16[192,4096]{1,0:T(8,128)(2,1)} %g_any.1), custom_call_target="tpu_custom_call" | custom-call | bytes 1800000 | tf_op jit(solution)/shard_map/slice_group/pallas_call | solution.py:132
  24.1 0.0 collective-permute-done.1
  24.1 0.0 collective-permute-done.3
  24.1 12.3 %collective-permute-done.4 = bf16[64,56,128]{2,1,0:T(8,128)(2,1)S(1)} collective-permute-done((bf16[64,56,128]{2,1,0:T(8,128)(2,1)}, bf16[64,56,128]{2,1,0:T(8,128)(2,1)S(1)}, u32[]{:S(2)}, u32[]{:S(2)}) %collective-permute-start.4) | collective-permute-done | bytes 917536 | tf_op jit(solution)/shard_map/ppermute | solution.py:462
  36.4 1.1 maximum_select_fusion
  37.5 15.5 %all-to-all-start = ((bf16[64,56,128]{2,1,0:T(8,128)(2,1)}), bf16[64,56,128]{2,1,0:T(8,128)(2,1)S(1)}, u32[]{:S(2)}, u32[]{:S(2)}) async-start(bf16[64,56,128]{2,1,0:T(8,128)(2,1)} %maximum_select_fusion), calls=%async_computation | async-start | bytes 1835008 | tf_op jit(solution)/shard_map/all_to_all | solution.py:463
  53.0 2.2 %collective-permute-start.6 = (bf16[192,2304]{1,0:T(8,128)(2,1)S(1)}, bf16[192,2304]{1,0:T(8,128)(2,1)}, u32[]{:S(2)}, u32[]{:S(2)}) collective-permute-start(bf16[192,2304]{1,0:T(8,128)(2,1)S(1)} %copy-done.2), channel_id=1, source_target_pairs={{0,1},{1,2},{2,3},{4,5},{5,6},{6,7},{8,9},{9,10},{10,11},{12,13},{... | collective-permute-start | bytes 2654216 | tf_op jit(solution)/shard_map/ppermute | solution.py:462
  55.2 1.9 %collective-permute-start.7 = (bf16[192,2304]{1,0:T(8,128)(2,1)S(1)}, bf16[192,2304]{1,0:T(8,128)(2,1)}, u32[]{:S(2)}, u32[]{:S(2)}) collective-permute-start(bf16[192,2304]{1,0:T(8,128)(2,1)S(1)} %copy-done.1), channel_id=1, source_target_pairs={{1,0},{2,1},{0,3},{5,4},{6,5},{4,7},{9,8},{10,9},{8,11},{13,12},{1... | collective-permute-start | bytes 2654216 | tf_op jit(solution)/shard_map/ppermute | solution.py:462
  57.1 6.5 %collective-permute-start.8 = (bf16[192,2304]{1,0:T(8,128)(2,1)}, bf16[192,2304]{1,0:T(8,128)(2,1)}, u32[]{:S(2)}, u32[]{:S(2)}) collective-permute-start(bf16[192,2304]{1,0:T(8,128)(2,1)} %slice_group.5), channel_id=1, source_target_pairs={{0,2},{2,0},{1,3},{4,6},{6,4},{5,7},{8,10},{10,8},{9,11},{12,14},{... | collective-permute-start | bytes 2654216 | tf_op jit(solution)/shard_map/ppermute | solution.py:462
  63.6 0.1 slice.3
  63.7 0.6 reshape.43.row_ref
  64.3 0.9 reshape.44.col_ref
  65.2 0.1 copy.15.col_ref
  65.3 13.3 %all-to-all-done.in_ref = bf16[64,56,128]{2,1,0:T(8,128)(2,1)S(1)} async-done(((bf16[64,56,128]{2,1,0:T(8,128)(2,1)}), bf16[64,56,128]{2,1,0:T(8,128)(2,1)S(1)}, u32[]{:S(2)}, u32[]{:S(2)}) %all-to-all-start) | async-done | bytes 917536 | tf_op jit(solution)/shard_map/all_to_all | solution.py:463
  78.7 6.7 %route.1 = bf16[64,56,128]{2,1,0:T(8,128)(2,1)} custom-call(bf16[64,56,128]{2,1,0:T(8,128)(2,1)S(1)} %all-to-all-done.in_ref), custom_call_target="tpu_custom_call" | custom-call | flops 4831838208 | bytes 2000000 | tf_op jit(solution)/shard_map/route/pallas_call | solution.py:208
  85.4 6.2 %all-to-all-start.1 = ((bf16[64,56,128]{2,1,0:T(8,128)(2,1)}), bf16[64,56,128]{2,1,0:T(8,128)(2,1)S(1)}, u32[]{:S(2)}, u32[]{:S(2)}) async-start(bf16[64,56,128]{2,1,0:T(8,128)(2,1)} %route.1), calls=%async_computation.1 | async-start | bytes 1835008 | tf_op jit(solution)/shard_map/all_to_all | solution.py:463
  91.6 0.0 collective-permute-done.6.plus
  91.7 4.4 %collective-permute-done.8.two = bf16[192,2304]{1,0:T(8,128)(2,1)} collective-permute-done((bf16[192,2304]{1,0:T(8,128)(2,1)}, bf16[192,2304]{1,0:T(8,128)(2,1)}, u32[]{:S(2)}, u32[]{:S(2)}) %collective-permute-start.8) | collective-permute-done | bytes 884768 | tf_op jit(solution)/shard_map/ppermute | solution.py:462
  96.0 12.6 %attend_stay.1 = (bf16[768,1024]{1,0:T(8,128)(2,1)}, bf16[768,1024]{1,0:T(8,128)(2,1)}, bf16[768,128]{1,0:T(8,128)(2,1)}, bf16[768,128]{1,0:T(8,128)(2,1)}) custom-call(s32[1]{0:T(128)} %bitcast.6.me_ref, bf16[192,4096]{1,0:T(8,128)(2,1)} %q_any.1, bf16[192,512]{1,0:T(8,128)(2,1)} %k_any.1, bf16[192,512]{1,0:T(8,128)(2,1)} %v_any.1, ...), custom_call_target="tpu_custom_call" | custom-call | flops 40768634880 | bytes 6000000 | tf_op jit(solution)/shard_map/attend_stay/pallas_call | solution.py:351
  108.7 8.7 %all-to-all-done.1.slots = bf16[64,56,128]{2,1,0:T(8,128)(2,1)S(1)} async-done(((bf16[64,56,128]{2,1,0:T(8,128)(2,1)}), bf16[64,56,128]{2,1,0:T(8,128)(2,1)S(1)}, u32[]{:S(2)}, u32[]{:S(2)}) %all-to-all-start.1) | async-done | bytes 917536 | tf_op jit(solution)/shard_map/all_to_all | solution.py:463
  117.4 2.8 %attend_tail.1 = (bf16[768,1024]{1,0:T(8,128)(2,1)}, bf16[768,1024]{1,0:T(8,128)(2,1)}, bf16[768,128]{1,0:T(8,128)(2,1)}, bf16[768,128]{1,0:T(8,128)(2,1)}) custom-call(bf16[64,56,128]{2,1,0:T(8,128)(2,1)S(1)} %all-to-all-done.1.slots, s32[256,1]{1,0:T(8,128)S(1)} %copy.15.col_ref, ...), custom_call_target="tpu_custom_call", output_to_operand_aliasing={{0}: (3, {}), {1}: (4, {}), {2}: (5, {}), {3}: (6, {})} | custom-call | flops 301989888 | bytes 2000000 | tf_op jit(solution)/shard_map/attend_tail/pallas_call | solution.py:426
  (12 shorter events, 0.0 us)
Async XLA Ops:
  3.3 12.1 %collective-permute-start = (bf16[32,56,128]{2,1,0:T(8,128)(2,1)}, bf16[32,56,128]{2,1,0:T(8,128)(2,1)S(1)}, u32[]{:S(2)}, u32[]{:S(2)}) collective-permute-start(bf16[32,56,128]{2,1,0:T(8,128)(2,1)} %get-tuple-element.23), channel_id=1, source_target_pairs={{3,0},{7,4},{11,8},{15,12},{19,16},{23,20},{27,24},{31,28},{35,32}... | collective-permute-start | bytes 1376264 | tf_op jit(solution)/shard_map/ppermute | solution.py:462
  4.6 12.1 %collective-permute-start.2 = (bf16[32,56,128]{2,1,0:T(8,128)(2,1)}, bf16[32,56,128]{2,1,0:T(8,128)(2,1)}, u32[]{:S(2)}, u32[]{:S(2)}) collective-permute-start(bf16[32,56,128]{2,1,0:T(8,128)(2,1)} %get-tuple-element.24), channel_id=1, source_target_pairs={{3,2},{7,6},{11,10},{15,14},{19,18},{23,22},{27,26},{31,30},{35,34... | collective-permute-start | bytes 1376264 | tf_op jit(solution)/shard_map/ppermute | solution.py:462
  11.2 25.1 %collective-permute-start.4 = (bf16[64,56,128]{2,1,0:T(8,128)(2,1)}, bf16[64,56,128]{2,1,0:T(8,128)(2,1)S(1)}, u32[]{:S(2)}, u32[]{:S(2)}) collective-permute-start(bf16[64,56,128]{2,1,0:T(8,128)(2,1)} %get-tuple-element.26), channel_id=1, source_target_pairs={{3,0},{7,4},{11,8},{15,12},{19,16},{23,20},{27,24},{31,28},{35,32}... | collective-permute-start | bytes 2752520 | tf_op jit(solution)/shard_map/ppermute | solution.py:462
  12.5 23.9 %collective-permute-start.5 = (bf16[64,56,128]{2,1,0:T(8,128)(2,1)}, bf16[64,56,128]{2,1,0:T(8,128)(2,1)S(1)}, u32[]{:S(2)}, u32[]{:S(2)}) collective-permute-start(bf16[64,56,128]{2,1,0:T(8,128)(2,1)} %get-tuple-element.27), channel_id=1, source_target_pairs={{3,2},{7,6},{11,10},{15,14},{19,18},{23,22},{27,26},{31,30},{35,34... | collective-permute-start | bytes 2752520 | tf_op jit(solution)/shard_map/ppermute | solution.py:462
  15.4 8.7 %collective-permute-start.1 = (bf16[32,56,128]{2,1,0:T(8,128)(2,1)S(1)}, bf16[32,56,128]{2,1,0:T(8,128)(2,1)S(1)}, u32[]{:S(2)}, u32[]{:S(2)}) collective-permute-start(bf16[32,56,128]{2,1,0:T(8,128)(2,1)S(1)} %collective-permute-done), channel_id=1, source_target_pairs={{0,1},{4,5},{8,9},{12,13},{16,17},{20,21},{24,25},{28,29},{32,33},... | collective-permute-start | bytes 1376264 | tf_op jit(solution)/shard_map/ppermute | solution.py:462
  16.8 7.3 %collective-permute-start.3 = (bf16[32,56,128]{2,1,0:T(8,128)(2,1)}, bf16[32,56,128]{2,1,0:T(8,128)(2,1)S(1)}, u32[]{:S(2)}, u32[]{:S(2)}) collective-permute-start(bf16[32,56,128]{2,1,0:T(8,128)(2,1)} %collective-permute-done.2), channel_id=1, source_target_pairs={{2,1},{6,5},{10,9},{14,13},{18,17},{22,21},{26,25},{30,29},{34,33}... | collective-permute-start | bytes 1376264 | tf_op jit(solution)/shard_map/ppermute | solution.py:462
  21.8 14.6 %copy-start = (bf16[64,56,128]{2,1,0:T(8,128)(2,1)S(1)}, bf16[64,56,128]{2,1,0:T(8,128)(2,1)}, u32[]{:S(2)}) copy-start(bf16[64,56,128]{2,1,0:T(8,128)(2,1)} %get-tuple-element.25) | copy-start | bytes 2752516
  37.5 15.5 %copy-start.2 = (bf16[192,2304]{1,0:T(8,128)(2,1)S(1)}, bf16[192,2304]{1,0:T(8,128)(2,1)}, u32[]{:S(2)}) copy-start(bf16[192,2304]{1,0:T(8,128)(2,1)} %slice_group.3) | copy-start | bytes 2654212
  37.5 17.7 %copy-start.1 = (bf16[192,2304]{1,0:T(8,128)(2,1)S(1)}, bf16[192,2304]{1,0:T(8,128)(2,1)}, u32[]{:S(2)}) copy-start(bf16[192,2304]{1,0:T(8,128)(2,1)} %slice_group.4) | copy-start | bytes 2654212
  37.5 26.1 %copy-start.3 = (s32[768]{0:T(1024)S(1)}, s32[768]{0:T(1024)}, u32[]{:S(2)}) copy-start(s32[768]{0:T(1024)} %param.11) | copy-start | bytes 9220
  37.5 41.2 %all-to-all-start = ((bf16[64,56,128]{2,1,0:T(8,128)(2,1)}), bf16[64,56,128]{2,1,0:T(8,128)(2,1)S(1)}, u32[]{:S(2)}, u32[]{:S(2)}) async-start(bf16[64,56,128]{2,1,0:T(8,128)(2,1)} %maximum_select_fusion), calls=%async_computation | async-start | bytes 1835008 | tf_op jit(solution)/shard_map/all_to_all | solution.py:463
  53.0 38.7 %collective-permute-start.6 = (bf16[192,2304]{1,0:T(8,128)(2,1)S(1)}, bf16[192,2304]{1,0:T(8,128)(2,1)}, u32[]{:S(2)}, u32[]{:S(2)}) collective-permute-start(bf16[192,2304]{1,0:T(8,128)(2,1)S(1)} %copy-done.2), channel_id=1, source_target_pairs={{0,1},{1,2},{2,3},{4,5},{5,6},{6,7},{8,9},{9,10},{10,11},{12,13},{... | collective-permute-start | bytes 2654216 | tf_op jit(solution)/shard_map/ppermute | solution.py:462
  55.2 36.5 %collective-permute-start.7 = (bf16[192,2304]{1,0:T(8,128)(2,1)S(1)}, bf16[192,2304]{1,0:T(8,128)(2,1)}, u32[]{:S(2)}, u32[]{:S(2)}) collective-permute-start(bf16[192,2304]{1,0:T(8,128)(2,1)S(1)} %copy-done.1), channel_id=1, source_target_pairs={{1,0},{2,1},{0,3},{5,4},{6,5},{4,7},{9,8},{10,9},{8,11},{13,12},{1... | collective-permute-start | bytes 2654216 | tf_op jit(solution)/shard_map/ppermute | solution.py:462
  57.1 39.0 %collective-permute-start.8 = (bf16[192,2304]{1,0:T(8,128)(2,1)}, bf16[192,2304]{1,0:T(8,128)(2,1)}, u32[]{:S(2)}, u32[]{:S(2)}) collective-permute-start(bf16[192,2304]{1,0:T(8,128)(2,1)} %slice_group.5), channel_id=1, source_target_pairs={{0,2},{2,0},{1,3},{4,6},{6,4},{5,7},{8,10},{10,8},{9,11},{12,14},{... | collective-permute-start | bytes 2654216 | tf_op jit(solution)/shard_map/ppermute | solution.py:462
  85.4 32.0 %all-to-all-start.1 = ((bf16[64,56,128]{2,1,0:T(8,128)(2,1)}), bf16[64,56,128]{2,1,0:T(8,128)(2,1)S(1)}, u32[]{:S(2)}, u32[]{:S(2)}) async-start(bf16[64,56,128]{2,1,0:T(8,128)(2,1)} %route.1), calls=%async_computation.1 | async-start | bytes 1835008 | tf_op jit(solution)/shard_map/all_to_all | solution.py:463
